TPU v7x, 32 devices: a whole 2x2x4 slice. The times are simulated.
32 devices in a mesh: gx: 8 (over z, x), gy: 4 (over y, core).
Axes of the slice: x: 2, y: 2, z: 4, core: 2. Of those that a mesh axis runs over, the one named last changes fastest.
Arguments:
- features: float32 [16, 64, 64, 128], P(None, 'gx', 'gy'), may hold values from -6 to 6
- conv_weight: float32 [27, 16, 16], replicated, may hold values from -0.3125 to 0.3125
- mix_weight: float32 [2, 16, 16, 4, 1728], P(None, None, None, 'gy', 'gx'), may hold values from -1 to 1
Outputs:
- layer_out: float32 [16, 64, 64, 128], P(None, 'gx', 'gy')
All inputs are finite; a program needn't handle non-finite values.
Results may differ from a plain program's by a relative error of at most 0.0001.
Values sent between devices are 32-bit elements; how exact they have to be, the bound alone decides.
No kernel may reach another device: no remote copies, remote signals or barrier semaphores. Data moves between devices by JAX's collectives and lax.ppermute only.
A program may use at most 128 MiB of HBM per device.

v0:
```python
import math

import jax
import jax.numpy as jnp
from jax import lax
from jax.sharding import PartitionSpec as P

KX = 24
KY = 24
KZ = 12


PRECISE = lax.Precision.HIGHEST


def padded_2(array, sides, width):
    for axis, dim in sides:
        size, length = (lax.axis_size(axis), array.shape[dim])
        up = [(i, (i + 1) % size) for i in range(size)]
        down = [(j, i) for i, j in up]
        last = lax.slice_in_dim(array, length - width, length, axis=dim)
        initial = lax.slice_in_dim(array, 0, width, axis=dim)
        before = lax.ppermute(last, axis, up)
        after = lax.ppermute(initial, axis, down)
        array = jnp.concatenate([before, array, after], axis=dim)
    return array


def angle_tables(positions, frequencies, length):
    product = positions[:, None] * frequencies[None, :] % length
    angles = product.astype(jnp.float32) * (2.0 * math.pi / length)
    return (jnp.cos(angles), jnp.sin(angles))


def kept_frequencies(amount, length):
    index = jnp.arange(amount, dtype=jnp.int32)
    return jnp.where(index < amount // 2, index, length - amount + index)


def forward_x(part_real, part_imag, cos_x, sin_x):
    out_real = jnp.einsum("cxm,xp->cpm", part_real, cos_x, precision=PRECISE) + jnp.einsum(
        "cxm,xp->cpm", part_imag, sin_x, precision=PRECISE
    )
    out_imag = jnp.einsum("cxm,xp->cpm", part_imag, cos_x, precision=PRECISE) - jnp.einsum(
        "cxm,xp->cpm", part_real, sin_x, precision=PRECISE
    )
    return (out_real, out_imag)


def inverse_x(part_real, part_imag, cos_x, sin_x):
    out_real = jnp.einsum("cpm,xp->cxm", part_real, cos_x, precision=PRECISE) - jnp.einsum(
        "cpm,xp->cxm", part_imag, sin_x, precision=PRECISE
    )
    out_imag = jnp.einsum("cpm,xp->cxm", part_imag, cos_x, precision=PRECISE) + jnp.einsum(
        "cpm,xp->cxm", part_real, sin_x, precision=PRECISE
    )
    return (out_real, out_imag)


def shards(features, conv_weight, mix_weight):
    channels, cells_x, cells_y, length_z = features.shape
    count_gx = lax.axis_size("gx")
    count_gy = lax.axis_size("gy")
    length_x = cells_x * count_gx
    length_y = cells_y * count_gy
    block_yz = KY * KZ // count_gy
    padded = padded_2(features, (("gx", 1), ("gy", 2)), 1)
    wrapped = jnp.concatenate([padded[..., -1:], padded, padded[..., :1]], axis=3)
    kernel = conv_weight.reshape(3, 3, 3, channels, channels).transpose(3, 4, 0, 1, 2)
    conv_sum = lax.conv_general_dilated(
        wrapped[None],
        kernel,
        (1, 1, 1),
        "VALID",
        dimension_numbers=("NCDHW", "OIDHW", "NCDHW"),
        precision=PRECISE,
    )[0]
    cos_z, sin_z = angle_tables(
        jnp.arange(length_z, dtype=jnp.int32), jnp.arange(KZ, dtype=jnp.int32), length_z
    )
    y_places = lax.axis_index("gy") * cells_y + jnp.arange(cells_y, dtype=jnp.int32)
    x_places = lax.axis_index("gx") * cells_x + jnp.arange(cells_x, dtype=jnp.int32)
    cos_y, sin_y = angle_tables(y_places, kept_frequencies(KY, length_y), length_y)
    cos_x, sin_x = angle_tables(x_places, kept_frequencies(KX, length_x), length_x)
    table_z = jnp.concatenate([cos_z, -sin_z], axis=1)
    along_z = jnp.dot(features, table_z, precision=PRECISE)
    z_real = along_z[..., :KZ]
    z_imag = along_z[..., KZ:]
    y_real = jnp.einsum("cxyk,yq->cxqk", z_real, cos_y, precision=PRECISE) + jnp.einsum(
        "cxyk,yq->cxqk", z_imag, sin_y, precision=PRECISE
    )
    y_imag = jnp.einsum("cxyk,yq->cxqk", z_imag, cos_y, precision=PRECISE) - jnp.einsum(
        "cxyk,yq->cxqk", z_real, sin_y, precision=PRECISE
    )
    partial_value = jnp.stack([y_real, y_imag], axis=2).reshape(channels, cells_x, 2, KY * KZ)
    y_share = lax.psum_scatter(partial_value, "gy", scatter_dimension=3, tiled=True)
    x_real, x_imag = forward_x(y_share[:, :, 0], y_share[:, :, 1], cos_x, sin_x)
    x_partial = jnp.stack([x_real, x_imag], axis=1).reshape(channels, 2, KX * block_yz)
    owned_modes = lax.psum_scatter(x_partial, "gx", scatter_dimension=2, tiled=True)
    forward_scale = 1.0 / math.sqrt(length_x * length_y * length_z)
    owned_modes = owned_modes * forward_scale
    coef_real = owned_modes[:, 0]
    coef_imag = owned_modes[:, 1]
    weight_real = mix_weight[0, :, :, 0, :]
    weight_imag = mix_weight[1, :, :, 0, :]
    mixed_real = jnp.einsum("oim,im->om", weight_real, coef_real, precision=PRECISE) - jnp.einsum(
        "oim,im->om", weight_imag, coef_imag, precision=PRECISE
    )
    mixed_imag = jnp.einsum("oim,im->om", weight_real, coef_imag, precision=PRECISE) + jnp.einsum(
        "oim,im->om", weight_imag, coef_real, precision=PRECISE
    )
    mixed_modes = jnp.stack([mixed_real, mixed_imag], axis=1)
    row_modes = lax.all_gather(mixed_modes, "gx", axis=2, tiled=True).reshape(
        channels, 2, KX, block_yz
    )
    back_real, back_imag = inverse_x(row_modes[:, 0], row_modes[:, 1], cos_x, sin_x)
    x_inverse = jnp.stack([back_real, back_imag], axis=2)
    gathered = lax.all_gather(x_inverse, "gy", axis=3, tiled=True)
    back_real = gathered[:, :, 0].reshape(channels, cells_x, KY, KZ)
    back_imag = gathered[:, :, 1].reshape(channels, cells_x, KY, KZ)
    plane_real = jnp.einsum("cxqk,yq->cxyk", back_real, cos_y, precision=PRECISE) - jnp.einsum(
        "cxqk,yq->cxyk", back_imag, sin_y, precision=PRECISE
    )
    plane_imag = jnp.einsum("cxqk,yq->cxyk", back_imag, cos_y, precision=PRECISE) + jnp.einsum(
        "cxqk,yq->cxyk", back_real, sin_y, precision=PRECISE
    )
    table_back = jnp.concatenate([cos_z.T, -sin_z.T], axis=0)
    inverse_scale = 1.0 / math.sqrt(KX * KY * KZ)
    spectral = (
        jnp.dot(jnp.concatenate([plane_real, plane_imag], axis=3), table_back, precision=PRECISE)
        * inverse_scale
    )
    return jax.nn.gelu(conv_sum + spectral, approximate=False)


def solution(mesh):
    in_specs = (P(None, "gx", "gy", None), P(), P(None, None, None, "gy", "gx"))
    out_specs = P(None, "gx", "gy", None)
    return jax.shard_map(shards, mesh=mesh, in_specs=in_specs, out_specs=out_specs, check_vma=False)
```

profile of v0, /device:TPU:0, one launch (start us, length us, event | category | flops | bytes accessed | tf_op | source)
XLA Modules:
  0.0 403.1 jit_solution(18035166529168039495)
XLA Ops:
  6.6 2.2 convolution_bitcast_fusion
  8.8 1.3 fusion.187
  10.1 2.1 copy.51
  14.9 1.8 fusion.13
  16.7 2.0 copy.53
  21.4 3.9 copy.110
  25.3 5.0 %reshape.61 = f32[288,256]{1,0:T(8,128)} reshape(f32[288,2,16,8]{3,2,1,0:T(8,128)} %bitcast.188) | data formatting | bytes 589824
  30.5 3.0 collective-permute-start
  33.5 3.1 collective-permute-start.1
  39.2 0.9 collective-permute-done
  41.4 1.7 collective-permute-start.3
  43.2 2.1 collective-permute-done.2
  45.9 1.2 maximum_bitcast_fusion
  47.4 6.5 %reshape.36 = f32[16,10,18,1,8,17]{5,4,0,2,1,3:T(8,128)} reshape(f32[16,10,18,1,136]{4,0,2,1,3:T(8,128)S(1)} %pad) | data formatting | bytes 3133440 | tf_op jit(solution)/shard_map/conv_general_dilated | solution.py:70
  54.0 15.0 %copy.47 = f32[16,10,18,1,8,17]{0,4,5,2,1,3:T(8,128)} copy(f32[16,10,18,1,8,17]{5,4,0,2,1,3:T(8,128)} %reshape.36) | data formatting | bytes 3133440 | tf_op jit(solution)/shard_map/conv_general_dilated | solution.py:70
  69.0 1.5 slice.80
  70.5 9.5 %fusion.202 = f32[16,10,18,8,19]{0,3,4,2,1:T(8,128)} fusion(f32[16,10,18,1,7,2]{0,4,5,2,1,3:T(8,128)S(1)} %slice.80, f32[16,10,18,1,8,17]{0,4,5,2,1,3:T(8,128)} %copy.47), kind=kLoop, calls=%fused_computation.1.clone.clone.clone.clone.1 | loop fusion | flops 1313280 | bytes 3479040 | tf_op jit(solution)/shard_map/conv_general_dilated | solution.py:70
  80.0 1.5 reshape.62
  85.1 213.4 %broadcast_select_fusion = f32[8,16,8,17,16]{4,2,3,1,0:T(8,128)} fusion(pred[8,17]{0,1:T(8,128)(4,1)S(1)} %copy-done.7, f32[3,3,3,16,16]{4,3,2,1,0:T(8,128)S(1)} %bitcast.193, f32[16,10,18,8,19]{0,3,4,2,1:T(8,128)} %fusion.202), kind=kOutput, calls=%fused_computation.8 | convolution fusion | flops 1444167680 | bytes 2892936 | tf_op jit(solution)/shard_map/conv_general_dilated | solution.py:70
  298.6 12.5 %copy.98 = f32[8,16,8,17,16]{3,2,1,0,4:T(8,128)} copy(f32[8,16,8,17,16]{4,2,3,1,0:T(8,128)} %broadcast_select_fusion) | data formatting | bytes 2228224 | tf_op jit(solution)/shard_map/conv_general_dilated | solution.py:70
  311.1 7.0 %reshape.60 = f32[8,16,1,136,16]{3,1,0,4,2:T(8,128)} reshape(f32[8,16,8,17,16]{3,2,1,0,4:T(8,128)} %copy.98) | data formatting | bytes 2228224 | tf_op jit(solution)/shard_map/conv_general_dilated | solution.py:70
  319.4 39.8 %all_gather.6 = f32[16,2,1728]{0,1,2:T(2,128)S(1)} all-gather(f32[16,2,216]{0,1,2:T(2,128)S(1)} %copy.57), channel_id=1, replica_groups=mesh['gx'=8,'gy'=4] {'gx'}, dimensions={2}, use_global_device_ids=true | all-gather | bytes 248832 | tf_op jit(solution)/shard_map/all_gather | solution.py:113
  359.2 1.4 fusion.182
  363.3 16.8 %all_gather.7 = f32[16,8,2,288]{0,1,2,3:T(8,128)S(1)} all-gather(f32[16,8,2,72]{0,1,2,3:T(8,128)S(1)} %copy.59), channel_id=1, replica_groups=mesh['gx'=8,'gy'=4] {'gy'}, dimensions={3}, use_global_device_ids=true | all-gather | bytes 368640 | tf_op jit(solution)/shard_map/all_gather | solution.py:118
  380.1 1.2 fusion.181
  381.3 1.7 copy.93
  383.0 2.2 fusion.67
  385.2 2.9 copy.94
  388.1 1.2 fusion.65
  389.3 1.2 fusion.10
  390.5 1.2 fusion.9
  392.1 4.2 %fusion.19 = f32[16,8,16,128]{3,2,1,0:T(8,128)} fusion(f32[16,8,16,12]{3,2,1,0:T(8,128)S(1)} %fusion.9, f32[16,8,16,12]{3,2,1,0:T(8,128)S(1)} %fusion.10, f32[8,16,1,136,16]{3,1,0,4,2:T(8,128)S(1)} %copy-done.2, f32[12,128]{1,0:T(8,128)S(1)} %get-tuple-element.31, f32[12,128]{1,0:T(8,128)S(1)} %get-tuple-element.32), kind=kOutput, calls=%fused_computation.32 | convolution fusion | flops 92851200 | bytes 2306048 | tf_op jit(solution)/shard_map/dot_general | solution.py:130
  (76 shorter events, 17.5 us)
Async XLA Ops:
  6.5 73.5 %reduce-scatter.5.cloned.1.call-start = ((), (), s32[]{:S(2)}) async-start(), calls=%async_computation.1 | async-start | bytes 368640
  25.3 5.1 %copy-start = (f32[16,8,16,128]{3,2,1,0:T(8,128)S(1)}, f32[16,8,16,128]{3,2,1,0:T(8,128)}, u32[]{:S(2)}) copy-start(f32[16,8,16,128]{3,2,1,0:T(8,128)} %param.3) | copy-start | bytes 3145732
  30.3 6.3 %copy-start.3 = (f32[2,16,16,1,216]{4,3,2,1,0:T(1,128)S(1)}, f32[2,16,16,1,216]{4,3,2,1,0:T(1,128)}, u32[]{:S(2)}) copy-start(f32[2,16,16,1,216]{4,3,2,1,0:T(1,128)} %param.5) | copy-start | bytes 1327108
  30.3 6.7 %copy-start.5 = (f32[27,16,16]{0,2,1:T(8,128)S(1)}, f32[27,16,16]{0,2,1:T(8,128)}, u32[]{:S(2)}) copy-start(f32[27,16,16]{0,2,1:T(8,128)} %param.4) | copy-start | bytes 82948
  30.3 7.6 %copy-start.6 = (u32[32]{0:T(128)S(1)}, u32[32]{0:T(128)}, u32[]{:S(2)}) copy-start(u32[32]{0:T(128)} %constant.137) | copy-start | bytes 388
  30.3 287.7 %all-reduce.3.cloned.1.call-start = ((), (), s32[]{:S(2)}) async-start(), calls=%async_computation.2 | async-start | bytes 458752
  30.5 9.6 %collective-permute-start = (f32[16,1,16,128]{3,0,2,1:T(8,128)S(1)}, f32[16,1,16,128]{3,0,2,1:T(8,128)S(1)}, u32[]{:S(2)}, u32[]{:S(2)}) collective-permute-start(f32[16,1,16,128]{3,0,2,1:T(8,128)S(1)} %copy.128), channel_id=1, source_target_pairs={{0,4},{4,8},{8,12},{12,16},{16,20},{20,24},{24,28},{28,0},{1,5},{5... | collective-permute-start | bytes 393224 | tf_op jit(solution)/shard_map/ppermute | solution.py:23
  33.5 7.8 %collective-permute-start.1 = (f32[16,1,16,128]{3,0,2,1:T(8,128)S(1)}, f32[16,1,16,128]{3,0,2,1:T(8,128)S(1)}, u32[]{:S(2)}, u32[]{:S(2)}) collective-permute-start(f32[16,1,16,128]{3,0,2,1:T(8,128)S(1)} %copy.129), channel_id=1, source_target_pairs={{4,0},{8,4},{12,8},{16,12},{20,16},{24,20},{28,24},{0,28},{5,1},{9... | collective-permute-start | bytes 393224 | tf_op jit(solution)/shard_map/ppermute | solution.py:24
  41.4 3.9 collective-permute-start.2
  41.4 3.9 collective-permute-start.3
  81.9 3.2 copy-start.4
  81.9 3.2 copy-start.7
  388.1 1.2 copy-start.1
  390.5 1.6 copy-start.2
Sparse Core Ops, SparseCore 0:
  30.5 22.9 reduce-scatter.4
  85.2 70.7 all-reduce.2
where the time goes:
time: 404 us; the launch traced here: 403 us
  matrix products  233 us (58%)
  local copies, waits for them, and re-layouts  74.3 us (18%)
  blocking collectives  56.7 us (14%)
  between operations  14.5 us (4%)
  other arithmetic  12.8 us (3%)
  starting transfers between devices  7.93 us (2%)
    conv_general_dilated x1, matrix products, shards(): lax.conv_general_dilated(wrapped[None], kernel, (1, 1, 1), 'VALID', dimen...  213 us
    conv_general_dilated x5, local copies, waits for them, and re-layouts, shards(): lax.conv_general_dilated(wrapped[None], kernel, (1, 1, 1), 'VALID', dimen...  42.6 us
    all_gather x1, blocking collectives, shards(): lax.all_gather(mixed_modes, 'gx', axis=2, tiled=True)  39.8 us
    all_gather x1, blocking collectives, shards(): gathered = lax.all_gather(x_inverse, 'gy', axis=3, tiled=True)  16.8 us
    unnamed x30, local copies, waits for them, and re-layouts  14.6 us
    conv_general_dilated x1, other arithmetic, shards(): lax.conv_general_dilated(wrapped[None], kernel, (1, 1, 1), 'VALID', dimen...  9.53 us
  transfers between devices with their start and end apart: 6, of which 3 were waited for; matrix products, arithmetic and copies ran while one was open for 67% of the time, Pallas kernels for 0%

commit v1 on v0

v1 whole, which is shorter than its diff:
```python
import functools
import math

import jax
import jax.numpy as jnp
import ml_dtypes
import numpy as np
from jax import lax
from jax.experimental import pallas as pl
from jax.experimental.pallas import tpu as pltpu
from jax.sharding import PartitionSpec as P

KX = 24
KY = 24
KZ = 12
LANES = 128
F32 = jnp.float32
BF16 = jnp.bfloat16
PRECISE = lax.Precision.HIGHEST
VMEM_LIMIT = 48 * 1024 * 1024
NN = (((1,), (0,)), ((), ()))
NT = (((1,), (1,)), ((), ()))


def kernel_call(body, out_shape, scratch=(), grid_spec=None, **kw):
    params = pltpu.CompilerParams(vmem_limit_bytes=VMEM_LIMIT)
    if grid_spec is not None:
        kw["grid_spec"] = grid_spec
    else:
        kw["scratch_shapes"] = list(scratch)
    return pl.pallas_call(body, out_shape=out_shape, compiler_params=params, **kw)


def halves(value):
    high = value.astype(BF16)
    return high, (value - high.astype(F32)).astype(BF16)


def dot(a, b, dims=NN):
    return lax.dot_general(a, b, dims, preferred_element_type=F32)


def dot3(a, b, dims=NN):
    return dot(a[0], b[0], dims) + (dot(a[0], b[1], dims) + dot(a[1], b[0], dims))


def table_halves(table):
    table = np.asarray(table, np.float64)
    high = table.astype(ml_dtypes.bfloat16)
    low = (table - high.astype(np.float64)).astype(ml_dtypes.bfloat16)
    return high, low


def kept_np(amount, length):
    index = np.arange(amount)
    return np.where(index < amount // 2, index, length - amount + index)


def angles_np(positions, frequencies, length):
    return 2.0 * np.pi * ((positions[:, None] * frequencies[None, :]) % length) / length


def band_kernel(channels, cells_y, weight_ref, main_h, main_l, side_h, side_l, base_h, base_l):
    main = channels * cells_y
    width = main + 2 * channels
    w_h, w_l = halves(weight_ref[...])
    row = lax.broadcasted_iota(jnp.int32, (channels, width), 0)
    col = lax.broadcasted_iota(jnp.int32, (channels, width), 1)
    source = jnp.where(col < main, col // cells_y, (col - main) % channels)
    spread = jnp.where(row == source, 1.0, 0.0).astype(BF16)
    base_h[...] = dot(w_h, spread)
    base_l[...] = dot(w_l, spread)
    y_out = lax.broadcasted_iota(jnp.int32, (cells_y, main), 0)
    y_in = lax.broadcasted_iota(jnp.int32, (cells_y, main), 1) % cells_y
    tap = y_in - y_out + 1
    side_y = lax.broadcasted_iota(jnp.int32, (cells_y, 2 * channels), 0)
    side_c = lax.broadcasted_iota(jnp.int32, (cells_y, 2 * channels), 1)
    first = (side_y == 0) & (side_c < channels)
    last = (side_y == cells_y - 1) & (side_c >= channels)

    def step(o, carry):
        for base, out_main, out_side in ((base_h, main_h, side_h), (base_l, main_l, side_l)):
            for c in range(3):
                at = pl.multiple_of(c * main + o * cells_y, cells_y)
                for a in range(3):
                    taps = [base[pl.ds((9 * a + 3 * b + c) * channels + o, 1), :] for b in range(3)]
                    block = jnp.zeros((cells_y, main), F32)
                    for b in range(3):
                        block = jnp.where(tap == b, taps[b][:, :main], block)
                    out_main[pl.ds(at, cells_y), a * main : (a + 1) * main] = block.astype(BF16)
                    edge = jnp.where(first, taps[0][:, main:], jnp.where(last, taps[2][:, main:], 0.0))
                    out_side[a, pl.ds(at, cells_y), :] = edge.astype(BF16)
        return carry

    lax.fori_loop(0, channels, step, 0)


def band_weights(conv_weight, cells_y):
    channels = conv_weight.shape[1]
    main = channels * cells_y
    shapes = [
        jax.ShapeDtypeStruct((3 * main, 3 * main), BF16),
        jax.ShapeDtypeStruct((3 * main, 3 * main), BF16),
        jax.ShapeDtypeStruct((3, 3 * main, 2 * channels), BF16),
        jax.ShapeDtypeStruct((3, 3 * main, 2 * channels), BF16),
    ]
    return kernel_call(
        functools.partial(band_kernel, channels, cells_y),
        shapes,
        [pltpu.VMEM((27 * channels, main + 2 * channels), F32)] * 2,
    )(conv_weight.reshape(27 * channels, channels))


def conv_kernel(feat, x_low, x_high, y_low, y_high, main_h, main_l, side_h, side_l, out, rows_h, rows_l, edge_h, edge_l):
    channels, cells_x, cells_y, length_z = feat.shape
    main = channels * cells_y
    side = 2 * channels
    for x in range(cells_x + 2):
        if x == 0:
            plane = x_low[:, 0]
        elif x == cells_x + 1:
            plane = x_high[:, 0]
        else:
            plane = feat[:, x - 1]
        high, low = halves(plane.reshape(main, length_z))
        rows_h[x * main : (x + 1) * main, :] = high
        rows_l[x * main : (x + 1) * main, :] = low
        edge = jnp.concatenate([y_low[x], y_high[x]], axis=0)
        high, low = halves(edge)
        edge_h[x * side : (x + 1) * side, :] = high
        edge_l[x * side : (x + 1) * side, :] = low
    for x in range(0, cells_x, 2):
        def pair(ref, size, count):
            return jnp.concatenate([ref[(x + p) * size : (x + p + count) * size, :] for p in (0, 1)], axis=1)

        body = (pair(rows_h, main, 3), pair(rows_l, main, 3))
        total = [None, None]
        for c in range(3):
            part = dot3((main_h[c * main : (c + 1) * main, :], main_l[c * main : (c + 1) * main, :]), body)
            for a in range(3):
                rim_at = [jnp.concatenate([ref[(x + p + a) * side : (x + p + a + 1) * side, :] for p in (0, 1)], axis=1) for ref in (edge_h, edge_l)]
                part = part + dot3((side_h[a, c * main : (c + 1) * main, :], side_l[a, c * main : (c + 1) * main, :]), rim_at)
            for p in (0, 1):
                piece = part[:, p * length_z : (p + 1) * length_z]
                if c != 1:
                    piece = pltpu.roll(piece, (1 - c) % length_z, 1)
                total[p] = piece if total[p] is None else total[p] + piece
        for p in (0, 1):
            out[:, x + p] = total[p].reshape(channels, cells_y, length_z)


def conv_bricks(feat, x_low, x_high, y_low, y_high, bands):
    channels, cells_x, cells_y, length_z = feat.shape
    main = channels * cells_y
    side = 2 * channels
    reach = cells_x + 2
    return kernel_call(
        conv_kernel,
        jax.ShapeDtypeStruct(feat.shape, F32),
        [
            pltpu.VMEM((reach * main, length_z), BF16),
            pltpu.VMEM((reach * main, length_z), BF16),
            pltpu.VMEM((reach * side, length_z), BF16),
            pltpu.VMEM((reach * side, length_z), BF16),
        ],
    )(feat, x_low, x_high, y_low, y_high, *bands)


def ring(value, axis, step):
    size = lax.axis_size(axis)
    return lax.ppermute(value, axis, [(i, (i + step) % size) for i in range(size)])


def halos(features):
    cells_x, cells_y = features.shape[1:3]
    with jax.named_scope("halo_x"):
        x_low = ring(features[:, cells_x - 1 :], "gx", 1)
        x_high = ring(features[:, :1], "gx", -1)
    with jax.named_scope("halo_y"):
        def face(y):
            whole = jnp.concatenate([x_low[:, :, y], features[:, :, y], x_high[:, :, y]], axis=1)
            return whole.transpose(1, 0, 2)

        y_low = ring(face(cells_y - 1), "gy", 1)
        y_high = ring(face(0), "gy", -1)
    return x_low, x_high, y_low, y_high


def angle_tables(positions, frequencies, length):
    product = positions[:, None] * frequencies[None, :] % length
    angles = product.astype(jnp.float32) * (2.0 * math.pi / length)
    return (jnp.cos(angles), jnp.sin(angles))


def kept_frequencies(amount, length):
    index = jnp.arange(amount, dtype=jnp.int32)
    return jnp.where(index < amount // 2, index, length - amount + index)


def times(form, a, b, c, d):
    one = functools.partial(jnp.einsum, form, precision=PRECISE)
    return one(a, c) + one(b, d)


def spectral_any(features, mix_weight):
    channels, cells_x, cells_y, length_z = features.shape
    count_gx = lax.axis_size("gx")
    count_gy = lax.axis_size("gy")
    length_x = cells_x * count_gx
    length_y = cells_y * count_gy
    block_yz = KY * KZ // count_gy
    cos_z, sin_z = angle_tables(jnp.arange(length_z, dtype=jnp.int32), jnp.arange(KZ, dtype=jnp.int32), length_z)
    y_places = lax.axis_index("gy") * cells_y + jnp.arange(cells_y, dtype=jnp.int32)
    x_places = lax.axis_index("gx") * cells_x + jnp.arange(cells_x, dtype=jnp.int32)
    cos_y, sin_y = angle_tables(y_places, kept_frequencies(KY, length_y), length_y)
    cos_x, sin_x = angle_tables(x_places, kept_frequencies(KX, length_x), length_x)
    along_z = jnp.dot(features, jnp.concatenate([cos_z, -sin_z], axis=1), precision=PRECISE)
    z_real = along_z[..., :KZ]
    z_imag = along_z[..., KZ:]
    y_real = times("cxyk,yq->cxqk", z_real, z_imag, cos_y, sin_y)
    y_imag = times("cxyk,yq->cxqk", z_imag, z_real, cos_y, -sin_y)
    partial_value = jnp.stack([y_real, y_imag], axis=2).reshape(channels, cells_x, 2, KY * KZ)
    y_share = lax.psum_scatter(partial_value, "gy", scatter_dimension=3, tiled=True)
    x_real = times("cxm,xp->cpm", y_share[:, :, 0], y_share[:, :, 1], cos_x, sin_x)
    x_imag = times("cxm,xp->cpm", y_share[:, :, 1], y_share[:, :, 0], cos_x, -sin_x)
    x_partial = jnp.stack([x_real, x_imag], axis=1).reshape(channels, 2, KX * block_yz)
    owned_modes = lax.psum_scatter(x_partial, "gx", scatter_dimension=2, tiled=True)
    owned_modes = owned_modes * (1.0 / math.sqrt(length_x * length_y * length_z))
    coef_real = owned_modes[:, 0]
    coef_imag = owned_modes[:, 1]
    weight_real = mix_weight[0, :, :, 0, :]
    weight_imag = mix_weight[1, :, :, 0, :]
    mixed_real = times("oim,im->om", weight_real, weight_imag, coef_real, -coef_imag)
    mixed_imag = times("oim,im->om", weight_real, weight_imag, coef_imag, coef_real)
    mixed_modes = jnp.stack([mixed_real, mixed_imag], axis=1)
    row_modes = lax.all_gather(mixed_modes, "gx", axis=2, tiled=True).reshape(channels, 2, KX, block_yz)
    back_real = times("cpm,xp->cxm", row_modes[:, 0], row_modes[:, 1], cos_x, -sin_x)
    back_imag = times("cpm,xp->cxm", row_modes[:, 1], row_modes[:, 0], cos_x, sin_x)
    gathered = lax.all_gather(jnp.stack([back_real, back_imag], axis=2), "gy", axis=3, tiled=True)
    back_real = gathered[:, :, 0].reshape(channels, cells_x, KY, KZ)
    back_imag = gathered[:, :, 1].reshape(channels, cells_x, KY, KZ)
    plane_real = times("cxqk,yq->cxyk", back_real, back_imag, cos_y, -sin_y)
    plane_imag = times("cxqk,yq->cxyk", back_imag, back_real, cos_y, sin_y)
    table_back = jnp.concatenate([cos_z.T, -sin_z.T], axis=0)
    planes = jnp.concatenate([plane_real, plane_imag], axis=3)
    return jnp.dot(planes, table_back, precision=PRECISE) * (1.0 / math.sqrt(KX * KY * KZ))


class Plan:
    def __init__(self, feature_shape, count_gx, count_gy):
        self.channels, self.cells_x, self.cells_y, self.length_z = feature_shape
        self.count_gx, self.count_gy = count_gx, count_gy
        self.outer = count_gx // 2
        self.block = KY * KZ // count_gy
        self.part = self.block // 2
        self.per_gx = KX // count_gx
        self.rows = 2 * self.part
        self.pad_k = -(-2 * KZ // 32) * 32
        self.length_x = self.cells_x * count_gx
        self.length_y = self.cells_y * count_gy

    @staticmethod
    def fits(feature_shape, count_gx, count_gy):
        channels, cells_x, cells_y, length_z = feature_shape
        outer = count_gx // 2
        if count_gy != 4 or count_gx % 2 or outer & (outer - 1) or outer > 4:
            return False
        if KX % count_gx or (KY * KZ) % (2 * count_gy) or channels * cells_x != LANES:
            return False
        part = KY * KZ // count_gy // 2
        per = KX // count_gx
        return (
            length_z == LANES
            and cells_y % 4 == 0
            and channels % 16 == 0
            and (2 * part) % 8 == 0
            and 4 * 2 * part % 16 == 0
            and per * part <= LANES
            and 2 * per * channels <= LANES
            and 2 * per * part <= 2 * LANES
            and 2 * part <= LANES
        )

    def table_z(self):
        table = np.zeros((self.pad_k, self.length_z))
        angle = angles_np(np.arange(KZ), np.arange(self.length_z), self.length_z)
        table[:KZ] = np.cos(angle)
        table[KZ : 2 * KZ] = -np.sin(angle)
        return table

    def table_z_group(self):
        group = LANES // self.pad_k
        return np.kron(np.eye(group), self.table_z())

    def table_y(self):
        kept = kept_np(KY, self.length_y)
        tables = []
        for gy in range(self.count_gy):
            places = gy * self.cells_y + np.arange(self.cells_y)
            angle = angles_np(places, kept, self.length_y)
            for pair in range(2):
                order = []
                for core in range(2):
                    for yy in range(2):
                        for xx in range(2):
                            owner = ((gy >> 1) ^ yy) * 2 + ((gy & 1) ^ core)
                            order.append(owner * self.block + (pair ^ xx) * self.part + np.arange(self.part))
                order = np.stack(order)
                turn, line = order // KZ, order % KZ
                cos, sin = np.cos(angle)[:, turn], np.sin(angle)[:, turn]
                same = line[None, :, :, None] == np.arange(KZ)
                table = np.zeros((8, 2, self.part, self.cells_y, self.pad_k))
                cos = np.moveaxis(cos[..., None] * same, 0, 2)
                sin = np.moveaxis(sin[..., None] * same, 0, 2)
                table[:, 0, :, :, :KZ] = cos
                table[:, 0, :, :, KZ : 2 * KZ] = sin
                table[:, 1, :, :, :KZ] = -sin
                table[:, 1, :, :, KZ : 2 * KZ] = cos
                tables.append(table.reshape(8 * self.rows, self.cells_y * self.pad_k))
        return np.stack(tables)

    def table_x(self):
        kept = kept_np(KX, self.length_x)
        tables = []
        for gx in range(self.count_gx):
            outer, pair = gx // 2, gx % 2
            places = np.stack([(gx ^ xx) * self.cells_x + np.arange(self.cells_x) for xx in range(2)])
            modes = np.stack(
                [
                    np.concatenate([(2 * (outer ^ zz) + (pair ^ h)) * self.per_gx + np.arange(self.per_gx) for h in range(2)])
                    for zz in range(self.outer)
                ]
            )
            angle = angles_np(places.reshape(-1), kept[modes.reshape(-1)], self.length_x)
            table = np.zeros((2, self.channels, self.cells_x, 2, self.outer, LANES))
            for at, value in enumerate((np.cos(angle), np.sin(angle))):
                value = value.reshape(2, self.cells_x, self.outer, 2 * self.per_gx)
                for channel in range(self.channels):
                    table[:, channel, :, at, :, channel : 2 * self.per_gx * self.channels : self.channels] = value
            tables.append(table.reshape(2 * LANES, 2 * self.outer * LANES))
        return np.stack(tables)


def forward_kernel(plan, select, feat, tz_h, tz_l, ty_h, ty_l, send, keep0, keep1, keep2, keep3, face0, face1, v_h, v_l):
    table_z = (tz_h[...], tz_l[...])
    pad = plan.pad_k
    for y in range(plan.cells_y):
        plane = halves(feat[pl.ds(y, LANES, stride=plan.cells_y), :])
        high, low = halves(dot3(table_z, plane, NT))
        v_h[y * pad : (y + 1) * pad, :] = high
        v_l[y * pad : (y + 1) * pad, :] = low
    field = (v_h[...], v_l[...])
    rows = plan.rows
    for part in range(4):
        at = slice(part * 2 * rows, (part + 1) * 2 * rows)
        value = dot3((ty_h[0, at, :], ty_l[0, at, :]), field)
        if part < 2:
            (keep0, keep2)[part][...] = value[:rows]
            (keep1, keep3)[part][...] = value[rows:]
        else:
            send[(part - 2) * 2 * rows : (part - 1) * 2 * rows, :] = value
    channels, cells_x, cells_y = plan.channels, plan.cells_x, plan.cells_y
    for x in range(cells_x):
        for face, y in ((face0, 0), (face1, cells_y - 1)):
            face[x] = feat[pl.ds(x * cells_y + y, channels, stride=cells_x * cells_y), :]


def forward_modes(plan, features, select):
    rows = plan.rows
    ty_h, ty_l = table_halves(plan.table_y())
    tz_h, tz_l = table_halves(plan.table_z())
    whole = lambda shape: pl.BlockSpec(shape, lambda i, s: (0,) * len(shape))
    pick = pl.BlockSpec((1,) + ty_h.shape[1:], lambda i, s: (s[0], 0, 0))
    part = jax.ShapeDtypeStruct((rows, LANES), F32)
    face = jax.ShapeDtypeStruct((plan.cells_x, plan.channels, plan.length_z), F32)
    outs = [jax.ShapeDtypeStruct((4 * rows, LANES), F32), part, part, part, part, face, face]
    flat = features.reshape(-1, plan.length_z)
    grid_spec = pltpu.PrefetchScalarGridSpec(
        num_scalar_prefetch=1,
        grid=(1,),
        in_specs=[whole(flat.shape), whole(tz_h.shape), whole(tz_h.shape), pick, pick],
        out_specs=[whole(o.shape) for o in outs],
        scratch_shapes=[pltpu.VMEM((plan.cells_y * plan.pad_k, LANES), BF16)] * 2,
    )
    return kernel_call(functools.partial(forward_kernel, plan), outs, grid_spec=grid_spec)(
        select, flat, tz_h, tz_l, ty_h, ty_l
    )


def swapped(value, rows):
    return jnp.concatenate([value[rows // 2 :], value[: rows // 2]], axis=0)


def x_forward_kernel(plan, select, own, from_x, from_y, from_xy, tx_h, tx_l, *outs):
    rows = plan.rows
    near = own[...] + from_y[...]
    far = from_x[...] + from_xy[...]
    field = halves(jnp.concatenate([near, far], axis=1))
    value = dot3(field, (tx_h[0], tx_l[0]))
    half = plan.outer * LANES
    turned = swapped(value[:, half:], rows)
    sign = jnp.where(lax.broadcasted_iota(jnp.int32, (rows, half), 0) < rows // 2, 1.0, -1.0)
    value = value[:, :half] + sign * turned
    for at, out in enumerate(outs):
        out[...] = value[:, at * LANES : (at + 1) * LANES]


def x_inverse_kernel(plan, select, *refs):
    rows = plan.rows
    parts = refs[: plan.outer]
    tx_h, tx_l, near, far = refs[plan.outer :]
    field = halves(jnp.concatenate([p[...] for p in parts], axis=1))
    half = plan.outer * LANES
    cos = dot3(field, (tx_h[0, :, :half], tx_l[0, :, :half]), NT)
    sin = dot3(field, (tx_h[0, :, half:], tx_l[0, :, half:]), NT)
    sign = jnp.where(lax.broadcasted_iota(jnp.int32, (rows, 2 * LANES), 0) < rows // 2, -1.0, 1.0)
    value = cos + sign * swapped(sin, rows)
    near[...] = value[:, :LANES]
    far[...] = value[:, LANES:]


def x_call(plan, body, parts, tables, count, select):
    whole = lambda shape: pl.BlockSpec(shape, lambda i, s: (0,) * len(shape))
    pick = pl.BlockSpec((1,) + tables[0].shape[1:], lambda i, s: (s[0], 0, 0))
    part = jax.ShapeDtypeStruct((plan.rows, LANES), F32)
    grid_spec = pltpu.PrefetchScalarGridSpec(
        num_scalar_prefetch=1,
        grid=(1,),
        in_specs=[whole(p.shape) for p in parts] + [pick, pick],
        out_specs=[whole(part.shape)] * count,
    )
    return kernel_call(functools.partial(body, plan), [part] * count, grid_spec=grid_spec)(select, *parts, *tables)


def weight_kernel(plan, select, weight, keep, send):
    lane = lax.broadcasted_iota(jnp.int32, keep.shape[1:], 1)
    part, block = plan.part, plan.block
    width = 2 * LANES
    for which in range(2):
        value = weight[which]
        choice = []
        for half in range(2):
            total = jnp.zeros(keep.shape[1:], F32)
            for j in range(plan.per_gx):
                shift = (j * part - j * block - half * part) % width
                moved = value if shift == 0 else pltpu.roll(value, shift, 1)
                inside = (lane >= j * part) & (lane < (j + 1) * part)
                total = jnp.where(inside, moved[:, :LANES], total)
            choice.append(total)
        first = select[0] == 0
        keep[which] = jnp.where(first, choice[0], choice[1])
        send[which] = jnp.where(first, choice[1], choice[0])


def weight_parts(plan, mix_weight, pair):
    square = plan.channels * plan.channels
    flat = mix_weight.reshape(2, square, mix_weight.shape[-1])
    block = (2, square, 2 * LANES)
    out = jax.ShapeDtypeStruct((2, square, LANES), F32)
    grid_spec = pltpu.PrefetchScalarGridSpec(
        num_scalar_prefetch=1,
        grid=(1,),
        in_specs=[pl.BlockSpec(block, lambda i, s: (0, 0, 0))],
        out_specs=[pl.BlockSpec(out.shape, lambda i, s: (0, 0, 0))] * 2,
    )
    return kernel_call(functools.partial(weight_kernel, plan), [out, out], grid_spec=grid_spec)(pair, flat)


def mix_kernel(plan, *refs):
    parts = refs[: plan.outer]
    near, far, out = refs[plan.outer :]
    channels, part, per, rows = plan.channels, plan.part, plan.per_gx, plan.rows
    total = parts[0][...]
    for p in parts[1:]:
        total = total + p[...]
    scale = 1.0 / math.sqrt(plan.length_x * plan.length_y * plan.length_z) / math.sqrt(KX * KY * KZ)
    total = jnp.concatenate([total * scale, jnp.zeros((LANES - rows, LANES), F32)], axis=0).T
    lane = lax.broadcasted_iota(jnp.int32, (channels, LANES), 1)

    def moved(value, shift):
        return value if shift % LANES == 0 else pltpu.roll(value, shift % LANES, 1)

    def collect(half, which):
        value = jnp.zeros((channels, LANES), F32)
        for j in range(per):
            at = (half * per + j) * channels
            piece = moved(total[at : at + channels], (j - which) * part)
            value = jnp.where((lane >= j * part) & (lane < (j + 1) * part), piece, value)
        return value

    blocks = []
    for half, weight in enumerate((near, far)):
        c_real, c_imag = collect(half, 0), collect(half, 1)
        real = jnp.zeros((channels, LANES), F32)
        imag = jnp.zeros((channels, LANES), F32)
        for i in range(channels):
            w_real = weight[0, pl.ds(i, channels, stride=channels), :]
            w_imag = weight[1, pl.ds(i, channels, stride=channels), :]
            a, b = c_real[i : i + 1], c_imag[i : i + 1]
            real = real + (w_real * a - w_imag * b)
            imag = imag + (w_real * b + w_imag * a)
        for j in range(per):
            low = moved(real, -j * part)
            high = moved(imag, part - j * part)
            blocks.append(jnp.where(lane < part, low, jnp.where(lane < 2 * part, high, 0.0)))
    fill = LANES - 2 * per * channels
    if fill:
        blocks.append(jnp.zeros((fill, LANES), F32))
    out[...] = jnp.concatenate(blocks, axis=0).T[:rows]


def mix_modes(plan, parts, near, far):
    return kernel_call(functools.partial(mix_kernel, plan), jax.ShapeDtypeStruct((plan.rows, LANES), F32))(
        *parts, near, far
    )


def final_kernel(plan, select, own, other, conv, tz_h, tz_l, ty_h, ty_l, out):
    rows = plan.rows
    depth = 8 * rows
    pad = -depth % LANES
    parts = [own[...], other[...]]
    if pad:
        parts.append(jnp.zeros((pad, LANES), F32))
    field = jnp.concatenate(parts, axis=0)
    columns = jnp.concatenate([field[at : at + LANES].T for at in range(0, depth + pad, LANES)], axis=1)
    modes = halves(columns[:, :depth])
    planes = halves(dot3(modes, (ty_h[0], ty_l[0])))
    table_z = (tz_h[...], tz_l[...])
    group = LANES // plan.pad_k
    for g in range(plan.cells_y // group):
        at = slice(g * LANES, (g + 1) * LANES)
        value = dot3((planes[0][:, at], planes[1][:, at]), table_z)
        for k in range(group):
            index = pl.ds(g * group + k, LANES, stride=plan.cells_y)
            layer = conv[index, :] + value[:, k * LANES : (k + 1) * LANES]
            out[index, :] = layer * 0.5 * (1.0 + lax.erf(layer * math.sqrt(0.5)))


def final_layer(plan, own, other, conv, select):
    ty_h, ty_l = table_halves(plan.table_y())
    tz_h, tz_l = table_halves(plan.table_z_group())
    whole = lambda shape: pl.BlockSpec(shape, lambda i, s: (0,) * len(shape))
    pick = pl.BlockSpec((1,) + ty_h.shape[1:], lambda i, s: (s[0], 0, 0))
    flat = conv.reshape(-1, plan.length_z)
    grid_spec = pltpu.PrefetchScalarGridSpec(
        num_scalar_prefetch=1,
        grid=(1,),
        in_specs=[whole(own.shape), whole(other.shape), whole(flat.shape), whole(tz_h.shape), whole(tz_h.shape), pick, pick],
        out_specs=whole(flat.shape),
    )
    out = kernel_call(functools.partial(final_kernel, plan), jax.ShapeDtypeStruct(flat.shape, F32), grid_spec=grid_spec)(
        select, own, other, flat, tz_h, tz_l, ty_h, ty_l
    )
    return out.reshape(conv.shape)


def swap(plan, value, outer=0, pair=0, yy=0, core=0):
    perm = []
    for gx in range(plan.count_gx):
        for gy in range(plan.count_gy):
            to_gx = gx ^ (outer * 2 + pair)
            to_gy = gy ^ (yy * 2 + core)
            perm.append((gx * plan.count_gy + gy, to_gx * plan.count_gy + to_gy))
    return lax.ppermute(value, ("gx", "gy"), perm)


def layer_paired(plan, features, conv_weight, mix_weight):
    rows = plan.rows
    at_gx, at_gy = lax.axis_index("gx"), lax.axis_index("gy")
    pair = at_gx % 2
    as_scalar = lambda v: v.astype(jnp.int32).reshape(1)
    select_y = as_scalar(at_gy * 2 + pair)
    select_x = as_scalar(at_gx)
    cells_x, cells_y = features.shape[1:3]

    x_low = ring(features[:, cells_x - 1 :], "gx", 1)
    x_high = ring(features[:, :1], "gx", -1)
    send, keep0, keep1, keep2, keep3, face0, face1 = forward_modes(plan, features, select_y)
    near, away = weight_parts(plan, mix_weight, as_scalar(pair))
    far = swap(plan, away, pair=1)
    bands = band_weights(conv_weight, cells_y)
    got = swap(plan, send, core=1)
    sums = [k + got[s * rows : (s + 1) * rows] for s, k in enumerate((keep0, keep1, keep2, keep3))]
    from_x = swap(plan, sums[1], pair=1)
    from_y = swap(plan, sums[2], yy=1)
    from_xy = swap(plan, sums[3], pair=1, yy=1)
    tables = table_halves(plan.table_x())
    chunks = x_call(plan, x_forward_kernel, [sums[0], from_x, from_y, from_xy], tables, plan.outer, select_x)
    parts = [chunks[0]] + [swap(plan, chunks[s], outer=s) for s in range(1, plan.outer)]
    mixed = mix_modes(plan, parts, near, far)
    parts = [mixed] + [swap(plan, mixed, outer=s) for s in range(1, plan.outer)]
    mine, theirs = x_call(plan, x_inverse_kernel, parts, tables, 2, select_x)
    from_x = swap(plan, theirs, pair=1)
    from_y = swap(plan, mine, yy=1)
    from_xy = swap(plan, theirs, pair=1, yy=1)
    own = jnp.concatenate([mine, from_x, from_y, from_xy], axis=0)
    other = swap(plan, own, core=1)

    def face(low, middle, high, y):
        return jnp.concatenate([low[:, :, y].transpose(1, 0, 2), middle, high[:, :, y].transpose(1, 0, 2)], axis=0)

    y_low = ring(face(x_low, face1, x_high, cells_y - 1), "gy", 1)
    y_high = ring(face(x_low, face0, x_high, 0), "gy", -1)
    conv = conv_bricks(features, x_low, x_high, y_low, y_high, bands)
    return final_layer(plan, own, other, conv, select_y)


def layer_any(features, conv_weight, mix_weight):
    bands = band_weights(conv_weight, features.shape[2])
    conv = conv_bricks(features, *halos(features), bands)
    return jax.nn.gelu(conv + spectral_any(features, mix_weight), approximate=False)


def shards(features, conv_weight, mix_weight):
    counts = lax.axis_size("gx"), lax.axis_size("gy")
    if Plan.fits(features.shape, *counts):
        return layer_paired(Plan(features.shape, *counts), features, conv_weight, mix_weight)
    return layer_any(features, conv_weight, mix_weight)


def solution(mesh):
    in_specs = (P(None, "gx", "gy", None), P(), P(None, None, None, "gy", "gx"))
    out_specs = P(None, "gx", "gy", None)
    return jax.shard_map(shards, mesh=mesh, in_specs=in_specs, out_specs=out_specs, check_vma=False)
```

time: 404 us -> 69.2 us (0.17)
  matrix products: 233 us -> 0 us
  local copies, waits for them, and re-layouts: 74.3 us -> 5.42 us
  blocking collectives: 56.7 us -> 0 us
  Pallas kernels: 0 us -> 20 us
  starting transfers between devices: 7.93 us -> 24.6 us
  waiting for transfers between devices: 3.68 us -> 18.6 us
  between operations: 14.5 us -> 0.21 us
  other arithmetic: 12.8 us -> 0.04 us
    conv_general_dilated x1 -> x0, matrix products: 213 us -> none  [shards(): lax.conv_general_dilated(wrapped[None], kernel, (1, 1, 1), 'VALID', dimen...]
    all_gather x2 -> x0, blocking collectives: 56.7 us -> none  [the longest x1 39.8 us: shards(): lax.all_gather(mixed_modes, 'gx', axis=2, tiled=True)]
    conv_general_dilated x5 -> x0, local copies, waits for them, and re-layouts: 42.6 us -> none  [shards(): lax.conv_general_dilated(wrapped[None], kernel, (1, 1, 1), 'VALID', dimen...]
    pallas_call x0 -> x8, Pallas kernels: none -> 20 us  [the longest x1 7.78 us: conv_bricks(): kernel_call(conv_kernel, jax.ShapeDtypeStruct(feat.shape, F32), [pltpu.VM...]
    dot_general x18 -> x0, matrix products: 19.7 us -> none  [the longest x1 4.19 us: shards(): jnp.dot(jnp.concatenate([plane_real, plane_imag], axis=3), table_back, pr...]
    ppermute x4 -> x19, starting transfers between devices: 7.89 us -> 24.6 us  [the longest x15 18.4 us: swap(): return lax.ppermute(value, ('gx', 'gy'), perm)]
    ppermute x4 -> x19, waiting for transfers between devices: 3.64 us -> 18.6 us  [the longest x15 17.1 us: swap(): return lax.ppermute(value, ('gx', 'gy'), perm)]
    conv_general_dilated x1 -> x0, other arithmetic: 9.53 us -> none  [shards(): lax.conv_general_dilated(wrapped[None], kernel, (1, 1, 1), 'VALID', dimen...]
  transfers between devices with their start and end apart: 6 -> 19, of which waited for: 3 -> 8; matrix products, arithmetic and copies ran while one was open for 67% -> 1% of each run, Pallas kernels for 0% -> 19%
where the time goes in v1:
time: 69.2 us; the launch traced here: 68.8 us
  starting transfers between devices  24.6 us (36%)
  Pallas kernels  20 us (29%)
  waiting for transfers between devices  18.6 us (27%)
  local copies, waits for them, and re-layouts  5.42 us (8%)
    ppermute x15, starting transfers between devices, swap(): return lax.ppermute(value, ('gx', 'gy'), perm)  18.4 us
    ppermute x15, waiting for transfers between devices, swap(): return lax.ppermute(value, ('gx', 'gy'), perm)  17.1 us
    pallas_call x1, Pallas kernels, conv_bricks(): kernel_call(conv_kernel, jax.ShapeDtypeStruct(feat.shape, F32), [pltpu.VM...  7.78 us
    ppermute x4, starting transfers between devices, ring(): lax.ppermute(value, axis, [(i, (i + step) % size) for i in range(size)])  6.21 us
    unnamed x27, local copies, waits for them, and re-layouts  5.3 us
    pallas_call x1, Pallas kernels, final_layer(): kernel_call(functools.partial(final_kernel, plan), jax.ShapeDtypeStruct(f...  3.71 us
    pallas_call x2, Pallas kernels, x_call(): kernel_call(functools.partial(body, plan), [part] * count, grid_spec=grid...  3.09 us
    pallas_call x1, Pallas kernels, forward_modes(): kernel_call(functools.partial(forward_kernel, plan), outs, grid_spec=grid...  2.83 us
  transfers between devices with their start and end apart: 19, of which 8 were waited for; matrix products, arithmetic and copies ran while one was open for 1% of the time, Pallas kernels for 19%

profile of v1, /device:TPU:0, one launch (start us, length us, event | category | flops | bytes accessed | tf_op | source)
XLA Modules:
  0.0 68.8 jit_solution(1369505042965152015)
XLA Ops:
  0.0 2.3 %copy-done = bf16[8,576,512]{2,1,0:T(8,128)(2,1)S(1)} copy-done((bf16[8,576,512]{2,1,0:T(8,128)(2,1)S(1)}, bf16[8,576,512]{2,1,0:T(8,128)(2,1)}, u32[]{:S(2)}) %copy-start) | copy-done | bytes 4718616
  2.3 1.2 %copy-done.2 = f32[16,8,16,128]{3,2,1,0:T(8,128)S(1)} copy-done((f32[16,8,16,128]{3,2,1,0:T(8,128)S(1)}, f32[16,8,16,128]{3,2,1,0:T(8,128)}, u32[]{:S(2)}) %copy-start.2) | copy-done | bytes 1048600
  3.6 0.7 %copy-done.6 = bf16[32,128]{1,0:T(8,128)(2,1)S(1)} copy-done((bf16[32,128]{1,0:T(8,128)(2,1)S(1)}, bf16[32,128]{1,0:T(8,128)(2,1)}, u32[]{:S(2)}) %copy-start.6) | copy-done | bytes 8216
  4.3 0.7 %copy-done.7 = bf16[32,128]{1,0:T(8,128)(2,1)S(1)} copy-done((bf16[32,128]{1,0:T(8,128)(2,1)S(1)}, bf16[32,128]{1,0:T(8,128)(2,1)}, u32[]{:S(2)}) %copy-start.7) | copy-done | bytes 8216
  5.0 2.8 %shard_map.127 = (f32[288,128]{1,0:T(8,128)S(1)}, f32[72,128]{1,0:T(8,128)S(1)}, f32[72,128]{1,0:T(8,128)S(1)}, f32[72,128]{1,0:T(8,128)S(1)}, f32[72,128]{1,0:T...) custom-call(s32[1]{0:T(128)} %bitcast.select, f32[2048,128]{1,0:T(8,128)S(1)} %bitcast.16, ...), custom_call_target="tpu_custom_call" | custom-call | tf_op jit(solution)/shard_map/pallas_call | solution.py:385
  7.8 0.5 collective-permute-start
  8.4 2.6 %collective-permute-start.15 = (f32[16,1,16,128]{3,0,2,1:T(8,128)S(1)}, f32[16,1,16,128]{3,0,2,1:T(8,128)S(1)}, u32[]{:S(2)}, u32[]{:S(2)}) collective-permute-start(f32[16,1,16,128]{3,0,2,1:T(8,128)S(1)} %copy.25), channel_id=1, source_target_pairs={{0,4},{4,8},{8,12},{12,16},{16,20},{20,24},{24,28},{28,0},{1,5},{5... | collective-permute-start | bytes 393224 | tf_op jit(solution)/shard_map/ppermute | solution.py:171
  11.0 3.1 %collective-permute-start.16 = (f32[16,1,16,128]{3,0,2,1:T(8,128)S(1)}, f32[16,1,16,128]{3,0,2,1:T(8,128)S(1)}, u32[]{:S(2)}, u32[]{:S(2)}) collective-permute-start(f32[16,1,16,128]{3,0,2,1:T(8,128)S(1)} %copy.26), channel_id=1, source_target_pairs={{0,28},{4,0},{8,4},{12,8},{16,12},{20,16},{24,20},{28,24},{1,29},{... | collective-permute-start | bytes 393224 | tf_op jit(solution)/shard_map/ppermute | solution.py:171
  14.1 0.5 shard_map.129
  14.8 3.2 %collective-permute-start.3 = (f32[72,128]{1,0:T(8,128)S(1)}, f32[72,128]{1,0:T(8,128)S(1)}, u32[]{:S(2)}, u32[]{:S(2)}) collective-permute-start(f32[72,128]{1,0:T(8,128)S(1)} %get-tuple-element.45), channel_id=1, source_target_pairs={{0,6},{1,7},{2,4},{3,5},{4,2},{5,3},{6,0},{7,1},{8,14},{9,15},{10,... | collective-permute-start | bytes 110600 | tf_op jit(solution)/shard_map/ppermute | solution.py:565
  18.3 1.7 %collective-permute-start.1 = (f32[72,128]{1,0:T(8,128)S(1)}, f32[72,128]{1,0:T(8,128)S(1)}, u32[]{:S(2)}, u32[]{:S(2)}) collective-permute-start(f32[72,128]{1,0:T(8,128)S(1)} %get-tuple-element.47), channel_id=1, source_target_pairs={{0,4},{1,5},{2,6},{3,7},{4,0},{5,1},{6,2},{7,3},{8,12},{9,13},{10,... | collective-permute-start | bytes 110600 | tf_op jit(solution)/shard_map/ppermute | solution.py:565
  20.0 7.2 %collective-permute-done.3.from_xy = f32[72,128]{1,0:T(8,128)S(1)} collective-permute-done((f32[72,128]{1,0:T(8,128)S(1)}, f32[72,128]{1,0:T(8,128)S(1)}, u32[]{:S(2)}, u32[]{:S(2)}) %collective-permute-start.3) | collective-permute-done | bytes 36896 | tf_op jit(solution)/shard_map/ppermute | solution.py:565
  27.2 1.4 %shard_map.128 = (f32[72,128]{1,0:T(8,128)S(1)}, f32[72,128]{1,0:T(8,128)S(1)}, f32[72,128]{1,0:T(8,128)S(1)}, f32[72,128]{1,0:T(8,128)S(1)}) custom-call(s32[1]{0:T(128)} %bitcast.1.select, f32[72,128]{1,0:T(8,128)S(1)} %get-tuple-element.48.own, f32[72,128]{1,0:T(8,128)S(1)} %collective-permute-done.1.from_x, f32[72,128]{1,0:T(8,128)S(1)} %collective-permute-done.2.from_y, ...), custom_call_target="tpu_custom_call" | custom-call | tf_op jit(solution)/shard_map/pallas_call | solution.py:432
  28.7 0.9 %collective-permute-start.4 = (f32[72,128]{1,0:T(8,128)S(1)}, f32[72,128]{1,0:T(8,128)S(1)}, u32[]{:S(2)}, u32[]{:S(2)}) collective-permute-start(f32[72,128]{1,0:T(8,128)S(1)} %get-tuple-element.30), channel_id=1, source_target_pairs={{0,8},{1,9},{2,10},{3,11},{4,12},{5,13},{6,14},{7,15},{8,0},{9,1},... | collective-permute-start | bytes 110600 | tf_op jit(solution)/shard_map/ppermute | solution.py:565
  29.6 2.6 %collective-permute-start.5 = (f32[72,128]{1,0:T(8,128)S(1)}, f32[72,128]{1,0:T(8,128)S(1)}, u32[]{:S(2)}, u32[]{:S(2)}) collective-permute-start(f32[72,128]{1,0:T(8,128)S(1)} %get-tuple-element.31), channel_id=1, source_target_pairs={{0,16},{1,17},{2,18},{3,19},{4,20},{5,21},{6,22},{7,23},{8,24},{9,... | collective-permute-start | bytes 110600 | tf_op jit(solution)/shard_map/ppermute | solution.py:565
  32.2 1.0 %collective-permute-start.6 = (f32[72,128]{1,0:T(8,128)S(1)}, f32[72,128]{1,0:T(8,128)S(1)}, u32[]{:S(2)}, u32[]{:S(2)}) collective-permute-start(f32[72,128]{1,0:T(8,128)S(1)} %get-tuple-element.32), channel_id=1, source_target_pairs={{0,24},{1,25},{2,26},{3,27},{4,28},{5,29},{6,30},{7,31},{8,16},{9,... | collective-permute-start | bytes 110600 | tf_op jit(solution)/shard_map/ppermute | solution.py:565
  33.1 2.1 %collective-permute-done.5.refs_2_ = f32[72,128]{1,0:T(8,128)S(1)} collective-permute-done((f32[72,128]{1,0:T(8,128)S(1)}, f32[72,128]{1,0:T(8,128)S(1)}, u32[]{:S(2)}, u32[]{:S(2)}) %collective-permute-start.5) | collective-permute-done | bytes 36896 | tf_op jit(solution)/shard_map/ppermute | solution.py:565
  35.2 2.7 %collective-permute-done.6.refs_3_ = f32[72,128]{1,0:T(8,128)S(1)} collective-permute-done((f32[72,128]{1,0:T(8,128)S(1)}, f32[72,128]{1,0:T(8,128)S(1)}, u32[]{:S(2)}, u32[]{:S(2)}) %collective-permute-start.6) | collective-permute-done | bytes 36896 | tf_op jit(solution)/shard_map/ppermute | solution.py:565
  38.4 1.0 %collective-permute-start.10 = (f32[72,128]{1,0:T(8,128)S(1)}, f32[72,128]{1,0:T(8,128)S(1)}, u32[]{:S(2)}, u32[]{:S(2)}) collective-permute-start(f32[72,128]{1,0:T(8,128)S(1)} %shard_map.130.refs_0_), channel_id=1, source_target_pairs={{0,24},{1,25},{2,26},{3,27},{4,28},{5,29},{6,30},{7,31},{8,16},{9,... | collective-permute-start | bytes 110600 | tf_op jit(solution)/shard_map/ppermute | solution.py:565
  39.4 3.4 %collective-permute-start.8 = (f32[72,128]{1,0:T(8,128)S(1)}, f32[72,128]{1,0:T(8,128)S(1)}, u32[]{:S(2)}, u32[]{:S(2)}) collective-permute-start(f32[72,128]{1,0:T(8,128)S(1)} %shard_map.130.refs_0_), channel_id=1, source_target_pairs={{0,8},{1,9},{2,10},{3,11},{4,12},{5,13},{6,14},{7,15},{8,0},{9,1},... | collective-permute-start | bytes 110600 | tf_op jit(solution)/shard_map/ppermute | solution.py:565
  42.9 1.3 %collective-permute-done.10.refs_3_ = f32[72,128]{1,0:T(8,128)S(1)} collective-permute-done((f32[72,128]{1,0:T(8,128)S(1)}, f32[72,128]{1,0:T(8,128)S(1)}, u32[]{:S(2)}, u32[]{:S(2)}) %collective-permute-start.10) | collective-permute-done | bytes 36896 | tf_op jit(solution)/shard_map/ppermute | solution.py:565
  44.2 0.9 %collective-permute-done.9.refs_2_ = f32[72,128]{1,0:T(8,128)S(1)} collective-permute-done((f32[72,128]{1,0:T(8,128)S(1)}, f32[72,128]{1,0:T(8,128)S(1)}, u32[]{:S(2)}, u32[]{:S(2)}) %collective-permute-start.9) | collective-permute-done | bytes 36896 | tf_op jit(solution)/shard_map/ppermute | solution.py:565
  45.1 1.6 %shard_map.131 = (f32[72,128]{1,0:T(8,128)S(1)}, f32[72,128]{1,0:T(8,128)S(1)}) custom-call(s32[1]{0:T(128)} %bitcast.1.select, f32[72,128]{1,0:T(8,128)S(1)} %shard_map.130.refs_0_, f32[72,128]{1,0:T(8,128)S(1)} %collective-permute-done.8.refs_1_, f32[72,128]{1,0:T(8,128)S(1)} %collective-permute-done.9.refs_2_, ...), custom_call_target="tpu_custom_call" | custom-call | tf_op jit(solution)/shard_map/pallas_call | solution.py:432
  46.8 1.1 %collective-permute-start.13 = (f32[72,128]{1,0:T(8,128)S(1)}, f32[72,128]{1,0:T(8,128)S(1)}, u32[]{:S(2)}, u32[]{:S(2)}) collective-permute-start(f32[72,128]{1,0:T(8,128)S(1)} %get-tuple-element.36), channel_id=1, source_target_pairs={{0,6},{1,7},{2,4},{3,5},{4,2},{5,3},{6,0},{7,1},{8,14},{9,15},{10,... | collective-permute-start | bytes 110600 | tf_op jit(solution)/shard_map/ppermute | solution.py:565
  47.8 1.5 %collective-permute-start.11 = (f32[72,128]{1,0:T(8,128)S(1)}, f32[72,128]{1,0:T(8,128)S(1)}, u32[]{:S(2)}, u32[]{:S(2)}) collective-permute-start(f32[72,128]{1,0:T(8,128)S(1)} %get-tuple-element.36), channel_id=1, source_target_pairs={{0,4},{1,5},{2,6},{3,7},{4,0},{5,1},{6,2},{7,3},{8,12},{9,13},{10,... | collective-permute-start | bytes 110600 | tf_op jit(solution)/shard_map/ppermute | solution.py:565
  49.3 1.0 %collective-permute-start.12 = (f32[72,128]{1,0:T(8,128)S(1)}, f32[72,128]{1,0:T(8,128)S(1)}, u32[]{:S(2)}, u32[]{:S(2)}) collective-permute-start(f32[72,128]{1,0:T(8,128)S(1)} %get-tuple-element.35), channel_id=1, source_target_pairs={{0,2},{1,3},{2,0},{3,1},{4,6},{5,7},{6,4},{7,5},{8,10},{9,11},{10,... | collective-permute-start | bytes 110600 | tf_op jit(solution)/shard_map/ppermute | solution.py:565
  50.3 1.5 %collective-permute-done.11 = f32[72,128]{1,0:T(8,128)S(1)} collective-permute-done((f32[72,128]{1,0:T(8,128)S(1)}, f32[72,128]{1,0:T(8,128)S(1)}, u32[]{:S(2)}, u32[]{:S(2)}) %collective-permute-start.11) | collective-permute-done | bytes 36896 | tf_op jit(solution)/shard_map/ppermute | solution.py:565
  51.8 1.5 %collective-permute-done.12 = f32[72,128]{1,0:T(8,128)S(1)} collective-permute-done((f32[72,128]{1,0:T(8,128)S(1)}, f32[72,128]{1,0:T(8,128)S(1)}, u32[]{:S(2)}, u32[]{:S(2)}) %collective-permute-start.12) | collective-permute-done | bytes 36896 | tf_op jit(solution)/shard_map/ppermute | solution.py:565
  54.1 1.6 %shard_map.132 = (bf16[768,768]{1,0:T(8,128)(2,1)S(1)}, bf16[768,768]{1,0:T(8,128)(2,1)S(1)}, bf16[3,768,32]{2,1,0:T(8,128)(2,1)S(1)}, bf16[3,768,32]{2,1,0:T(8,128)(2,1)S(1)}) custom-call(f32[432,16]{1,0:T(8,128)S(1)} %bitcast.19), custom_call_target="tpu_custom_call" | custom-call | tf_op jit(solution)/shard_map/pallas_call | solution.py:107
  55.8 1.5 %collective-permute-done.17.y_low = f32[10,16,128]{2,1,0:T(8,128)S(1)} collective-permute-done((f32[10,16,128]{2,1,0:T(8,128)S(1)}, f32[10,16,128]{2,1,0:T(8,128)S(1)}, u32[]{:S(2)}, u32[]{:S(2)}) %collective-permute-start.17) | collective-permute-done | bytes 81952 | tf_op jit(solution)/shard_map/ppermute | solution.py:171
  57.3 7.8 %shard_map.133 = f32[16,8,16,128]{3,2,1,0:T(8,128)S(1)} custom-call(f32[16,8,16,128]{3,2,1,0:T(8,128)S(1)} %copy-done.3, f32[16,1,16,128]{3,2,1,0:T(8,128)S(1)} %copy.22.x_low, f32[16,1,16,128]{3,2,1,0:T(8,128)S(1)} %copy.23.x_high, f32[10,16,128]{2,1,0:T(8,128)S(1)} %collective-permute-done.17.y_low, f32[10,16,128]{2,1,0:T(8,128)S(1)} %collective-permute-done.18.y_high, ...), custom_call_target="tpu_custom_call" | custom-call | tf_op jit(solution)/shard_map/pallas_call | solution.py:157
  65.1 3.7 %shard_map.134 = f32[2048,128]{1,0:T(8,128)} custom-call(s32[1]{0:T(128)} %bitcast.select, f32[288,128]{1,0:T(8,128)S(1)} %constant_dynamic-update-slice_fusion.own, f32[288,128]{1,0:T(8,128)S(1)} %collective-permute-done.14.other, f32[2048,128]{1,0:T(8,128)S(1)} %bitcast.17, bf16[128,512]{1,0:T(8,128)(2,1)S(1)} %copy-done.5, ...), custom_call_target="tpu_custom_call" | custom-call | tf_op jit(solution)/shard_map/pallas_call | solution.py:552
  (50 shorter events, 2.0 us)
Async XLA Ops:
  0.0 2.3 %copy-start = (bf16[8,576,512]{2,1,0:T(8,128)(2,1)S(1)}, bf16[8,576,512]{2,1,0:T(8,128)(2,1)}, u32[]{:S(2)}) copy-start(bf16[8,576,512]{2,1,0:T(8,128)(2,1)} %constant.40.clone.ty_h) | copy-start | bytes 14155780
  2.3 1.2 %copy-start.2 = (f32[16,8,16,128]{3,2,1,0:T(8,128)S(1)}, f32[16,8,16,128]{3,2,1,0:T(8,128)}, u32[]{:S(2)}) copy-start(f32[16,8,16,128]{3,2,1,0:T(8,128)} %feat.1) | copy-start | bytes 3145732
  3.6 0.7 %copy-start.6 = (bf16[32,128]{1,0:T(8,128)(2,1)S(1)}, bf16[32,128]{1,0:T(8,128)(2,1)}, u32[]{:S(2)}) copy-start(bf16[32,128]{1,0:T(8,128)(2,1)} %constant.39.clone.tz_l) | copy-start | bytes 24580
  4.3 0.7 %copy-start.7 = (bf16[32,128]{1,0:T(8,128)(2,1)S(1)}, bf16[32,128]{1,0:T(8,128)(2,1)}, u32[]{:S(2)}) copy-start(bf16[32,128]{1,0:T(8,128)(2,1)} %constant.38.clone.tz_h) | copy-start | bytes 24580
  5.0 9.1 %copy-start.8 = (f32[2,16,16,1,216]{4,3,2,1,0:T(1,128)S(1)}, f32[2,16,16,1,216]{4,3,2,1,0:T(1,128)}, u32[]{:S(2)}) copy-start(f32[2,16,16,1,216]{4,3,2,1,0:T(1,128)} %param.15) | copy-start | bytes 1327108
  5.0 22.3 %copy-start.1 = (bf16[8,256,1024]{2,1,0:T(8,128)(2,1)S(1)}, bf16[8,256,1024]{2,1,0:T(8,128)(2,1)}, u32[]{:S(2)}) copy-start(bf16[8,256,1024]{2,1,0:T(8,128)(2,1)} %constant.42.clone.tx_h.refs_4_) | copy-start | bytes 12582916
  7.8 6.9 %collective-permute-start = (f32[288,128]{1,0:T(8,128)S(1)}, f32[288,128]{1,0:T(8,128)S(1)}, u32[]{:S(2)}, u32[]{:S(2)}) collective-permute-start(f32[288,128]{1,0:T(8,128)S(1)} %get-tuple-element.25), channel_id=1, source_target_pairs={{0,1},{1,0},{2,3},{3,2},{4,5},{5,4},{6,7},{7,6},{8,9},{9,8},{10,11... | collective-permute-start | bytes 442376 | tf_op jit(solution)/shard_map/ppermute | solution.py:565
  8.4 9.9 %collective-permute-start.15 = (f32[16,1,16,128]{3,0,2,1:T(8,128)S(1)}, f32[16,1,16,128]{3,0,2,1:T(8,128)S(1)}, u32[]{:S(2)}, u32[]{:S(2)}) collective-permute-start(f32[16,1,16,128]{3,0,2,1:T(8,128)S(1)} %copy.25), channel_id=1, source_target_pairs={{0,4},{4,8},{8,12},{12,16},{16,20},{20,24},{24,28},{28,0},{1,5},{5... | collective-permute-start | bytes 393224 | tf_op jit(solution)/shard_map/ppermute | solution.py:171
  11.0 22.2 %collective-permute-start.16 = (f32[16,1,16,128]{3,0,2,1:T(8,128)S(1)}, f32[16,1,16,128]{3,0,2,1:T(8,128)S(1)}, u32[]{:S(2)}, u32[]{:S(2)}) collective-permute-start(f32[16,1,16,128]{3,0,2,1:T(8,128)S(1)} %copy.26), channel_id=1, source_target_pairs={{0,28},{4,0},{8,4},{12,8},{16,12},{20,16},{24,20},{28,24},{1,29},{... | collective-permute-start | bytes 393224 | tf_op jit(solution)/shard_map/ppermute | solution.py:171
  14.6 23.3 %collective-permute-start.7 = (f32[2,256,128]{2,1,0:T(8,128)S(1)}, f32[2,256,128]{2,1,0:T(8,128)S(1)}, u32[]{:S(2)}, u32[]{:S(2)}) collective-permute-start(f32[2,256,128]{2,1,0:T(8,128)S(1)} %get-tuple-element.34), channel_id=1, source_target_pairs={{0,4},{1,5},{2,6},{3,7},{4,0},{5,1},{6,2},{7,3},{8,12},{9,13},{10,... | collective-permute-start | bytes 786440 | tf_op jit(solution)/shard_map/ppermute | solution.py:565
  14.8 12.5 %collective-permute-start.3 = (f32[72,128]{1,0:T(8,128)S(1)}, f32[72,128]{1,0:T(8,128)S(1)}, u32[]{:S(2)}, u32[]{:S(2)}) collective-permute-start(f32[72,128]{1,0:T(8,128)S(1)} %get-tuple-element.45), channel_id=1, source_target_pairs={{0,6},{1,7},{2,4},{3,5},{4,2},{5,3},{6,0},{7,1},{8,14},{9,15},{10,... | collective-permute-start | bytes 110600 | tf_op jit(solution)/shard_map/ppermute | solution.py:565
  18.0 9.3 %collective-permute-start.2 = (f32[72,128]{1,0:T(8,128)S(1)}, f32[72,128]{1,0:T(8,128)S(1)}, u32[]{:S(2)}, u32[]{:S(2)}) collective-permute-start(f32[72,128]{1,0:T(8,128)S(1)} %get-tuple-element.46), channel_id=1, source_target_pairs={{0,2},{1,3},{2,0},{3,1},{4,6},{5,7},{6,4},{7,5},{8,10},{9,11},{10,... | collective-permute-start | bytes 110600 | tf_op jit(solution)/shard_map/ppermute | solution.py:565
  18.3 8.9 %collective-permute-start.1 = (f32[72,128]{1,0:T(8,128)S(1)}, f32[72,128]{1,0:T(8,128)S(1)}, u32[]{:S(2)}, u32[]{:S(2)}) collective-permute-start(f32[72,128]{1,0:T(8,128)S(1)} %get-tuple-element.47), channel_id=1, source_target_pairs={{0,4},{1,5},{2,6},{3,7},{4,0},{5,1},{6,2},{7,3},{8,12},{9,13},{10,... | collective-permute-start | bytes 110600 | tf_op jit(solution)/shard_map/ppermute | solution.py:565
  28.7 4.5 %collective-permute-start.4 = (f32[72,128]{1,0:T(8,128)S(1)}, f32[72,128]{1,0:T(8,128)S(1)}, u32[]{:S(2)}, u32[]{:S(2)}) collective-permute-start(f32[72,128]{1,0:T(8,128)S(1)} %get-tuple-element.30), channel_id=1, source_target_pairs={{0,8},{1,9},{2,10},{3,11},{4,12},{5,13},{6,14},{7,15},{8,0},{9,1},... | collective-permute-start | bytes 110600 | tf_op jit(solution)/shard_map/ppermute | solution.py:565
  29.6 5.6 %collective-permute-start.5 = (f32[72,128]{1,0:T(8,128)S(1)}, f32[72,128]{1,0:T(8,128)S(1)}, u32[]{:S(2)}, u32[]{:S(2)}) collective-permute-start(f32[72,128]{1,0:T(8,128)S(1)} %get-tuple-element.31), channel_id=1, source_target_pairs={{0,16},{1,17},{2,18},{3,19},{4,20},{5,21},{6,22},{7,23},{8,24},{9,... | collective-permute-start | bytes 110600 | tf_op jit(solution)/shard_map/ppermute | solution.py:565
  32.2 5.8 %collective-permute-start.6 = (f32[72,128]{1,0:T(8,128)S(1)}, f32[72,128]{1,0:T(8,128)S(1)}, u32[]{:S(2)}, u32[]{:S(2)}) collective-permute-start(f32[72,128]{1,0:T(8,128)S(1)} %get-tuple-element.32), channel_id=1, source_target_pairs={{0,24},{1,25},{2,26},{3,27},{4,28},{5,29},{6,30},{7,31},{8,16},{9,... | collective-permute-start | bytes 110600 | tf_op jit(solution)/shard_map/ppermute | solution.py:565
  38.4 5.9 %collective-permute-start.10 = (f32[72,128]{1,0:T(8,128)S(1)}, f32[72,128]{1,0:T(8,128)S(1)}, u32[]{:S(2)}, u32[]{:S(2)}) collective-permute-start(f32[72,128]{1,0:T(8,128)S(1)} %shard_map.130.refs_0_), channel_id=1, source_target_pairs={{0,24},{1,25},{2,26},{3,27},{4,28},{5,29},{6,30},{7,31},{8,16},{9,... | collective-permute-start | bytes 110600 | tf_op jit(solution)/shard_map/ppermute | solution.py:565
  39.4 5.7 %collective-permute-start.9 = (f32[72,128]{1,0:T(8,128)S(1)}, f32[72,128]{1,0:T(8,128)S(1)}, u32[]{:S(2)}, u32[]{:S(2)}) collective-permute-start(f32[72,128]{1,0:T(8,128)S(1)} %shard_map.130.refs_0_), channel_id=1, source_target_pairs={{0,16},{1,17},{2,18},{3,19},{4,20},{5,21},{6,22},{7,23},{8,24},{9,... | collective-permute-start | bytes 110600 | tf_op jit(solution)/shard_map/ppermute | solution.py:565
  39.4 5.7 %collective-permute-start.8 = (f32[72,128]{1,0:T(8,128)S(1)}, f32[72,128]{1,0:T(8,128)S(1)}, u32[]{:S(2)}, u32[]{:S(2)}) collective-permute-start(f32[72,128]{1,0:T(8,128)S(1)} %shard_map.130.refs_0_), channel_id=1, source_target_pairs={{0,8},{1,9},{2,10},{3,11},{4,12},{5,13},{6,14},{7,15},{8,0},{9,1},... | collective-permute-start | bytes 110600 | tf_op jit(solution)/shard_map/ppermute | solution.py:565
  42.8 11.0 %copy-start.9 = (f32[27,16,16]{0,2,1:T(8,128)S(1)}, f32[27,16,16]{0,2,1:T(8,128)}, u32[]{:S(2)}) copy-start(f32[27,16,16]{0,2,1:T(8,128)} %param.14) | copy-start | bytes 82948
  42.8 14.5 %copy-start.3 = (f32[16,8,16,128]{3,2,1,0:T(8,128)S(1)}, f32[16,8,16,128]{3,2,1,0:T(8,128)}, u32[]{:S(2)}) copy-start(f32[16,8,16,128]{3,2,1,0:T(8,128)} %feat.1) | copy-start | bytes 3145732
  42.9 12.9 %collective-permute-start.18 = (f32[10,16,128]{2,1,0:T(8,128)S(1)}, f32[10,16,128]{2,1,0:T(8,128)S(1)}, u32[]{:S(2)}, u32[]{:S(2)}) collective-permute-start(f32[10,16,128]{2,1,0:T(8,128)S(1)} %pad_maximum_fusion.1), channel_id=1, source_target_pairs={{0,3},{1,0},{2,1},{3,2},{4,7},{5,4},{6,5},{7,6},{8,11},{9,8},{10,9... | collective-permute-start | bytes 245768 | tf_op jit(solution)/shard_map/ppermute | solution.py:171
  46.8 18.3 %copy-start.4 = (bf16[128,512]{1,0:T(8,128)(2,1)S(1)}, bf16[128,512]{1,0:T(8,128)(2,1)}, u32[]{:S(2)}) copy-start(bf16[128,512]{1,0:T(8,128)(2,1)} %constant.45.clone.tz_l) | copy-start | bytes 393220
  46.8 18.3 %copy-start.5 = (bf16[128,512]{1,0:T(8,128)(2,1)S(1)}, bf16[128,512]{1,0:T(8,128)(2,1)}, u32[]{:S(2)}) copy-start(bf16[128,512]{1,0:T(8,128)(2,1)} %constant.44.clone.tz_h) | copy-start | bytes 393220
  46.8 6.5 %collective-permute-start.13 = (f32[72,128]{1,0:T(8,128)S(1)}, f32[72,128]{1,0:T(8,128)S(1)}, u32[]{:S(2)}, u32[]{:S(2)}) collective-permute-start(f32[72,128]{1,0:T(8,128)S(1)} %get-tuple-element.36), channel_id=1, source_target_pairs={{0,6},{1,7},{2,4},{3,5},{4,2},{5,3},{6,0},{7,1},{8,14},{9,15},{10,... | collective-permute-start | bytes 110600 | tf_op jit(solution)/shard_map/ppermute | solution.py:565
  47.8 4.0 %collective-permute-start.11 = (f32[72,128]{1,0:T(8,128)S(1)}, f32[72,128]{1,0:T(8,128)S(1)}, u32[]{:S(2)}, u32[]{:S(2)}) collective-permute-start(f32[72,128]{1,0:T(8,128)S(1)} %get-tuple-element.36), channel_id=1, source_target_pairs={{0,4},{1,5},{2,6},{3,7},{4,0},{5,1},{6,2},{7,3},{8,12},{9,13},{10,... | collective-permute-start | bytes 110600 | tf_op jit(solution)/shard_map/ppermute | solution.py:565
  49.3 4.0 %collective-permute-start.12 = (f32[72,128]{1,0:T(8,128)S(1)}, f32[72,128]{1,0:T(8,128)S(1)}, u32[]{:S(2)}, u32[]{:S(2)}) collective-permute-start(f32[72,128]{1,0:T(8,128)S(1)} %get-tuple-element.35), channel_id=1, source_target_pairs={{0,2},{1,3},{2,0},{3,1},{4,6},{5,7},{6,4},{7,5},{8,10},{9,11},{10,... | collective-permute-start | bytes 110600 | tf_op jit(solution)/shard_map/ppermute | solution.py:565
  53.3 11.8 %collective-permute-start.14 = (f32[288,128]{1,0:T(8,128)S(1)}, f32[288,128]{1,0:T(8,128)S(1)}, u32[]{:S(2)}, u32[]{:S(2)}) collective-permute-start(f32[288,128]{1,0:T(8,128)S(1)} %constant_dynamic-update-slice_fusion.own), channel_id=1, source_target_pairs={{0,1},{1,0},{2,3},{3,2},{4,5},{5,4},{6,7},{7,6},{8,9},{9,8},{10,11... | collective-permute-start | bytes 442376 | tf_op jit(solution)/shard_map/ppermute | solution.py:565
  53.4 3.9 %collective-permute-start.17 = (f32[10,16,128]{2,1,0:T(8,128)S(1)}, f32[10,16,128]{2,1,0:T(8,128)S(1)}, u32[]{:S(2)}, u32[]{:S(2)}) collective-permute-start(f32[10,16,128]{2,1,0:T(8,128)S(1)} %pad_maximum_fusion), channel_id=1, source_target_pairs={{0,1},{1,2},{2,3},{3,0},{4,5},{5,6},{6,7},{7,4},{8,9},{9,10},{10,1... | collective-permute-start | bytes 245768 | tf_op jit(solution)/shard_map/ppermute | solution.py:171

commit v2 on v0

v2 whole, which is shorter than its diff:
```python
import functools
import math

import jax
import jax.numpy as jnp
import ml_dtypes
import numpy as np
from jax import lax
from jax.experimental import pallas as pl
from jax.experimental.pallas import tpu as pltpu
from jax.sharding import PartitionSpec as P

KX = 24
KY = 24
KZ = 12
LANES = 128
F32 = jnp.float32
BF16 = jnp.bfloat16
PRECISE = lax.Precision.HIGHEST
VMEM_LIMIT = 24 * 1024 * 1024
NN = (((1,), (0,)), ((), ()))
NT = (((1,), (1,)), ((), ()))


def kernel_call(body, out_shape, scratch=(), grid_spec=None, **kw):
    params = pltpu.CompilerParams(vmem_limit_bytes=VMEM_LIMIT)
    if grid_spec is not None:
        kw["grid_spec"] = grid_spec
    else:
        kw["scratch_shapes"] = list(scratch)
    return pl.pallas_call(body, out_shape=out_shape, compiler_params=params, **kw)


def halves(value):
    high = value.astype(BF16)
    return high, (value - high.astype(F32)).astype(BF16)


def dot(a, b, dims=NN):
    return lax.dot_general(a, b, dims, preferred_element_type=F32)


def dot3(a, b, dims=NN):
    return dot(a[0], b[0], dims) + (dot(a[0], b[1], dims) + dot(a[1], b[0], dims))


def table_halves(table):
    table = np.asarray(table, np.float64)
    high = table.astype(ml_dtypes.bfloat16)
    low = (table - high.astype(np.float64)).astype(ml_dtypes.bfloat16)
    return high, low


def triple(parts, axis, twice_high_around):
    high, low = parts
    return jnp.concatenate([high, low, high] if twice_high_around else [high, high, low], axis=axis)


def kept_np(amount, length):
    index = np.arange(amount)
    return np.where(index < amount // 2, index, length - amount + index)


def angles_np(positions, frequencies, length):
    return 2.0 * np.pi * ((positions[:, None] * frequencies[None, :]) % length) / length


def split_kernel(feat, high, low):
    channels, cells_x, cells_y, length_z = feat.shape
    for x in range(cells_x):
        for y in range(cells_y):
            high[y, x], low[y, x] = halves(feat[:, x, y, :])


def conv_kernel(first, rows_y, count_gy, place, own_h, own_l, near_x, far_x, near_y, far_y, weight, after, out, token, edge_h, edge_l, rim_h, rim_l):
    cells_y, cells_x, channels, length_z = own_h.shape
    count = out.shape[0]
    span = rows_y + 2
    depth = 3 * span * channels
    even_x, even_y = place[0] // count_gy % 2 == 0, place[0] % count_gy % 2 == 0
    column, row = (cells_y + 2) * channels, cells_x * channels

    def tail(ref, size, at):
        return ref[ref.shape[0] - size + at : ref.shape[0] - size + at + channels, :]

    def pick(side, even, near, far, size, at):
        near, far = (tail(ref, size, at * channels) for ref in (near, far))
        return halves(jnp.where(even, near, far) if side else jnp.where(even, far, near))

    for side in range(2):
        if (0, cells_x + 1)[side] in range(first, first + count + 2):
            for y in range(cells_y):
                edge_h[side, y + 1], edge_l[side, y + 1] = pick(side, even_x, near_x, far_x, column, y)
            corners = [
                jnp.where(even_x == bool(side), *(tail(ref, column, (cells_y + n) * channels) for ref in (near_x, far_x)))
                for n in range(2)
            ]
            for up in range(2):
                value = jnp.where(even_y == bool(up), *corners)
                edge_h[side, up * (cells_y + 1)], edge_l[side, up * (cells_y + 1)] = halves(value)
        for x in range(max(first - 1, 0), min(first + count + 1, cells_x)):
            rim_h[side, x], rim_l[side, x] = pick(side, even_y, near_y, far_y, row, x)

    def cell(which, x, y):
        own, edge, rim = ((own_h, edge_h, rim_h), (own_l, edge_l, rim_l))[which]
        if x in (0, cells_x + 1):
            return edge[0 if x == 0 else 1, y]
        if y in (0, cells_y + 1):
            return rim[0 if y == 0 else 1, x - 1]
        return own[y - 1, x - 1]

    taps = halves(weight[...])
    tap = lax.broadcasted_iota(jnp.int32, (weight.shape[1], depth), 0)
    at = lax.broadcasted_iota(jnp.int32, (weight.shape[1], depth), 1)
    tap_a, tap_b, tap_i = tap // (3 * channels), tap // channels % 3, tap % channels
    at_a, at_y, at_i = at // (span * channels), at // channels % span, at % channels
    bands = [[], []]
    for y in range(rows_y):
        match = (tap_a == at_a) & (tap_b + y == at_y) & (tap_i == at_i)
        match = jnp.where(match, 1.0, 0.0).astype(BF16)
        for which in range(2):
            bands[which].append(dot(taps[which], match).astype(BF16))
    bands = [jnp.concatenate(b, axis=0) for b in bands]
    for x in range(0, count, 2):
        for y in range(0, cells_y, rows_y):
            field = []
            for which in range(2):
                columns = []
                for p in range(2):
                    cells = [cell(which, first + x + p + a, y + k) for a in range(3) for k in range(span)]
                    columns.append(jnp.concatenate(cells, axis=0))
                field.append(jnp.concatenate(columns, axis=1))
            value = dot3(bands, field)
            for k in range(rows_y):
                for p in range(2):
                    total = None
                    for c in range(3):
                        row = (k * 3 + c) * channels
                        piece = value[row : row + channels, p * length_z : (p + 1) * length_z]
                        if c != 1:
                            piece = pltpu.roll(piece, (1 - c) % length_z, 1)
                        total = piece if total is None else total + piece
                    out[x + p, y + k] = total
    token[...] = jnp.zeros(token.shape, F32)


def conv_taps(conv_weight):
    channels = conv_weight.shape[1]
    taps = conv_weight.reshape(3, 3, 3, channels, channels).transpose(2, 3, 0, 1, 4)
    return taps.reshape(3 * channels, 9 * channels)


def specs(count, first=None):
    vmem = pl.BlockSpec(memory_space=pltpu.VMEM)
    return [pl.BlockSpec(memory_space=pltpu.SMEM)] + [vmem] * count


def conv_bricks(place, own, near_x, far_x, near_y, far_y, taps, after, first, count):
    cells_y, cells_x, channels, length_z = own[0].shape
    return kernel_call(
        functools.partial(conv_kernel, first, 2, lax.axis_size("gy")),
        [jax.ShapeDtypeStruct((count, cells_y, channels, length_z), F32), jax.ShapeDtypeStruct((8, LANES), F32)],
        [pltpu.VMEM((2, cells_y + 2, channels, length_z), BF16)] * 2 + [pltpu.VMEM((2, cells_x, channels, length_z), BF16)] * 2,
        in_specs=specs(8),
    )(place, *own, near_x, far_x, near_y, far_y, taps, after)


def ring(value, axis, step):
    size = lax.axis_size(axis)
    return lax.ppermute(value, axis, [(i, (i + step) % size) for i in range(size)])


def halos(features):
    channels, cells_x, cells_y, length_z = features.shape
    flat = lambda v: v.transpose(1, 0, 2).reshape(-1, length_z)
    low_y = ring(features[:, :, cells_y - 1], "gy", 1)
    high_y = ring(features[:, :, 0], "gy", -1)

    def face(x):
        return jnp.concatenate([features[:, x], high_y[:, x][:, None], low_y[:, x][:, None]], axis=1)

    low_x = ring(face(cells_x - 1), "gx", 1)
    high_x = ring(face(0), "gx", -1)
    return flat(high_x), flat(low_x), flat(high_y), flat(low_y)


def angle_tables(positions, frequencies, length):
    product = positions[:, None] * frequencies[None, :] % length
    angles = product.astype(jnp.float32) * (2.0 * math.pi / length)
    return (jnp.cos(angles), jnp.sin(angles))


def kept_frequencies(amount, length):
    index = jnp.arange(amount, dtype=jnp.int32)
    return jnp.where(index < amount // 2, index, length - amount + index)


def times(form, a, b, c, d):
    one = functools.partial(jnp.einsum, form, precision=PRECISE)
    return one(a, c) + one(b, d)


def spectral_any(features, mix_weight):
    channels, cells_x, cells_y, length_z = features.shape
    count_gx = lax.axis_size("gx")
    count_gy = lax.axis_size("gy")
    length_x = cells_x * count_gx
    length_y = cells_y * count_gy
    block_yz = KY * KZ // count_gy
    cos_z, sin_z = angle_tables(jnp.arange(length_z, dtype=jnp.int32), jnp.arange(KZ, dtype=jnp.int32), length_z)
    y_places = lax.axis_index("gy") * cells_y + jnp.arange(cells_y, dtype=jnp.int32)
    x_places = lax.axis_index("gx") * cells_x + jnp.arange(cells_x, dtype=jnp.int32)
    cos_y, sin_y = angle_tables(y_places, kept_frequencies(KY, length_y), length_y)
    cos_x, sin_x = angle_tables(x_places, kept_frequencies(KX, length_x), length_x)
    along_z = jnp.dot(features, jnp.concatenate([cos_z, -sin_z], axis=1), precision=PRECISE)
    z_real = along_z[..., :KZ]
    z_imag = along_z[..., KZ:]
    y_real = times("cxyk,yq->cxqk", z_real, z_imag, cos_y, sin_y)
    y_imag = times("cxyk,yq->cxqk", z_imag, z_real, cos_y, -sin_y)
    partial_value = jnp.stack([y_real, y_imag], axis=2).reshape(channels, cells_x, 2, KY * KZ)
    y_share = lax.psum_scatter(partial_value, "gy", scatter_dimension=3, tiled=True)
    x_real = times("cxm,xp->cpm", y_share[:, :, 0], y_share[:, :, 1], cos_x, sin_x)
    x_imag = times("cxm,xp->cpm", y_share[:, :, 1], y_share[:, :, 0], cos_x, -sin_x)
    x_partial = jnp.stack([x_real, x_imag], axis=1).reshape(channels, 2, KX * block_yz)
    owned_modes = lax.psum_scatter(x_partial, "gx", scatter_dimension=2, tiled=True)
    owned_modes = owned_modes * (1.0 / math.sqrt(length_x * length_y * length_z))
    coef_real = owned_modes[:, 0]
    coef_imag = owned_modes[:, 1]
    weight_real = mix_weight[0, :, :, 0, :]
    weight_imag = mix_weight[1, :, :, 0, :]
    mixed_real = times("oim,im->om", weight_real, weight_imag, coef_real, -coef_imag)
    mixed_imag = times("oim,im->om", weight_real, weight_imag, coef_imag, coef_real)
    mixed_modes = jnp.stack([mixed_real, mixed_imag], axis=1)
    row_modes = lax.all_gather(mixed_modes, "gx", axis=2, tiled=True).reshape(channels, 2, KX, block_yz)
    back_real = times("cpm,xp->cxm", row_modes[:, 0], row_modes[:, 1], cos_x, -sin_x)
    back_imag = times("cpm,xp->cxm", row_modes[:, 1], row_modes[:, 0], cos_x, sin_x)
    gathered = lax.all_gather(jnp.stack([back_real, back_imag], axis=2), "gy", axis=3, tiled=True)
    back_real = gathered[:, :, 0].reshape(channels, cells_x, KY, KZ)
    back_imag = gathered[:, :, 1].reshape(channels, cells_x, KY, KZ)
    plane_real = times("cxqk,yq->cxyk", back_real, back_imag, cos_y, -sin_y)
    plane_imag = times("cxqk,yq->cxyk", back_imag, back_real, cos_y, sin_y)
    table_back = jnp.concatenate([cos_z.T, -sin_z.T], axis=0)
    planes = jnp.concatenate([plane_real, plane_imag], axis=3)
    return jnp.dot(planes, table_back, precision=PRECISE) * (1.0 / math.sqrt(KX * KY * KZ))


class Plan:
    def __init__(self, feature_shape, count_gx, count_gy):
        self.channels, self.cells_x, self.cells_y, self.length_z = feature_shape
        self.count_gx, self.count_gy = count_gx, count_gy
        self.outer = count_gx // 2
        self.block = KY * KZ // count_gy
        self.part = self.block // 2
        self.per_gx = KX // count_gx
        self.rows = 2 * self.part
        self.pad_k = -(-KZ // 8) * 8
        self.pad_z = 2 * self.pad_k
        self.turns = self.part // KZ
        self.length_x = self.cells_x * count_gx
        self.length_y = self.cells_y * count_gy

    def spot(self, place):
        return place[0] // self.count_gy, place[0] % self.count_gy

    @staticmethod
    def fits(feature_shape, count_gx, count_gy):
        channels, cells_x, cells_y, length_z = feature_shape
        outer = count_gx // 2
        if count_gy != 4 or count_gx % 2 or outer & (outer - 1) or outer > 4:
            return False
        if KX % count_gx or (KY * KZ) % (2 * count_gy) or channels * cells_x != LANES:
            return False
        part = KY * KZ // count_gy // 2
        per = KX // count_gx
        return (
            length_z == LANES
            and cells_y % (LANES // (2 * (-(-KZ // 8) * 8))) == 0
            and channels % 16 == 0
            and (2 * part) % 8 == 0
            and 4 * 2 * part % 16 == 0
            and part % KZ == 0
            and per * part <= LANES
            and 2 * per * channels <= LANES
            and 2 * per * part <= 2 * LANES
            and 2 * part <= LANES
        )

    def table_z(self):
        table = np.zeros((2, self.pad_k, self.length_z))
        angle = angles_np(np.arange(KZ), np.arange(self.length_z), self.length_z)
        table[0, :KZ] = np.cos(angle)
        table[1, :KZ] = -np.sin(angle)
        return table.reshape(self.pad_z, self.length_z)

    def table_z_group(self):
        return np.kron(np.eye(LANES // self.pad_z), self.table_z())

    def table_y(self):
        kept = kept_np(KY, self.length_y)
        tables = []
        for gy in range(self.count_gy):
            places = gy * self.cells_y + np.arange(self.cells_y)
            angle = angles_np(kept, places, self.length_y)
            for pair in range(2):
                order = []
                for core in range(2):
                    for yy in range(2):
                        for xx in range(2):
                            owner = ((gy >> 1) ^ yy) * 2 + ((gy & 1) ^ core)
                            order.append((owner * 2 + (pair ^ xx)) * self.turns + np.arange(self.turns))
                cos, sin = np.cos(angle)[np.stack(order)], np.sin(angle)[np.stack(order)]
                table = np.zeros((8, 2, self.turns, self.cells_y, 2))
                table[:, 0, :, :, 0] = cos
                table[:, 0, :, :, 1] = sin
                table[:, 1, :, :, 0] = -sin
                table[:, 1, :, :, 1] = cos
                tables.append(table.reshape(16 * self.turns, self.cells_y * 2))
        return np.stack(tables)

    def trig_z(self):
        shape = (self.pad_z, self.length_z)
        row, z = (lax.broadcasted_iota(jnp.int32, shape, n) for n in range(2))
        k, imag = row % self.pad_k, row // self.pad_k
        turn = k * z % self.length_z
        turn = jnp.where(imag == 1, turn + self.length_z // 4, turn) % self.length_z
        value = jnp.cos(turn.astype(F32) * (2.0 * math.pi / self.length_z))
        return jnp.where(k < KZ, value, 0.0)

    def trig_y(self, gx, gy):
        shape = (16 * self.turns, 2 * self.cells_y)
        row, col = (lax.broadcasted_iota(jnp.int32, shape, n) for n in range(2))
        offset = row // (2 * self.turns)
        y_bit = (gy // 2 + offset // 2) % 2
        owner = (y_bit * 2 + (gy + offset // 4) % 2) * 2 + (gx + offset) % 2
        mode = owner * self.turns + row % self.turns
        kept = jnp.where(mode < KY // 2, mode, self.length_y - KY + mode)
        turn = kept * (gy * self.cells_y + col // 2) % self.length_y
        quarter = self.length_y // 4
        out_part, in_part = row // self.turns % 2, col % 2
        shift = jnp.where(out_part == in_part, 0, jnp.where(out_part == 0, 3 * quarter, quarter))
        return jnp.cos(((turn + shift) % self.length_y).astype(F32) * (2.0 * math.pi / self.length_y))

    def table_x(self):
        kept = kept_np(KX, self.length_x)
        tables = []
        for gx in range(self.count_gx):
            outer, pair = gx // 2, gx % 2
            places = np.stack([(gx ^ xx) * self.cells_x + np.arange(self.cells_x) for xx in range(2)]).reshape(-1)
            modes = np.stack([(2 * (outer ^ zz) + (pair ^ h)) * self.per_gx + np.arange(self.per_gx) for zz in range(self.outer) for h in range(2)])
            angle = angles_np(kept[modes.reshape(-1)], places, self.length_x)
            tables.append(np.concatenate([np.cos(angle), np.sin(angle)], axis=1))
        return np.stack(tables)


def tripled_table(table):
    high, low = table_halves(table)
    return np.concatenate([high, high, low], axis=-1)


def forward_kernel(plan, place, feat, keep, send, own_h, own_l, near_x, far_x, field):
    channels, cells_x, cells_y = plan.channels, plan.cells_x, plan.cells_y
    gx, gy = plan.spot(place)
    even_x, even_y = gx % 2 == 0, gy % 2 == 0
    pad = plan.pad_z
    z_table = triple(halves(plan.trig_z()), 1, False)
    ends = []
    for y in range(cells_y):
        plane = [feat[pl.ds(x * cells_y + y, channels, stride=cells_x * cells_y), :] for x in range(cells_x)]
        near_x[y] = jnp.where(even_x, plane[-1], plane[0])
        far_x[y] = jnp.where(even_x, plane[0], plane[-1])
        plane = jnp.concatenate(plane, axis=0)
        if y in (0, cells_y - 1):
            ends.append(plane)
        high, low = halves(plane)
        own_h[y] = high.reshape(cells_x, channels, -1)
        own_l[y] = low.reshape(cells_x, channels, -1)
        field[y * pad : (y + 1) * pad, :] = dot(z_table, triple((high, low), 1, True), NT)
    y_table = triple(halves(plan.trig_y(gx, gy)), 1, False)
    half = 8 * plan.turns
    for k in range(KZ):
        value = halves(field[pl.ds(k, 2 * cells_y, stride=plan.pad_k), :])
        value = dot(y_table, triple(value, 0, True))
        keep[pl.ds(k, half, stride=KZ), :] = value[:half]
        send[pl.ds(k, half, stride=KZ), :] = value[half:]
    start = half * KZ
    send[start : start + LANES, :] = jnp.where(even_y, ends[0], ends[1])
    send[start + LANES :, :] = jnp.where(even_y, ends[1], ends[0])


def forward_modes(plan, place, features):
    half, length_z = 4 * plan.rows, plan.length_z
    own = jax.ShapeDtypeStruct((plan.cells_y, plan.cells_x, plan.channels, length_z), BF16)
    face = jax.ShapeDtypeStruct((plan.cells_y, plan.channels, length_z), F32)
    shape = lambda *s: jax.ShapeDtypeStruct(s, F32)
    return kernel_call(
        functools.partial(forward_kernel, plan),
        [shape(half, LANES), shape(half + 2 * LANES, LANES), own, own, face, face],
        [pltpu.VMEM((plan.cells_y * plan.pad_z, LANES), F32)],
        in_specs=specs(1),
    )(place, features.reshape(-1, length_z))


def turned(value, part, sign):
    lane = lax.broadcasted_iota(jnp.int32, value.shape, 1)
    low = pltpu.roll(value, LANES - part, 1)
    high = pltpu.roll(value, part, 1)
    return jnp.where(lane < part, sign * low, -sign * high)


def square_turned(value):
    return jnp.concatenate([value, jnp.zeros((LANES - value.shape[0], LANES), F32)], axis=0).T


def x_forward_kernel(plan, place, own, from_x, from_y, from_xy, table, *refs):
    outs = refs[: plan.outer]
    straight, crossed, found = refs[plan.outer :]
    rows, channels, per = plan.rows, plan.channels, 2 * plan.per_gx
    near = own[...] + from_y[:rows, :]
    far = from_x[...] + from_xy[...]
    for at, value in enumerate((near, far)):
        value = square_turned(value)
        straight[at * LANES : (at + 1) * LANES, :] = value
        crossed[at * LANES : (at + 1) * LANES, :] = turned(value, plan.part, 1.0)
    factor = table[plan.spot(place)[0]]
    for c in range(channels):
        index = pl.ds(c, 2 * plan.cells_x, stride=channels)
        value = halves(jnp.concatenate([straight[index, :], crossed[index, :]], axis=0))
        found[pl.ds(c, plan.outer * per, stride=channels), :] = dot(factor, triple(value, 0, True))
    for at, out in enumerate(outs):
        size = per * channels
        out[...] = square_turned(found[at * size : (at + 1) * size, :])[:rows]


def x_inverse_kernel(plan, place, *refs):
    parts = refs[: plan.outer]
    table, near, far, straight, crossed, found = refs[plan.outer :]
    rows, channels, per = plan.rows, plan.channels, 2 * plan.per_gx
    size = per * channels
    for at, part in enumerate(parts):
        value = square_turned(part[...])[:size]
        straight[at * size : (at + 1) * size, :] = value
        crossed[at * size : (at + 1) * size, :] = turned(value, plan.part, -1.0)
    factor = table[plan.spot(place)[0]]
    for c in range(channels):
        index = pl.ds(c, plan.outer * per, stride=channels)
        value = halves(jnp.concatenate([straight[index, :], crossed[index, :]], axis=0))
        found[pl.ds(c, 2 * plan.cells_x, stride=channels), :] = dot(factor, triple(value, 0, True))
    for at, out in enumerate((near, far)):
        out[...] = found[at * LANES : (at + 1) * LANES, :].T[:rows]


def x_forward(plan, place, parts):
    part = jax.ShapeDtypeStruct((plan.rows, LANES), F32)
    size = plan.outer * 2 * plan.per_gx * plan.channels
    scratch = [pltpu.VMEM((n, LANES), F32) for n in (2 * LANES, 2 * LANES, size)]
    body = functools.partial(x_forward_kernel, plan)
    table = tripled_table(plan.table_x())
    return kernel_call(body, [part] * plan.outer, scratch, in_specs=specs(5))(place, *parts, table)


def x_inverse(plan, place, parts):
    part = jax.ShapeDtypeStruct((plan.rows, LANES), F32)
    size = plan.outer * 2 * plan.per_gx * plan.channels
    scratch = [pltpu.VMEM((n, LANES), F32) for n in (size, size, 2 * LANES)]
    body = functools.partial(x_inverse_kernel, plan)
    table = plan.table_x()
    half = table.shape[2] // 2
    table = tripled_table(np.concatenate([np.swapaxes(t, 1, 2) for t in (table[:, :, :half], table[:, :, half:])], axis=2))
    return kernel_call(body, [part] * 2, scratch, in_specs=specs(plan.outer + 1))(place, *parts, table)


def weight_kernel(plan, place, weight, keep, send, flat, sem):
    copy = pltpu.make_async_copy(weight.at[:, :, 0, :], flat, sem)
    copy.start()
    copy.wait()
    part, block = plan.part, plan.block
    square = plan.channels * plan.channels
    lane = lax.broadcasted_iota(jnp.int32, (square, LANES), 1)
    width = 2 * LANES
    held = flat.shape[2]
    even = plan.spot(place)[0] % 2 == 0
    for which in range(2):
        high = jnp.concatenate([flat[which, :, LANES:], jnp.zeros((square, width - held), F32)], axis=1)
        value = jnp.concatenate([flat[which, :, :LANES], high], axis=1)
        choice = []
        for half in range(2):
            total = jnp.zeros((square, LANES), F32)
            for j in range(plan.per_gx):
                shift = (j * part - j * block - half * part) % width
                moved = value if shift == 0 else pltpu.roll(value, shift, 1)
                inside = (lane >= j * part) & (lane < (j + 1) * part)
                total = jnp.where(inside, moved[:, :LANES], total)
            choice.append(total)
        at = slice(which * square, (which + 1) * square)
        keep[at, :] = jnp.where(even, choice[0], choice[1])
        send[at, :] = jnp.where(even, choice[1], choice[0])


def weight_parts(plan, place, mix_weight):
    square = plan.channels * plan.channels
    modes = mix_weight.shape[-1]
    out = jax.ShapeDtypeStruct((2 * square, LANES), F32)
    return kernel_call(
        functools.partial(weight_kernel, plan),
        [out, out],
        [pltpu.VMEM((2, square, modes), F32), pltpu.SemaphoreType.DMA],
        in_specs=specs(1),
    )(place, mix_weight.reshape(2, square, 1, modes))


def faces_kernel(plan, place, near_x, far_x, near_y, far_y, after, to_near, to_far):
    channels, cells_x, cells_y = plan.channels, plan.cells_x, plan.cells_y
    even = plan.spot(place)[0] % 2 == 0
    last = cells_x - 1
    for out, face, x in ((to_near, near_x, jnp.where(even, last, 0)), (to_far, far_x, jnp.where(even, 0, last))):
        for y in range(cells_y):
            out[y * channels : (y + 1) * channels, :] = face[y]
        for n, ref in enumerate((near_y, far_y)):
            at = pl.multiple_of(ref.shape[0] - LANES + x * channels, channels)
            start = (cells_y + n) * channels
            out[start : start + channels, :] = ref[pl.ds(at, channels), :]


def faces(plan, place, near_x, far_x, near_y, far_y, after):
    out = jax.ShapeDtypeStruct(((plan.cells_y + 2) * plan.channels, LANES), F32)
    return kernel_call(functools.partial(faces_kernel, plan), [out, out], in_specs=specs(5))(
        place, near_x, far_x, near_y, far_y, after
    )


def mix_kernel(plan, *refs):
    parts = refs[: plan.outer]
    near, far, out = refs[plan.outer :]
    channels, part, per, rows = plan.channels, plan.part, plan.per_gx, plan.rows
    total = parts[0][...]
    for p in parts[1:]:
        total = total + p[...]
    scale = 1.0 / math.sqrt(plan.length_x * plan.length_y * plan.length_z) / math.sqrt(KX * KY * KZ)
    total = jnp.concatenate([total * scale, jnp.zeros((LANES - rows, LANES), F32)], axis=0).T
    lane = lax.broadcasted_iota(jnp.int32, (channels, LANES), 1)

    def moved(value, shift):
        return value if shift % LANES == 0 else pltpu.roll(value, shift % LANES, 1)

    def collect(half, which):
        value = jnp.zeros((channels, LANES), F32)
        for j in range(per):
            at = (half * per + j) * channels
            piece = moved(total[at : at + channels], (j - which) * part)
            value = jnp.where((lane >= j * part) & (lane < (j + 1) * part), piece, value)
        return value

    blocks = []
    for half, weight in enumerate((near, far)):
        c_real, c_imag = collect(half, 0), collect(half, 1)
        real = jnp.zeros((channels, LANES), F32)
        imag = jnp.zeros((channels, LANES), F32)
        for i in range(channels):
            w_real = weight[pl.ds(i, channels, stride=channels), :]
            w_imag = weight[pl.ds(channels * channels + i, channels, stride=channels), :]
            a, b = c_real[i : i + 1], c_imag[i : i + 1]
            real = real + (w_real * a - w_imag * b)
            imag = imag + (w_real * b + w_imag * a)
        for j in range(per):
            low = moved(real, -j * part)
            high = moved(imag, part - j * part)
            blocks.append(jnp.where(lane < part, low, jnp.where(lane < 2 * part, high, 0.0)))
    fill = LANES - 2 * per * channels
    if fill:
        blocks.append(jnp.zeros((fill, LANES), F32))
    out[...] = jnp.concatenate(blocks, axis=0).T[:rows]


def mix_modes(plan, parts, near, far):
    return kernel_call(functools.partial(mix_kernel, plan), jax.ShapeDtypeStruct((plan.rows, LANES), F32))(
        *parts, near, far
    )


def final_kernel(plan, place, own, other, conv_a, conv_b, table_z, table_y, out, field):
    channels, cells_x, cells_y = plan.channels, plan.cells_x, plan.cells_y
    gx, gy = plan.spot(place)
    y_table = table_y[gy * 2 + gx % 2]
    half = 8 * plan.turns
    field[...] = jnp.zeros(field.shape, F32)
    for k in range(KZ):
        parts = [ref[pl.ds(k, half, stride=KZ), :] for ref in (own, other)]
        value = halves(jnp.concatenate(parts, axis=0))
        field[pl.ds(k, 2 * cells_y, stride=plan.pad_k), :] = dot(y_table, triple(value, 0, True))
    z_table = table_z[...]
    group = LANES // plan.pad_z
    for g in range(cells_y // group):
        planes = halves(field[g * LANES : (g + 1) * LANES, :].T)
        value = dot(triple(planes, 1, False), z_table)
        for k in range(group):
            y = g * group + k
            conv = [ref[x, y] for ref in (conv_a, conv_b) for x in range(ref.shape[0])]
            layer = jnp.concatenate(conv, axis=0) + value[:, k * LANES : (k + 1) * LANES]
            layer = layer * 0.5 * (1.0 + lax.erf(layer * math.sqrt(0.5)))
            for x in range(cells_x):
                out[pl.ds(x * cells_y + y, channels, stride=cells_x * cells_y), :] = layer[x * channels : (x + 1) * channels]


def final_layer(plan, place, own, other, convs):
    table_y = tripled_table(np.swapaxes(plan.table_y(), 1, 2))
    high, low = table_halves(plan.table_z_group())
    table_z = np.concatenate([high, low, high], axis=0)
    shape = (plan.channels, plan.cells_x, plan.cells_y, plan.length_z)
    flat = (plan.channels * plan.cells_x * plan.cells_y, plan.length_z)
    return kernel_call(
        functools.partial(final_kernel, plan),
        jax.ShapeDtypeStruct(flat, F32),
        [pltpu.VMEM((plan.cells_y * plan.pad_z, LANES), F32)],
        in_specs=specs(6),
    )(place, own, other, *convs, table_z, table_y).reshape(shape)


def swap(plan, value, outer=0, pair=0, yy=0, core=0):
    perm = []
    for gx in range(plan.count_gx):
        for gy in range(plan.count_gy):
            to_gx = gx ^ (outer * 2 + pair)
            to_gy = gy ^ (yy * 2 + core)
            perm.append((gx * plan.count_gy + gy, to_gx * plan.count_gy + to_gy))
    return lax.ppermute(value, ("gx", "gy"), perm)


def next_pair(value, axis):
    size = lax.axis_size(axis)
    return lax.ppermute(value, axis, [(i, (i + (1 if i % 2 else -1)) % size) for i in range(size)])


def after(value, *others):
    zero = sum(jnp.minimum(jnp.abs(other[:1]), 0.0) for other in others)
    return value + zero


def layer_paired(plan, features, conv_weight, mix_weight):
    rows = plan.rows
    place = (lax.axis_index("gx") * plan.count_gy + lax.axis_index("gy")).astype(jnp.int32).reshape(1)
    cells_x = features.shape[1]

    keep, send, own_h, own_l, near_x, far_x = forward_modes(plan, place, features)
    weight, away = weight_parts(plan, place, mix_weight)
    near_y = swap(plan, send, core=1)
    sums = [keep[s * rows : (s + 1) * rows] + near_y[s * rows : (s + 1) * rows] for s in range(4)]
    passed = near_y[4 * rows : 4 * rows + LANES]
    far_y = swap(plan, jnp.concatenate([sums[2], passed], axis=0), yy=1)
    from_x = swap(plan, sums[1], pair=1)
    from_xy = swap(plan, sums[3], pair=1, yy=1)
    away = after(away, from_x, far_y, from_xy)
    far_weight = swap(plan, away, pair=1)
    chunks = x_forward(plan, place, [sums[0], from_x, far_y, from_xy])
    parts = [chunks[0]] + [swap(plan, chunks[s], outer=s) for s in range(1, plan.outer)]
    mixed = mix_modes(plan, parts, weight, far_weight)
    to_near, to_far = faces(plan, place, near_x, far_x, near_y, far_y, mixed)
    near_x = swap(plan, to_near, pair=1)
    far_x = next_pair(to_far, "gx")
    parts = [mixed] + [swap(plan, mixed, outer=s) for s in range(1, plan.outer)]
    args = (near_x, far_x, near_y, far_y, conv_taps(conv_weight))
    half = cells_x // 2
    mine, theirs = x_inverse(plan, place, parts)
    from_x = swap(plan, theirs, pair=1)
    from_y = swap(plan, mine, yy=1)
    from_xy = swap(plan, theirs, pair=1, yy=1)
    conv_a, token_a = conv_bricks(place, (own_h, own_l), *args, mine, 0, half)
    conv_b, _ = conv_bricks(place, (own_h, own_l), *args, mine, half, cells_x - half)
    own = jnp.concatenate([mine + token_a[:1], from_x, from_y, from_xy], axis=0)
    other = swap(plan, own, core=1)
    return final_layer(plan, place, own, other, (conv_a, conv_b))


def layer_any(features, conv_weight, mix_weight):
    channels, cells_x, cells_y, length_z = features.shape
    own = jax.ShapeDtypeStruct((cells_y, cells_x, channels, length_z), BF16)
    own = kernel_call(split_kernel, [own, own])(features)
    taps = conv_taps(conv_weight)
    conv, _ = conv_bricks(jnp.zeros((1,), jnp.int32), own, *halos(features), taps, taps, 0, cells_x)
    return jax.nn.gelu(conv.transpose(2, 0, 1, 3) + spectral_any(features, mix_weight), approximate=False)


def shards(features, conv_weight, mix_weight):
    counts = lax.axis_size("gx"), lax.axis_size("gy")
    if Plan.fits(features.shape, *counts):
        return layer_paired(Plan(features.shape, *counts), features, conv_weight, mix_weight)
    return layer_any(features, conv_weight, mix_weight)


def solution(mesh):
    in_specs = (P(None, "gx", "gy", None), P(), P(None, None, None, "gy", "gx"))
    out_specs = P(None, "gx", "gy", None)
    return jax.shard_map(shards, mesh=mesh, in_specs=in_specs, out_specs=out_specs, check_vma=False)
```

time: 404 us -> 46.3 us (0.11)
  matrix products: 233 us -> 0 us
  local copies, waits for them, and re-layouts: 74.3 us -> 1.89 us
  blocking collectives: 56.7 us -> 0 us
  between operations: 14.5 us -> 0.18 us
  starting transfers between devices: 7.93 us -> 21 us
  other arithmetic: 12.8 us -> 0.08 us
  waiting for transfers between devices: 3.68 us -> 15 us
  Pallas kernels: 0 us -> 8 us
    conv_general_dilated x1 -> x0, matrix products: 213 us -> none  [shards(): lax.conv_general_dilated(wrapped[None], kernel, (1, 1, 1), 'VALID', dimen...]
    all_gather x2 -> x0, blocking collectives: 56.7 us -> none  [the longest x1 39.8 us: shards(): lax.all_gather(mixed_modes, 'gx', axis=2, tiled=True)]
    conv_general_dilated x5 -> x0, local copies, waits for them, and re-layouts: 42.6 us -> none  [shards(): lax.conv_general_dilated(wrapped[None], kernel, (1, 1, 1), 'VALID', dimen...]
    dot_general x18 -> x0, matrix products: 19.7 us -> none  [the longest x1 4.19 us: shards(): jnp.dot(jnp.concatenate([plane_real, plane_imag], axis=3), table_back, pr...]
    ppermute x4 -> x17, starting transfers between devices: 7.89 us -> 21 us  [the longest x16 20.5 us: swap(): return lax.ppermute(value, ('gx', 'gy'), perm)]
    unnamed x30 -> x15, local copies, waits for them, and re-layouts: 14.6 us -> 1.6 us
    ppermute x4 -> x17, waiting for transfers between devices: 3.64 us -> 15 us  [the longest x16 15 us: swap(): return lax.ppermute(value, ('gx', 'gy'), perm)]
    conv_general_dilated x1 -> x0, other arithmetic: 9.53 us -> none  [shards(): lax.conv_general_dilated(wrapped[None], kernel, (1, 1, 1), 'VALID', dimen...]
  transfers between devices with their start and end apart: 6 -> 17, of which waited for: 3 -> 10; matrix products, arithmetic and copies ran while one was open for 67% -> 1% of each run, Pallas kernels for 0% -> 9%
where the time goes in v2:
time: 46.3 us; the launch traced here: 46.1 us
  starting transfers between devices  21 us (45%)
  waiting for transfers between devices  15 us (32%)
  Pallas kernels  8 us (17%)
  local copies, waits for them, and re-layouts  1.89 us (4%)
    ppermute x16, starting transfers between devices, swap(): return lax.ppermute(value, ('gx', 'gy'), perm)  20.5 us
    ppermute x16, waiting for transfers between devices, swap(): return lax.ppermute(value, ('gx', 'gy'), perm)  15 us
    pallas_call x1, Pallas kernels, final_layer(): kernel_call(functools.partial(final_kernel, plan), jax.ShapeDtypeStruct(f...  2.26 us
    pallas_call x2, Pallas kernels, conv_bricks(): kernel_call(functools.partial(conv_kernel, first, 2, lax.axis_size('gy'))...  2.17 us
    unnamed x15, local copies, waits for them, and re-layouts  1.6 us
    pallas_call x1, Pallas kernels, forward_modes(): kernel_call(functools.partial(forward_kernel, plan), [shape(half, LANES),...  1.17 us
  transfers between devices with their start and end apart: 17, of which 10 were waited for; matrix products, arithmetic and copies ran while one was open for 1% of the time, Pallas kernels for 9%

profile of v2, /device:TPU:0, one launch (start us, length us, event | category | flops | bytes accessed | tf_op | source)
XLA Modules:
  0.0 46.1 jit_solution(4945278357745399206)
XLA Ops:
  0.0 1.2 %copy-done = f32[16,8,16,128]{3,2,1,0:T(8,128)S(1)} copy-done((f32[16,8,16,128]{3,2,1,0:T(8,128)S(1)}, f32[16,8,16,128]{3,2,1,0:T(8,128)}, u32[]{:S(2)}) %copy-start) | copy-done | bytes 1048600
  1.2 1.2 %shard_map.73 = (f32[288,128]{1,0:T(8,128)S(1)}, f32[544,128]{1,0:T(8,128)S(1)}, bf16[16,8,16,128]{3,2,1,0:T(8,128)(2,1)S(1)}, bf16[16,8,16,128]{3,2,1,0:T(8,128...) custom-call(s32[1]{0:T(128)} %bitcast.place, f32[2048,128]{1,0:T(8,128)S(1)} %bitcast.11), custom_call_target="tpu_custom_call" | custom-call | tf_op jit(solution)/shard_map/pallas_call | solution.py:395
  2.4 0.5 %collective-permute-start = (f32[544,128]{1,0:T(8,128)S(1)}, f32[544,128]{1,0:T(8,128)S(1)}, u32[]{:S(2)}, u32[]{:S(2)}) collective-permute-start(f32[544,128]{1,0:T(8,128)S(1)} %get-tuple-element.25), channel_id=1, source_target_pairs={{0,1},{1,0},{2,3},{3,2},{4,5},{5,4},{6,7},{7,6},{8,9},{9,8},{10,11... | collective-permute-start | bytes 835592 | tf_op jit(solution)/shard_map/ppermute | solution.py:625
  2.9 1.2 %collective-permute-done.near_y = f32[544,128]{1,0:T(8,128)S(1)} collective-permute-done((f32[544,128]{1,0:T(8,128)S(1)}, f32[544,128]{1,0:T(8,128)S(1)}, u32[]{:S(2)}, u32[]{:S(2)}) %collective-permute-start) | collective-permute-done | bytes 278560 | tf_op jit(solution)/shard_map/ppermute | solution.py:625
  4.2 3.0 %collective-permute-start.2 = (f32[200,128]{1,0:T(8,128)S(1)}, f32[200,128]{1,0:T(8,128)S(1)}, u32[]{:S(2)}, u32[]{:S(2)}) collective-permute-start(f32[200,128]{1,0:T(8,128)S(1)} %pad_maximum_fusion.1), channel_id=1, source_target_pairs={{0,2},{1,3},{2,0},{3,1},{4,6},{5,7},{6,4},{7,5},{8,10},{9,11},{10,... | collective-permute-start | bytes 307208 | tf_op jit(solution)/shard_map/ppermute | solution.py:625
  7.1 1.5 %collective-permute-start.1 = (f32[72,128]{1,0:T(8,128)S(1)}, f32[72,128]{1,0:T(8,128)S(1)}, u32[]{:S(2)}, u32[]{:S(2)}) collective-permute-start(f32[72,128]{1,0:T(8,128)S(1)} %get-tuple-element.45), channel_id=1, source_target_pairs={{0,4},{1,5},{2,6},{3,7},{4,0},{5,1},{6,2},{7,3},{8,12},{9,13},{10,... | collective-permute-start | bytes 110600 | tf_op jit(solution)/shard_map/ppermute | solution.py:625
  8.7 0.8 %shard_map.75 = (f32[512,128]{1,0:T(8,128)S(1)}, f32[512,128]{1,0:T(8,128)S(1)}) custom-call(s32[1]{0:T(128)} %bitcast.place, f32[2,256,1,216]{3,2,1,0:T(1,128)S(1)} %bitcast.12), custom_call_target="tpu_custom_call" | custom-call | tf_op jit(solution)/shard_map/pallas_call | solution.py:503
  9.5 1.9 %collective-permute-done.1.from_x = f32[72,128]{1,0:T(8,128)S(1)} collective-permute-done((f32[72,128]{1,0:T(8,128)S(1)}, f32[72,128]{1,0:T(8,128)S(1)}, u32[]{:S(2)}, u32[]{:S(2)}) %collective-permute-start.1) | collective-permute-done | bytes 36896 | tf_op jit(solution)/shard_map/ppermute | solution.py:625
  11.4 2.0 %collective-permute-done.3.from_xy = f32[72,128]{1,0:T(8,128)S(1)} collective-permute-done((f32[72,128]{1,0:T(8,128)S(1)}, f32[72,128]{1,0:T(8,128)S(1)}, u32[]{:S(2)}, u32[]{:S(2)}) %collective-permute-start.3) | collective-permute-done | bytes 36896 | tf_op jit(solution)/shard_map/ppermute | solution.py:625
  13.5 0.6 %collective-permute-start.7 = (f32[512,128]{1,0:T(8,128)S(1)}, f32[512,128]{1,0:T(8,128)S(1)}, u32[]{:S(2)}, u32[]{:S(2)}) collective-permute-start(f32[512,128]{1,0:T(8,128)S(1)} %broadcast_add_fusion), channel_id=1, source_target_pairs={{0,4},{1,5},{2,6},{3,7},{4,0},{5,1},{6,2},{7,3},{8,12},{9,13},{10,... | collective-permute-start | bytes 786440 | tf_op jit(solution)/shard_map/ppermute | solution.py:625
  14.3 0.5 %shard_map.74 = (f32[72,128]{1,0:T(8,128)S(1)}, f32[72,128]{1,0:T(8,128)S(1)}, f32[72,128]{1,0:T(8,128)S(1)}, f32[72,128]{1,0:T(8,128)S(1)}) custom-call(s32[1]{0:T(128)} %bitcast.place, f32[72,128]{1,0:T(8,128)S(1)} %get-tuple-element.46.own, f32[72,128]{1,0:T(8,128)S(1)} %collective-permute-done.1.from_x, ...), custom_call_target="tpu_custom_call" | custom-call | tf_op jit(solution)/shard_map/pallas_call | solution.py:458
  14.8 1.6 %collective-permute-start.4 = (f32[72,128]{1,0:T(8,128)S(1)}, f32[72,128]{1,0:T(8,128)S(1)}, u32[]{:S(2)}, u32[]{:S(2)}) collective-permute-start(f32[72,128]{1,0:T(8,128)S(1)} %get-tuple-element.27), channel_id=1, source_target_pairs={{0,8},{1,9},{2,10},{3,11},{4,12},{5,13},{6,14},{7,15},{8,0},{9,1},... | collective-permute-start | bytes 110600 | tf_op jit(solution)/shard_map/ppermute | solution.py:625
  16.5 2.6 %collective-permute-start.5 = (f32[72,128]{1,0:T(8,128)S(1)}, f32[72,128]{1,0:T(8,128)S(1)}, u32[]{:S(2)}, u32[]{:S(2)}) collective-permute-start(f32[72,128]{1,0:T(8,128)S(1)} %get-tuple-element.28), channel_id=1, source_target_pairs={{0,16},{1,17},{2,18},{3,19},{4,20},{5,21},{6,22},{7,23},{8,24},{9,... | collective-permute-start | bytes 110600 | tf_op jit(solution)/shard_map/ppermute | solution.py:625
  19.0 0.2 collective-permute-start.6
  19.3 2.8 %collective-permute-done.5.refs_2_ = f32[72,128]{1,0:T(8,128)S(1)} collective-permute-done((f32[72,128]{1,0:T(8,128)S(1)}, f32[72,128]{1,0:T(8,128)S(1)}, u32[]{:S(2)}, u32[]{:S(2)}) %collective-permute-start.5) | collective-permute-done | bytes 36896 | tf_op jit(solution)/shard_map/ppermute | solution.py:625
  22.0 2.9 %collective-permute-done.6.refs_3_ = f32[72,128]{1,0:T(8,128)S(1)} collective-permute-done((f32[72,128]{1,0:T(8,128)S(1)}, f32[72,128]{1,0:T(8,128)S(1)}, u32[]{:S(2)}, u32[]{:S(2)}) %collective-permute-start.6) | collective-permute-done | bytes 36896 | tf_op jit(solution)/shard_map/ppermute | solution.py:625
  24.9 0.4 shard_map.76.refs_0_.after
  25.4 1.3 %collective-permute-start.11 = (f32[288,128]{1,0:T(8,128)S(1)}, f32[288,128]{1,0:T(8,128)S(1)}, u32[]{:S(2)}, u32[]{:S(2)}) collective-permute-start(f32[288,128]{1,0:T(8,128)S(1)} %get-tuple-element.37), channel_id=1, source_target_pairs={{0,4},{1,5},{2,6},{3,7},{4,0},{5,1},{6,2},{7,3},{8,12},{9,13},{10,... | collective-permute-start | bytes 442376 | tf_op jit(solution)/shard_map/ppermute | solution.py:625
  26.7 0.5 %collective-permute-start.12 = (f32[288,128]{1,0:T(8,128)S(1)}, f32[288,128]{1,0:T(8,128)S(1)}, u32[]{:S(2)}, u32[]{:S(2)}) collective-permute-start(f32[288,128]{1,0:T(8,128)S(1)} %get-tuple-element.38), channel_id=1, source_target_pairs={{0,28},{4,8},{8,4},{12,16},{16,12},{20,24},{24,20},{28,0},{1,29},{... | collective-permute-start | bytes 442376 | tf_op jit(solution)/shard_map/ppermute | solution.py:630
  27.4 1.6 %collective-permute-start.8 = (f32[72,128]{1,0:T(8,128)S(1)}, f32[72,128]{1,0:T(8,128)S(1)}, u32[]{:S(2)}, u32[]{:S(2)}) collective-permute-start(f32[72,128]{1,0:T(8,128)S(1)} %shard_map.76.refs_0_.after), channel_id=1, source_target_pairs={{0,8},{1,9},{2,10},{3,11},{4,12},{5,13},{6,14},{7,15},{8,0},{9,1},... | collective-permute-start | bytes 110600 | tf_op jit(solution)/shard_map/ppermute | solution.py:625
  28.9 2.7 %collective-permute-start.9 = (f32[72,128]{1,0:T(8,128)S(1)}, f32[72,128]{1,0:T(8,128)S(1)}, u32[]{:S(2)}, u32[]{:S(2)}) collective-permute-start(f32[72,128]{1,0:T(8,128)S(1)} %shard_map.76.refs_0_.after), channel_id=1, source_target_pairs={{0,16},{1,17},{2,18},{3,19},{4,20},{5,21},{6,22},{7,23},{8,24},{9,... | collective-permute-start | bytes 110600 | tf_op jit(solution)/shard_map/ppermute | solution.py:625
  32.1 0.9 %collective-permute-done.10.refs_3_ = f32[72,128]{1,0:T(8,128)S(1)} collective-permute-done((f32[72,128]{1,0:T(8,128)S(1)}, f32[72,128]{1,0:T(8,128)S(1)}, u32[]{:S(2)}, u32[]{:S(2)}) %collective-permute-start.10) | collective-permute-done | bytes 36896 | tf_op jit(solution)/shard_map/ppermute | solution.py:625
  33.0 0.8 %collective-permute-done.9.refs_2_ = f32[72,128]{1,0:T(8,128)S(1)} collective-permute-done((f32[72,128]{1,0:T(8,128)S(1)}, f32[72,128]{1,0:T(8,128)S(1)}, u32[]{:S(2)}, u32[]{:S(2)}) %collective-permute-start.9) | collective-permute-done | bytes 36896 | tf_op jit(solution)/shard_map/ppermute | solution.py:625
  33.8 0.6 %shard_map.77 = (f32[72,128]{1,0:T(8,128)S(1)}, f32[72,128]{1,0:T(8,128)S(1)}) custom-call(s32[1]{0:T(128)} %bitcast.place, f32[72,128]{1,0:T(8,128)S(1)} %shard_map.76.refs_0_.after, f32[72,128]{1,0:T(8,128)S(1)} %collective-permute-done.8.refs_1_, f32[72,128]{1,0:T(8,128)S(1)} %collective-permute-done.9.refs_2_, ...), custom_call_target="tpu_custom_call" | custom-call | tf_op jit(solution)/shard_map/pallas_call | solution.py:469
  34.4 3.1 %collective-permute-start.13 = (f32[72,128]{1,0:T(8,128)S(1)}, f32[72,128]{1,0:T(8,128)S(1)}, u32[]{:S(2)}, u32[]{:S(2)}) collective-permute-start(f32[72,128]{1,0:T(8,128)S(1)} %get-tuple-element.40), channel_id=1, source_target_pairs={{0,4},{1,5},{2,6},{3,7},{4,0},{5,1},{6,2},{7,3},{8,12},{9,13},{10,... | collective-permute-start | bytes 110600 | tf_op jit(solution)/shard_map/ppermute | solution.py:625
  37.5 1.5 %collective-permute-start.14 = (f32[72,128]{1,0:T(8,128)S(1)}, f32[72,128]{1,0:T(8,128)S(1)}, u32[]{:S(2)}, u32[]{:S(2)}) collective-permute-start(f32[72,128]{1,0:T(8,128)S(1)} %get-tuple-element.32.after), channel_id=1, source_target_pairs={{0,2},{1,3},{2,0},{3,1},{4,6},{5,7},{6,4},{7,5},{8,10},{9,11},{10,... | collective-permute-start | bytes 110600 | tf_op jit(solution)/shard_map/ppermute | solution.py:625
  39.0 1.1 %shard_map.79 = (f32[4,16,16,128]{3,2,1,0:T(8,128)S(1)}, f32[8,128]{1,0:T(8,128)S(1)}) custom-call(s32[1]{0:T(128)} %bitcast.place, bf16[16,8,16,128]{3,2,1,0:T(8,128)(2,1)S(1)} %get-tuple-element.33.own_h, bf16[16,8,16,128]{3,2,1,0:T(8,128)(2,1)S(1)} %get-tuple-element.34.own_l, f32[288,128]{1,0:T(8,128)S(1)} %collective-permute-done.11.near_x, ...), custom_call_target="tpu_custom_call" | custom-call | tf_op jit(solution)/shard_map/pallas_call | solution.py:160
  40.2 1.3 %collective-permute-done.14 = f32[72,128]{1,0:T(8,128)S(1)} collective-permute-done((f32[72,128]{1,0:T(8,128)S(1)}, f32[72,128]{1,0:T(8,128)S(1)}, u32[]{:S(2)}, u32[]{:S(2)}) %collective-permute-start.14) | collective-permute-done | bytes 36896 | tf_op jit(solution)/shard_map/ppermute | solution.py:625
  41.5 0.9 %collective-permute-done.15 = f32[72,128]{1,0:T(8,128)S(1)} collective-permute-done((f32[72,128]{1,0:T(8,128)S(1)}, f32[72,128]{1,0:T(8,128)S(1)}, u32[]{:S(2)}, u32[]{:S(2)}) %collective-permute-start.15) | collective-permute-done | bytes 36896 | tf_op jit(solution)/shard_map/ppermute | solution.py:625
  42.5 1.1 %shard_map.80 = (f32[4,16,16,128]{3,2,1,0:T(8,128)S(1)}, f32[8,128]{1,0:T(8,128)}) custom-call(s32[1]{0:T(128)} %bitcast.place, bf16[16,8,16,128]{3,2,1,0:T(8,128)(2,1)S(1)} %get-tuple-element.33.own_h, bf16[16,8,16,128]{3,2,1,0:T(8,128)(2,1)S(1)} %get-tuple-element.34.own_l, f32[288,128]{1,0:T(8,128)S(1)} %collective-permute-done.11.near_x, ...), custom_call_target="tpu_custom_call" | custom-call | tf_op jit(solution)/shard_map/pallas_call | solution.py:160
  43.6 0.3 collective-permute-done.16.other
  43.8 2.3 %shard_map.81 = f32[2048,128]{1,0:T(8,128)} custom-call(s32[1]{0:T(128)} %bitcast.place, f32[288,128]{1,0:T(8,128)S(1)} %pad_maximum_fusion.own, f32[288,128]{1,0:T(8,128)S(1)} %collective-permute-done.16.other, f32[4,16,16,128]{3,2,1,0:T(8,128)S(1)} %get-tuple-element.41.conv_a, f32[4,16,16,128]{3,2,1,0:T(8,128)S(1)} %get-tuple-element.42.conv_b, ...), custom_call_target="tpu_custom_call" | custom-call | tf_op jit(solution)/shard_map/pallas_call | solution.py:610
  (36 shorter events, 1.1 us)
Async XLA Ops:
  0.0 1.2 %copy-start = (f32[16,8,16,128]{3,2,1,0:T(8,128)S(1)}, f32[16,8,16,128]{3,2,1,0:T(8,128)}, u32[]{:S(2)}) copy-start(f32[16,8,16,128]{3,2,1,0:T(8,128)} %param.7) | copy-start | bytes 3145732
  2.4 6.3 %copy-start.1 = (f32[2,16,16,1,216]{4,3,2,1,0:T(1,128)S(1)}, f32[2,16,16,1,216]{4,3,2,1,0:T(1,128)}, u32[]{:S(2)}) copy-start(f32[2,16,16,1,216]{4,3,2,1,0:T(1,128)} %param.9) | copy-start | bytes 1327108
  2.4 1.7 %collective-permute-start = (f32[544,128]{1,0:T(8,128)S(1)}, f32[544,128]{1,0:T(8,128)S(1)}, u32[]{:S(2)}, u32[]{:S(2)}) collective-permute-start(f32[544,128]{1,0:T(8,128)S(1)} %get-tuple-element.25), channel_id=1, source_target_pairs={{0,1},{1,0},{2,3},{3,2},{4,5},{5,4},{6,7},{7,6},{8,9},{9,8},{10,11... | collective-permute-start | bytes 835592 | tf_op jit(solution)/shard_map/ppermute | solution.py:625
  4.2 9.3 %collective-permute-start.2 = (f32[200,128]{1,0:T(8,128)S(1)}, f32[200,128]{1,0:T(8,128)S(1)}, u32[]{:S(2)}, u32[]{:S(2)}) collective-permute-start(f32[200,128]{1,0:T(8,128)S(1)} %pad_maximum_fusion.1), channel_id=1, source_target_pairs={{0,2},{1,3},{2,0},{3,1},{4,6},{5,7},{6,4},{7,5},{8,10},{9,11},{10,... | collective-permute-start | bytes 307208 | tf_op jit(solution)/shard_map/ppermute | solution.py:625
  7.1 4.3 %collective-permute-start.1 = (f32[72,128]{1,0:T(8,128)S(1)}, f32[72,128]{1,0:T(8,128)S(1)}, u32[]{:S(2)}, u32[]{:S(2)}) collective-permute-start(f32[72,128]{1,0:T(8,128)S(1)} %get-tuple-element.45), channel_id=1, source_target_pairs={{0,4},{1,5},{2,6},{3,7},{4,0},{5,1},{6,2},{7,3},{8,12},{9,13},{10,... | collective-permute-start | bytes 110600 | tf_op jit(solution)/shard_map/ppermute | solution.py:625
  8.6 4.9 %collective-permute-start.3 = (f32[72,128]{1,0:T(8,128)S(1)}, f32[72,128]{1,0:T(8,128)S(1)}, u32[]{:S(2)}, u32[]{:S(2)}) collective-permute-start(f32[72,128]{1,0:T(8,128)S(1)} %get-tuple-element.43), channel_id=1, source_target_pairs={{0,6},{1,7},{2,4},{3,5},{4,2},{5,3},{6,0},{7,1},{8,14},{9,15},{10,... | collective-permute-start | bytes 110600 | tf_op jit(solution)/shard_map/ppermute | solution.py:625
  13.5 0.8 %copy-start.5 = (bf16[8,24,96]{2,1,0:T(8,128)(2,1)S(1)}, bf16[8,24,96]{2,1,0:T(8,128)(2,1)}, u32[]{:S(2)}) copy-start(bf16[8,24,96]{2,1,0:T(8,128)(2,1)} %constant.21.clone.table) | copy-start | bytes 110596
  13.5 11.4 %collective-permute-start.7 = (f32[512,128]{1,0:T(8,128)S(1)}, f32[512,128]{1,0:T(8,128)S(1)}, u32[]{:S(2)}, u32[]{:S(2)}) collective-permute-start(f32[512,128]{1,0:T(8,128)S(1)} %broadcast_add_fusion), channel_id=1, source_target_pairs={{0,4},{1,5},{2,6},{3,7},{4,0},{5,1},{6,2},{7,3},{8,12},{9,13},{10,... | collective-permute-start | bytes 786440 | tf_op jit(solution)/shard_map/ppermute | solution.py:625
  14.8 4.5 %collective-permute-start.4 = (f32[72,128]{1,0:T(8,128)S(1)}, f32[72,128]{1,0:T(8,128)S(1)}, u32[]{:S(2)}, u32[]{:S(2)}) collective-permute-start(f32[72,128]{1,0:T(8,128)S(1)} %get-tuple-element.27), channel_id=1, source_target_pairs={{0,8},{1,9},{2,10},{3,11},{4,12},{5,13},{6,14},{7,15},{8,0},{9,1},... | collective-permute-start | bytes 110600 | tf_op jit(solution)/shard_map/ppermute | solution.py:625
  16.5 5.6 %collective-permute-start.5 = (f32[72,128]{1,0:T(8,128)S(1)}, f32[72,128]{1,0:T(8,128)S(1)}, u32[]{:S(2)}, u32[]{:S(2)}) collective-permute-start(f32[72,128]{1,0:T(8,128)S(1)} %get-tuple-element.28), channel_id=1, source_target_pairs={{0,16},{1,17},{2,18},{3,19},{4,20},{5,21},{6,22},{7,23},{8,24},{9,... | collective-permute-start | bytes 110600 | tf_op jit(solution)/shard_map/ppermute | solution.py:625
  19.0 5.9 %collective-permute-start.6 = (f32[72,128]{1,0:T(8,128)S(1)}, f32[72,128]{1,0:T(8,128)S(1)}, u32[]{:S(2)}, u32[]{:S(2)}) collective-permute-start(f32[72,128]{1,0:T(8,128)S(1)} %get-tuple-element.29), channel_id=1, source_target_pairs={{0,24},{1,25},{2,26},{3,27},{4,28},{5,29},{6,30},{7,31},{8,16},{9,... | collective-permute-start | bytes 110600 | tf_op jit(solution)/shard_map/ppermute | solution.py:625
  25.3 6.3 %copy-start.6 = (f32[27,16,16]{0,2,1:T(8,128)S(1)}, f32[27,16,16]{0,2,1:T(8,128)}, u32[]{:S(2)}) copy-start(f32[27,16,16]{0,2,1:T(8,128)} %param.8) | copy-start | bytes 82948
  25.4 13.7 %collective-permute-start.11 = (f32[288,128]{1,0:T(8,128)S(1)}, f32[288,128]{1,0:T(8,128)S(1)}, u32[]{:S(2)}, u32[]{:S(2)}) collective-permute-start(f32[288,128]{1,0:T(8,128)S(1)} %get-tuple-element.37), channel_id=1, source_target_pairs={{0,4},{1,5},{2,6},{3,7},{4,0},{5,1},{6,2},{7,3},{8,12},{9,13},{10,... | collective-permute-start | bytes 442376 | tf_op jit(solution)/shard_map/ppermute | solution.py:625
  26.7 12.4 %collective-permute-start.12 = (f32[288,128]{1,0:T(8,128)S(1)}, f32[288,128]{1,0:T(8,128)S(1)}, u32[]{:S(2)}, u32[]{:S(2)}) collective-permute-start(f32[288,128]{1,0:T(8,128)S(1)} %get-tuple-element.38), channel_id=1, source_target_pairs={{0,28},{4,8},{8,4},{12,16},{16,12},{20,24},{24,20},{28,0},{1,29},{... | collective-permute-start | bytes 442376 | tf_op jit(solution)/shard_map/ppermute | solution.py:630
  27.2 5.8 %collective-permute-start.10 = (f32[72,128]{1,0:T(8,128)S(1)}, f32[72,128]{1,0:T(8,128)S(1)}, u32[]{:S(2)}, u32[]{:S(2)}) collective-permute-start(f32[72,128]{1,0:T(8,128)S(1)} %shard_map.76.refs_0_.after), channel_id=1, source_target_pairs={{0,24},{1,25},{2,26},{3,27},{4,28},{5,29},{6,30},{7,31},{8,16},{9,... | collective-permute-start | bytes 110600 | tf_op jit(solution)/shard_map/ppermute | solution.py:625
  27.4 5.6 %collective-permute-start.8 = (f32[72,128]{1,0:T(8,128)S(1)}, f32[72,128]{1,0:T(8,128)S(1)}, u32[]{:S(2)}, u32[]{:S(2)}) collective-permute-start(f32[72,128]{1,0:T(8,128)S(1)} %shard_map.76.refs_0_.after), channel_id=1, source_target_pairs={{0,8},{1,9},{2,10},{3,11},{4,12},{5,13},{6,14},{7,15},{8,0},{9,1},... | collective-permute-start | bytes 110600 | tf_op jit(solution)/shard_map/ppermute | solution.py:625
  28.9 4.9 %collective-permute-start.9 = (f32[72,128]{1,0:T(8,128)S(1)}, f32[72,128]{1,0:T(8,128)S(1)}, u32[]{:S(2)}, u32[]{:S(2)}) collective-permute-start(f32[72,128]{1,0:T(8,128)S(1)} %shard_map.76.refs_0_.after), channel_id=1, source_target_pairs={{0,16},{1,17},{2,18},{3,19},{4,20},{5,21},{6,22},{7,23},{8,24},{9,... | collective-permute-start | bytes 110600 | tf_op jit(solution)/shard_map/ppermute | solution.py:625
  31.9 1.9 %copy-start.4 = (bf16[8,16,144]{2,1,0:T(8,128)(2,1)S(1)}, bf16[8,16,144]{2,1,0:T(8,128)(2,1)}, u32[]{:S(2)}) copy-start(bf16[8,16,144]{2,1,0:T(8,128)(2,1)} %constant.22.clone.refs_4_) | copy-start | bytes 110596
  34.4 5.8 %collective-permute-start.13 = (f32[72,128]{1,0:T(8,128)S(1)}, f32[72,128]{1,0:T(8,128)S(1)}, u32[]{:S(2)}, u32[]{:S(2)}) collective-permute-start(f32[72,128]{1,0:T(8,128)S(1)} %get-tuple-element.40), channel_id=1, source_target_pairs={{0,4},{1,5},{2,6},{3,7},{4,0},{5,1},{6,2},{7,3},{8,12},{9,13},{10,... | collective-permute-start | bytes 110600 | tf_op jit(solution)/shard_map/ppermute | solution.py:625
  37.5 4.9 %collective-permute-start.15 = (f32[72,128]{1,0:T(8,128)S(1)}, f32[72,128]{1,0:T(8,128)S(1)}, u32[]{:S(2)}, u32[]{:S(2)}) collective-permute-start(f32[72,128]{1,0:T(8,128)S(1)} %get-tuple-element.40), channel_id=1, source_target_pairs={{0,6},{1,7},{2,4},{3,5},{4,2},{5,3},{6,0},{7,1},{8,14},{9,15},{10,... | collective-permute-start | bytes 110600 | tf_op jit(solution)/shard_map/ppermute | solution.py:625
  37.5 4.0 %collective-permute-start.14 = (f32[72,128]{1,0:T(8,128)S(1)}, f32[72,128]{1,0:T(8,128)S(1)}, u32[]{:S(2)}, u32[]{:S(2)}) collective-permute-start(f32[72,128]{1,0:T(8,128)S(1)} %get-tuple-element.32.after), channel_id=1, source_target_pairs={{0,2},{1,3},{2,0},{3,1},{4,6},{5,7},{6,4},{7,5},{8,10},{9,11},{10,... | collective-permute-start | bytes 110600 | tf_op jit(solution)/shard_map/ppermute | solution.py:625
  42.4 1.5 %copy-start.2 = (bf16[384,512]{1,0:T(8,128)(2,1)S(1)}, bf16[384,512]{1,0:T(8,128)(2,1)}, u32[]{:S(2)}) copy-start(bf16[384,512]{1,0:T(8,128)(2,1)} %constant.23.clone.table_z) | copy-start | bytes 1179652
  42.4 1.5 %copy-start.3 = (bf16[8,32,144]{2,1,0:T(8,128)(2,1)S(1)}, bf16[8,32,144]{2,1,0:T(8,128)(2,1)}, u32[]{:S(2)}) copy-start(bf16[8,32,144]{2,1,0:T(8,128)(2,1)} %constant.24.clone.table_y) | copy-start | bytes 221188
  42.4 1.4 %collective-permute-start.16 = (f32[288,128]{1,0:T(8,128)S(1)}, f32[288,128]{1,0:T(8,128)S(1)}, u32[]{:S(2)}, u32[]{:S(2)}) collective-permute-start(f32[288,128]{1,0:T(8,128)S(1)} %pad_maximum_fusion.own), channel_id=1, source_target_pairs={{0,1},{1,0},{2,3},{3,2},{4,5},{5,4},{6,7},{7,6},{8,9},{9,8},{10,11... | collective-permute-start | bytes 442376 | tf_op jit(solution)/shard_map/ppermute | solution.py:625

commit v3 on v2

--- a/solution.py
+++ b/solution.py
@@ -295,28 +295,6 @@
     def table_z_group(self):
         return np.kron(np.eye(LANES // self.pad_z), self.table_z())
 
-    def table_y(self):
-        kept = kept_np(KY, self.length_y)
-        tables = []
-        for gy in range(self.count_gy):
-            places = gy * self.cells_y + np.arange(self.cells_y)
-            angle = angles_np(kept, places, self.length_y)
-            for pair in range(2):
-                order = []
-                for core in range(2):
-                    for yy in range(2):
-                        for xx in range(2):
-                            owner = ((gy >> 1) ^ yy) * 2 + ((gy & 1) ^ core)
-                            order.append((owner * 2 + (pair ^ xx)) * self.turns + np.arange(self.turns))
-                cos, sin = np.cos(angle)[np.stack(order)], np.sin(angle)[np.stack(order)]
-                table = np.zeros((8, 2, self.turns, self.cells_y, 2))
-                table[:, 0, :, :, 0] = cos
-                table[:, 0, :, :, 1] = sin
-                table[:, 1, :, :, 0] = -sin
-                table[:, 1, :, :, 1] = cos
-                tables.append(table.reshape(16 * self.turns, self.cells_y * 2))
-        return np.stack(tables)
-
     def trig_z(self):
         shape = (self.pad_z, self.length_z)
         row, z = (lax.broadcasted_iota(jnp.int32, shape, n) for n in range(2))
@@ -326,12 +304,15 @@
         value = jnp.cos(turn.astype(F32) * (2.0 * math.pi / self.length_z))
         return jnp.where(k < KZ, value, 0.0)
 
-    def trig_y(self, gx, gy):
+    def half_of(self, gx, gy):
+        return (gy + gy // 2 + gx // 2 + gx) % 2
+
+    def trig_y(self, gx, gy, turned):
         shape = (16 * self.turns, 2 * self.cells_y)
-        row, col = (lax.broadcasted_iota(jnp.int32, shape, n) for n in range(2))
+        row, col = (lax.broadcasted_iota(jnp.int32, shape[::-1] if turned else shape, n ^ int(turned)) for n in range(2))
         offset = row // (2 * self.turns)
         y_bit = (gy // 2 + offset // 2) % 2
-        owner = (y_bit * 2 + (gy + offset // 4) % 2) * 2 + (gx + offset) % 2
+        owner = (y_bit * 2 + (self.half_of(gx, gy) + offset // 4) % 2) * 2 + (gx + offset) % 2
         mode = owner * self.turns + row % self.turns
         kept = jnp.where(mode < KY // 2, mode, self.length_y - KY + mode)
         turn = kept * (gy * self.cells_y + col // 2) % self.length_y
@@ -340,16 +321,25 @@
         shift = jnp.where(out_part == in_part, 0, jnp.where(out_part == 0, 3 * quarter, quarter))
         return jnp.cos(((turn + shift) % self.length_y).astype(F32) * (2.0 * math.pi / self.length_y))
 
-    def table_x(self):
-        kept = kept_np(KX, self.length_x)
-        tables = []
-        for gx in range(self.count_gx):
-            outer, pair = gx // 2, gx % 2
-            places = np.stack([(gx ^ xx) * self.cells_x + np.arange(self.cells_x) for xx in range(2)]).reshape(-1)
-            modes = np.stack([(2 * (outer ^ zz) + (pair ^ h)) * self.per_gx + np.arange(self.per_gx) for zz in range(self.outer) for h in range(2)])
-            angle = angles_np(kept[modes.reshape(-1)], places, self.length_x)
-            tables.append(np.concatenate([np.cos(angle), np.sin(angle)], axis=1))
-        return np.stack(tables)
+    def trig_x(self, gx, inverse):
+        modes, places = self.outer * 2 * self.per_gx, 2 * self.cells_x
+        shape = (places, 2 * modes) if inverse else (modes, 2 * places)
+        row, col = (lax.broadcasted_iota(jnp.int32, shape, n) for n in range(2))
+        width = modes if inverse else places
+        crossed = col // width
+        mode, at = (col % width, row) if inverse else (row, col % width)
+        outer, pair = gx // 2, gx % 2
+        offset, inner = mode // (2 * self.per_gx), mode % (2 * self.per_gx)
+        other = jnp.zeros_like(offset)
+        for s in range(self.outer):
+            other = jnp.where(offset == s, outer ^ s, other)
+        index = (2 * other + (pair + inner // self.per_gx) % 2) * self.per_gx + inner % self.per_gx
+        kept = jnp.where(index < KX // 2, index, self.length_x - KX + index)
+        far = (2 * outer + 1 - pair) * self.cells_x + at - self.cells_x
+        x = jnp.where(at < self.cells_x, gx * self.cells_x + at, far)
+        turn = kept * x % self.length_x
+        turn = (turn + jnp.where(crossed == 1, 3 * (self.length_x // 4), 0)) % self.length_x
+        return jnp.cos(turn.astype(F32) * (2.0 * math.pi / self.length_x))
 
 
 def tripled_table(table):
@@ -357,7 +347,7 @@
     return np.concatenate([high, high, low], axis=-1)
 
 
-def forward_kernel(plan, place, feat, keep, send, own_h, own_l, near_x, far_x, field):
+def forward_kernel(plan, place, feat, keep, send, own_h, own_l, near_x, far_x, far_y, field):
     channels, cells_x, cells_y = plan.channels, plan.cells_x, plan.cells_y
     gx, gy = plan.spot(place)
     even_x, even_y = gx % 2 == 0, gy % 2 == 0
@@ -375,7 +365,7 @@
         own_h[y] = high.reshape(cells_x, channels, -1)
         own_l[y] = low.reshape(cells_x, channels, -1)
         field[y * pad : (y + 1) * pad, :] = dot(z_table, triple((high, low), 1, True), NT)
-    y_table = triple(halves(plan.trig_y(gx, gy)), 1, False)
+    y_table = triple(halves(plan.trig_y(gx, gy, False)), 1, False)
     half = 8 * plan.turns
     for k in range(KZ):
         value = halves(field[pl.ds(k, 2 * cells_y, stride=plan.pad_k), :])
@@ -383,8 +373,8 @@
         keep[pl.ds(k, half, stride=KZ), :] = value[:half]
         send[pl.ds(k, half, stride=KZ), :] = value[half:]
     start = half * KZ
-    send[start : start + LANES, :] = jnp.where(even_y, ends[0], ends[1])
-    send[start + LANES :, :] = jnp.where(even_y, ends[1], ends[0])
+    send[start:, :] = jnp.where(even_y, ends[1], ends[0])
+    far_y[...] = jnp.where(even_y, ends[0], ends[1])
 
 
 def forward_modes(plan, place, features):
@@ -394,7 +384,7 @@
     shape = lambda *s: jax.ShapeDtypeStruct(s, F32)
     return kernel_call(
         functools.partial(forward_kernel, plan),
-        [shape(half, LANES), shape(half + 2 * LANES, LANES), own, own, face, face],
+        [shape(half, LANES), shape(half + LANES, LANES), own, own, face, face, shape(LANES, LANES)],
         [pltpu.VMEM((plan.cells_y * plan.pad_z, LANES), F32)],
         in_specs=specs(1),
     )(place, features.reshape(-1, length_z))
@@ -411,7 +401,7 @@
     return jnp.concatenate([value, jnp.zeros((LANES - value.shape[0], LANES), F32)], axis=0).T
 
 
-def x_forward_kernel(plan, place, own, from_x, from_y, from_xy, table, *refs):
+def x_forward_kernel(plan, place, own, from_xy, from_y, from_x, *refs):
     outs = refs[: plan.outer]
     straight, crossed, found = refs[plan.outer :]
     rows, channels, per = plan.rows, plan.channels, 2 * plan.per_gx
@@ -421,7 +411,7 @@
         value = square_turned(value)
         straight[at * LANES : (at + 1) * LANES, :] = value
         crossed[at * LANES : (at + 1) * LANES, :] = turned(value, plan.part, 1.0)
-    factor = table[plan.spot(place)[0]]
+    factor = triple(halves(plan.trig_x(plan.spot(place)[0], False)), 1, False)
     for c in range(channels):
         index = pl.ds(c, 2 * plan.cells_x, stride=channels)
         value = halves(jnp.concatenate([straight[index, :], crossed[index, :]], axis=0))
@@ -433,14 +423,14 @@
 
 def x_inverse_kernel(plan, place, *refs):
     parts = refs[: plan.outer]
-    table, near, far, straight, crossed, found = refs[plan.outer :]
+    near, far, straight, crossed, found = refs[plan.outer :]
     rows, channels, per = plan.rows, plan.channels, 2 * plan.per_gx
     size = per * channels
     for at, part in enumerate(parts):
         value = square_turned(part[...])[:size]
         straight[at * size : (at + 1) * size, :] = value
         crossed[at * size : (at + 1) * size, :] = turned(value, plan.part, -1.0)
-    factor = table[plan.spot(place)[0]]
+    factor = triple(halves(plan.trig_x(plan.spot(place)[0], True)), 1, False)
     for c in range(channels):
         index = pl.ds(c, plan.outer * per, stride=channels)
         value = halves(jnp.concatenate([straight[index, :], crossed[index, :]], axis=0))
@@ -454,8 +444,7 @@
     size = plan.outer * 2 * plan.per_gx * plan.channels
     scratch = [pltpu.VMEM((n, LANES), F32) for n in (2 * LANES, 2 * LANES, size)]
     body = functools.partial(x_forward_kernel, plan)
-    table = tripled_table(plan.table_x())
-    return kernel_call(body, [part] * plan.outer, scratch, in_specs=specs(5))(place, *parts, table)
+    return kernel_call(body, [part] * plan.outer, scratch, in_specs=specs(4))(place, *parts)
 
 
 def x_inverse(plan, place, parts):
@@ -463,13 +452,10 @@
     size = plan.outer * 2 * plan.per_gx * plan.channels
     scratch = [pltpu.VMEM((n, LANES), F32) for n in (size, size, 2 * LANES)]
     body = functools.partial(x_inverse_kernel, plan)
-    table = plan.table_x()
-    half = table.shape[2] // 2
-    table = tripled_table(np.concatenate([np.swapaxes(t, 1, 2) for t in (table[:, :, :half], table[:, :, half:])], axis=2))
-    return kernel_call(body, [part] * 2, scratch, in_specs=specs(plan.outer + 1))(place, *parts, table)
-
-
-def weight_kernel(plan, place, weight, keep, send, flat, sem):
+    return kernel_call(body, [part] * 2, scratch, in_specs=specs(plan.outer))(place, *parts)
+
+
+def weight_kernel(plan, place, weight, out, flat, sem):
     copy = pltpu.make_async_copy(weight.at[:, :, 0, :], flat, sem)
     copy.start()
     copy.wait()
@@ -492,17 +478,16 @@
                 total = jnp.where(inside, moved[:, :LANES], total)
             choice.append(total)
         at = slice(which * square, (which + 1) * square)
-        keep[at, :] = jnp.where(even, choice[0], choice[1])
-        send[at, :] = jnp.where(even, choice[1], choice[0])
+        out[at, :] = jnp.where(even, choice[0], choice[1])
+        out[slice(at.start + 2 * square, at.stop + 2 * square), :] = jnp.where(even, choice[1], choice[0])
 
 
 def weight_parts(plan, place, mix_weight):
     square = plan.channels * plan.channels
     modes = mix_weight.shape[-1]
-    out = jax.ShapeDtypeStruct((2 * square, LANES), F32)
     return kernel_call(
         functools.partial(weight_kernel, plan),
-        [out, out],
+        jax.ShapeDtypeStruct((4 * square, LANES), F32),
         [pltpu.VMEM((2, square, modes), F32), pltpu.SemaphoreType.DMA],
         in_specs=specs(1),
     )(place, mix_weight.reshape(2, square, 1, modes))
@@ -577,10 +562,13 @@
     )
 
 
-def final_kernel(plan, place, own, other, conv_a, conv_b, table_z, table_y, out, field):
+def final_kernel(plan, place, own, other, conv_a, conv_b, table_z, out, field, ready, sems):
     channels, cells_x, cells_y = plan.channels, plan.cells_x, plan.cells_y
+    pieces = ready.shape[0]
+    deep = cells_y // pieces
+    copies = [pltpu.make_async_copy(ready.at[n], out.at[:, pl.ds(n * deep, deep), :], sems.at[n]) for n in range(pieces)]
     gx, gy = plan.spot(place)
-    y_table = table_y[gy * 2 + gx % 2]
+    y_table = triple(halves(plan.trig_y(gx, gy, True)), 1, False)
     half = 8 * plan.turns
     field[...] = jnp.zeros(field.shape, F32)
     for k in range(KZ):
@@ -597,22 +585,29 @@
             conv = [ref[x, y] for ref in (conv_a, conv_b) for x in range(ref.shape[0])]
             layer = jnp.concatenate(conv, axis=0) + value[:, k * LANES : (k + 1) * LANES]
             layer = layer * 0.5 * (1.0 + lax.erf(layer * math.sqrt(0.5)))
+            flat = ready.at[y // deep].reshape(channels * cells_x * deep, plan.length_z)
             for x in range(cells_x):
-                out[pl.ds(x * cells_y + y, channels, stride=cells_x * cells_y), :] = layer[x * channels : (x + 1) * channels]
+                flat[pl.ds(x * deep + y % deep, channels, stride=cells_x * deep), :] = layer[x * channels : (x + 1) * channels]
+            if y % deep == deep - 1:
+                copies[y // deep].start()
+    for copy in copies:
+        copy.wait()
 
 
 def final_layer(plan, place, own, other, convs):
-    table_y = tripled_table(np.swapaxes(plan.table_y(), 1, 2))
     high, low = table_halves(plan.table_z_group())
     table_z = np.concatenate([high, low, high], axis=0)
     shape = (plan.channels, plan.cells_x, plan.cells_y, plan.length_z)
-    flat = (plan.channels * plan.cells_x * plan.cells_y, plan.length_z)
+    flat = (plan.channels * plan.cells_x, plan.cells_y, plan.length_z)
+    pieces = plan.cells_y // 8
+    ready = pltpu.VMEM((pieces, plan.channels * plan.cells_x, 8, plan.length_z), F32)
     return kernel_call(
         functools.partial(final_kernel, plan),
         jax.ShapeDtypeStruct(flat, F32),
-        [pltpu.VMEM((plan.cells_y * plan.pad_z, LANES), F32)],
-        in_specs=specs(6),
-    )(place, own, other, *convs, table_z, table_y).reshape(shape)
+        [pltpu.VMEM((plan.cells_y * plan.pad_z, LANES), F32), ready, pltpu.SemaphoreType.DMA((pieces,))],
+        in_specs=specs(5),
+        out_specs=pl.BlockSpec(memory_space=pltpu.HBM),
+    )(place, own, other, *convs, table_z).reshape(shape)
 
 
 def swap(plan, value, outer=0, pair=0, yy=0, core=0):
@@ -640,28 +635,33 @@
     place = (lax.axis_index("gx") * plan.count_gy + lax.axis_index("gy")).astype(jnp.int32).reshape(1)
     cells_x = features.shape[1]
 
-    keep, send, own_h, own_l, near_x, far_x = forward_modes(plan, place, features)
-    weight, away = weight_parts(plan, place, mix_weight)
+    keep, send, own_h, own_l, near_x, far_x, far_y = forward_modes(plan, place, features)
+    both = weight_parts(plan, place, mix_weight)
+    exchanged = swap(plan, both, core=1)
+    at_gx, at_gy = lax.axis_index("gx"), lax.axis_index("gy")
+    both = jnp.where(plan.half_of(at_gx, at_gy) == at_gy % 2, both, exchanged)
+    weight, away = both[: both.shape[0] // 2], both[both.shape[0] // 2 :]
     near_y = swap(plan, send, core=1)
     sums = [keep[s * rows : (s + 1) * rows] + near_y[s * rows : (s + 1) * rows] for s in range(4)]
-    passed = near_y[4 * rows : 4 * rows + LANES]
-    far_y = swap(plan, jnp.concatenate([sums[2], passed], axis=0), yy=1)
-    from_x = swap(plan, sums[1], pair=1)
+    far_y = swap(plan, jnp.concatenate([sums[2], far_y], axis=0), yy=1, core=1)
+    from_x = swap(plan, sums[1], pair=1, core=1)
     from_xy = swap(plan, sums[3], pair=1, yy=1)
     away = after(away, from_x, far_y, from_xy)
-    far_weight = swap(plan, away, pair=1)
-    chunks = x_forward(plan, place, [sums[0], from_x, far_y, from_xy])
-    parts = [chunks[0]] + [swap(plan, chunks[s], outer=s) for s in range(1, plan.outer)]
+    far_weight = swap(plan, away, pair=1, core=1)
+    chunks = x_forward(plan, place, [sums[0], from_xy, far_y, from_x])
+    got = {s: swap(plan, chunks[s], outer=s, core=s % 2) for s in range(plan.outer - 1, 0, -1)}
+    parts = [chunks[0]] + [got[s] for s in range(plan.outer - 1, 0, -1)]
     mixed = mix_modes(plan, parts, weight, far_weight)
     to_near, to_far = faces(plan, place, near_x, far_x, near_y, far_y, mixed)
     near_x = swap(plan, to_near, pair=1)
     far_x = next_pair(to_far, "gx")
-    parts = [mixed] + [swap(plan, mixed, outer=s) for s in range(1, plan.outer)]
+    got = {s: swap(plan, mixed, outer=s, core=s % 2) for s in range(plan.outer - 1, 0, -1)}
+    parts = [mixed] + [got[s] for s in range(1, plan.outer)]
     args = (near_x, far_x, near_y, far_y, conv_taps(conv_weight))
     half = cells_x // 2
     mine, theirs = x_inverse(plan, place, parts)
-    from_x = swap(plan, theirs, pair=1)
-    from_y = swap(plan, mine, yy=1)
+    from_x = swap(plan, theirs, pair=1, core=1)
+    from_y = swap(plan, mine, yy=1, core=1)
     from_xy = swap(plan, theirs, pair=1, yy=1)
     conv_a, token_a = conv_bricks(place, (own_h, own_l), *args, mine, 0, half)
     conv_b, _ = conv_bricks(place, (own_h, own_l), *args, mine, half, cells_x - half)

time: 46.3 us -> 43.5 us (0.940)
  starting transfers between devices: 21 us -> 19.5 us
  waiting for transfers between devices: 15 us -> 13.8 us
    ppermute x16 -> x17, starting transfers between devices: 20.5 us -> 17 us  [swap(): return lax.ppermute(value, ('gx', 'gy'), perm)]
    ppermute x1, starting transfers between devices: 0.52 us -> 2.54 us  [next_pair(): lax.ppermute(value, axis, [(i, (i + (1 if i % 2 else -1)) % size) for i i...]
    ppermute x16 -> x17, waiting for transfers between devices: 15 us -> 13.8 us  [swap(): return lax.ppermute(value, ('gx', 'gy'), perm)]
    unnamed x15 -> x9, local copies, waits for them, and re-layouts: 1.6 us -> 1.42 us
  transfers between devices with their start and end apart: 17 -> 18, of which waited for: 10 -> 8; matrix products, arithmetic and copies ran while one was open for 1% -> 1% of each run, Pallas kernels for 9% -> 10%
where the time goes in v3:
time: 43.5 us; the launch traced here: 43.3 us
  starting transfers between devices  19.5 us (45%)
  waiting for transfers between devices  13.8 us (32%)
  Pallas kernels  8 us (18%)
  local copies, waits for them, and re-layouts  1.7 us (4%)
    ppermute x17, starting transfers between devices, swap(): return lax.ppermute(value, ('gx', 'gy'), perm)  17 us
    ppermute x17, waiting for transfers between devices, swap(): return lax.ppermute(value, ('gx', 'gy'), perm)  13.8 us
    ppermute x1, starting transfers between devices, next_pair(): lax.ppermute(value, axis, [(i, (i + (1 if i % 2 else -1)) % size) for i i...  2.54 us
    pallas_call x1, Pallas kernels, final_layer(): kernel_call(functools.partial(final_kernel, plan), jax.ShapeDtypeStruct(f...  2.26 us
    pallas_call x2, Pallas kernels, conv_bricks(): kernel_call(functools.partial(conv_kernel, first, 2, lax.axis_size('gy'))...  2.16 us
    unnamed x9, local copies, waits for them, and re-layouts  1.42 us
    pallas_call x1, Pallas kernels, forward_modes(): kernel_call(functools.partial(forward_kernel, plan), [shape(half, LANES),...  1.17 us
  transfers between devices with their start and end apart: 18, of which 8 were waited for; matrix products, arithmetic and copies ran while one was open for 1% of the time, Pallas kernels for 10%

profile of v3, /device:TPU:0, one launch (start us, length us, event | category | flops | bytes accessed | tf_op | source)
XLA Modules:
  0.0 43.3 jit_solution(3224328942021427367)
XLA Ops:
  0.0 1.2 %copy-done = f32[16,8,16,128]{3,2,1,0:T(8,128)S(1)} copy-done((f32[16,8,16,128]{3,2,1,0:T(8,128)S(1)}, f32[16,8,16,128]{3,2,1,0:T(8,128)}, u32[]{:S(2)}) %copy-start) | copy-done | bytes 1048600
  1.2 1.2 %shard_map.46 = (f32[288,128]{1,0:T(8,128)S(1)}, f32[416,128]{1,0:T(8,128)S(1)}, bf16[16,8,16,128]{3,2,1,0:T(8,128)(2,1)S(1)}, bf16[16,8,16,128]{3,2,1,0:T(8,128...) custom-call(s32[1]{0:T(128)} %bitcast.place, f32[2048,128]{1,0:T(8,128)S(1)} %bitcast.11), custom_call_target="tpu_custom_call" | custom-call | tf_op jit(solution)/shard_map/pallas_call | solution.py:385
  2.4 0.5 %collective-permute-start = (f32[416,128]{1,0:T(8,128)S(1)}, f32[416,128]{1,0:T(8,128)S(1)}, u32[]{:S(2)}, u32[]{:S(2)}) collective-permute-start(f32[416,128]{1,0:T(8,128)S(1)} %get-tuple-element.24), channel_id=1, source_target_pairs={{0,1},{1,0},{2,3},{3,2},{4,5},{5,4},{6,7},{7,6},{8,9},{9,8},{10,11... | collective-permute-start | bytes 638984 | tf_op jit(solution)/shard_map/ppermute | solution.py:620
  2.9 0.8 %shard_map.48 = f32[1024,128]{1,0:T(8,128)S(1)} custom-call(s32[1]{0:T(128)} %bitcast.place, f32[2,256,1,216]{3,2,1,0:T(1,128)S(1)} %bitcast.12), custom_call_target="tpu_custom_call" | custom-call | tf_op jit(solution)/shard_map/pallas_call | solution.py:488
  3.8 0.1 collective-permute-start.7
  3.9 0.1 collective-permute-done.near_y
  4.1 2.7 %collective-permute-start.2 = (f32[200,128]{1,0:T(8,128)S(1)}, f32[200,128]{1,0:T(8,128)S(1)}, u32[]{:S(2)}, u32[]{:S(2)}) collective-permute-start(f32[200,128]{1,0:T(8,128)S(1)} %pad_maximum_fusion.1), channel_id=1, source_target_pairs={{0,3},{1,2},{2,1},{3,0},{4,7},{5,6},{6,5},{7,4},{8,11},{9,10},{10,... | collective-permute-start | bytes 307208 | tf_op jit(solution)/shard_map/ppermute | solution.py:620
  6.8 1.4 %collective-permute-start.1 = (f32[72,128]{1,0:T(8,128)S(1)}, f32[72,128]{1,0:T(8,128)S(1)}, u32[]{:S(2)}, u32[]{:S(2)}) collective-permute-start(f32[72,128]{1,0:T(8,128)S(1)} %get-tuple-element.45), channel_id=1, source_target_pairs={{0,6},{1,7},{2,4},{3,5},{4,2},{5,3},{6,0},{7,1},{8,14},{9,15},{10,... | collective-permute-start | bytes 110600 | tf_op jit(solution)/shard_map/ppermute | solution.py:620
  8.2 3.4 %collective-permute-done.1.from_xy = f32[72,128]{1,0:T(8,128)S(1)} collective-permute-done((f32[72,128]{1,0:T(8,128)S(1)}, f32[72,128]{1,0:T(8,128)S(1)}, u32[]{:S(2)}, u32[]{:S(2)}) %collective-permute-start.1) | collective-permute-done | bytes 36896 | tf_op jit(solution)/shard_map/ppermute | solution.py:620
  11.8 0.8 %collective-permute-start.8 = (f32[512,128]{1,0:T(8,128)S(1)}, f32[512,128]{1,0:T(8,128)S(1)}, u32[]{:S(2)}, u32[]{:S(2)}) collective-permute-start(f32[512,128]{1,0:T(8,128)S(1)} %get-tuple-element.41), channel_id=1, source_target_pairs={{0,5},{1,4},{2,7},{3,6},{4,1},{5,0},{6,3},{7,2},{8,13},{9,12},{10,... | collective-permute-start | bytes 786440 | tf_op jit(solution)/shard_map/ppermute | solution.py:620
  12.7 0.5 %shard_map.47 = (f32[72,128]{1,0:T(8,128)S(1)}, f32[72,128]{1,0:T(8,128)S(1)}, f32[72,128]{1,0:T(8,128)S(1)}, f32[72,128]{1,0:T(8,128)S(1)}) custom-call(s32[1]{0:T(128)} %bitcast.place, f32[72,128]{1,0:T(8,128)S(1)} %get-tuple-element.46.own, f32[72,128]{1,0:T(8,128)S(1)} %collective-permute-done.1.from_xy, ...), custom_call_target="tpu_custom_call" | custom-call | tf_op jit(solution)/shard_map/pallas_call | solution.py:447
  13.2 4.4 %collective-permute-start.4 = (f32[72,128]{1,0:T(8,128)S(1)}, f32[72,128]{1,0:T(8,128)S(1)}, u32[]{:S(2)}, u32[]{:S(2)}) collective-permute-start(f32[72,128]{1,0:T(8,128)S(1)} %get-tuple-element.27), channel_id=1, source_target_pairs={{0,25},{1,24},{2,27},{3,26},{4,29},{5,28},{6,31},{7,30},{8,17},{9,... | collective-permute-start | bytes 110600 | tf_op jit(solution)/shard_map/ppermute | solution.py:620
  17.6 0.4 collective-permute-start.6
  18.0 1.4 %collective-permute-done.4.refs_1_ = f32[72,128]{1,0:T(8,128)S(1)} collective-permute-done((f32[72,128]{1,0:T(8,128)S(1)}, f32[72,128]{1,0:T(8,128)S(1)}, u32[]{:S(2)}, u32[]{:S(2)}) %collective-permute-start.4) | collective-permute-done | bytes 36896 | tf_op jit(solution)/shard_map/ppermute | solution.py:620
  19.3 3.1 %collective-permute-done.5.refs_2_ = f32[72,128]{1,0:T(8,128)S(1)} collective-permute-done((f32[72,128]{1,0:T(8,128)S(1)}, f32[72,128]{1,0:T(8,128)S(1)}, u32[]{:S(2)}, u32[]{:S(2)}) %collective-permute-start.5) | collective-permute-done | bytes 36896 | tf_op jit(solution)/shard_map/ppermute | solution.py:620
  22.5 0.4 shard_map.49.refs_0_.after
  22.9 0.3 collective-permute-start.12
  23.3 2.5 %collective-permute-start.13 = (f32[288,128]{1,0:T(8,128)S(1)}, f32[288,128]{1,0:T(8,128)S(1)}, u32[]{:S(2)}, u32[]{:S(2)}) collective-permute-start(f32[288,128]{1,0:T(8,128)S(1)} %get-tuple-element.36), channel_id=1, source_target_pairs={{0,28},{4,8},{8,4},{12,16},{16,12},{20,24},{24,20},{28,0},{1,29},{... | collective-permute-start | bytes 442376 | tf_op jit(solution)/shard_map/ppermute | solution.py:625
  25.8 0.7 %collective-permute-start.11 = (f32[72,128]{1,0:T(8,128)S(1)}, f32[72,128]{1,0:T(8,128)S(1)}, u32[]{:S(2)}, u32[]{:S(2)}) collective-permute-start(f32[72,128]{1,0:T(8,128)S(1)} %shard_map.49.refs_0_.after), channel_id=1, source_target_pairs={{0,25},{1,24},{2,27},{3,26},{4,29},{5,28},{6,31},{7,30},{8,17},{9,... | collective-permute-start | bytes 110600 | tf_op jit(solution)/shard_map/ppermute | solution.py:620
  26.5 2.5 %collective-permute-start.9 = (f32[72,128]{1,0:T(8,128)S(1)}, f32[72,128]{1,0:T(8,128)S(1)}, u32[]{:S(2)}, u32[]{:S(2)}) collective-permute-start(f32[72,128]{1,0:T(8,128)S(1)} %shard_map.49.refs_0_.after), channel_id=1, source_target_pairs={{0,9},{1,8},{2,11},{3,10},{4,13},{5,12},{6,15},{7,14},{8,1},{9,0},... | collective-permute-start | bytes 110600 | tf_op jit(solution)/shard_map/ppermute | solution.py:620
  29.0 0.2 copy.6
  29.3 0.2 reshape.22.weight
  29.5 2.6 %collective-permute-done.10.refs_2_ = f32[72,128]{1,0:T(8,128)S(1)} collective-permute-done((f32[72,128]{1,0:T(8,128)S(1)}, f32[72,128]{1,0:T(8,128)S(1)}, u32[]{:S(2)}, u32[]{:S(2)}) %collective-permute-start.10) | collective-permute-done | bytes 36896 | tf_op jit(solution)/shard_map/ppermute | solution.py:620
  32.1 0.6 %shard_map.50 = (f32[72,128]{1,0:T(8,128)S(1)}, f32[72,128]{1,0:T(8,128)S(1)}) custom-call(s32[1]{0:T(128)} %bitcast.place, f32[72,128]{1,0:T(8,128)S(1)} %shard_map.49.refs_0_.after, f32[72,128]{1,0:T(8,128)S(1)} %collective-permute-done.9.refs_1_, f32[72,128]{1,0:T(8,128)S(1)} %collective-permute-done.10.refs_2_, f32[72,128]{1,0:T(8,128)S(1)} %collective-permute-done.11.refs_3_), custom_call_target="tpu_custom_call" | custom-call | tf_op jit(solution)/shard_map/pallas_call | solution.py:455
  32.7 1.4 %collective-permute-start.14 = (f32[72,128]{1,0:T(8,128)S(1)}, f32[72,128]{1,0:T(8,128)S(1)}, u32[]{:S(2)}, u32[]{:S(2)}) collective-permute-start(f32[72,128]{1,0:T(8,128)S(1)} %get-tuple-element.38), channel_id=1, source_target_pairs={{0,5},{1,4},{2,7},{3,6},{4,1},{5,0},{6,3},{7,2},{8,13},{9,12},{10,... | collective-permute-start | bytes 110600 | tf_op jit(solution)/shard_map/ppermute | solution.py:620
  34.1 1.5 %collective-permute-start.16 = (f32[72,128]{1,0:T(8,128)S(1)}, f32[72,128]{1,0:T(8,128)S(1)}, u32[]{:S(2)}, u32[]{:S(2)}) collective-permute-start(f32[72,128]{1,0:T(8,128)S(1)} %get-tuple-element.38), channel_id=1, source_target_pairs={{0,6},{1,7},{2,4},{3,5},{4,2},{5,3},{6,0},{7,1},{8,14},{9,15},{10,... | collective-permute-start | bytes 110600 | tf_op jit(solution)/shard_map/ppermute | solution.py:620
  35.5 0.2 collective-permute-start.15
  35.7 1.1 %shard_map.52 = (f32[4,16,16,128]{3,2,1,0:T(8,128)S(1)}, f32[8,128]{1,0:T(8,128)S(1)}) custom-call(s32[1]{0:T(128)} %bitcast.place, bf16[16,8,16,128]{3,2,1,0:T(8,128)(2,1)S(1)} %get-tuple-element.31.own_h, bf16[16,8,16,128]{3,2,1,0:T(8,128)(2,1)S(1)} %get-tuple-element.32.own_l, f32[288,128]{1,0:T(8,128)S(1)} %collective-permute-done.12.near_x, ...), custom_call_target="tpu_custom_call" | custom-call | tf_op jit(solution)/shard_map/pallas_call | solution.py:160
  36.8 2.8 %collective-permute-done.15 = f32[72,128]{1,0:T(8,128)S(1)} collective-permute-done((f32[72,128]{1,0:T(8,128)S(1)}, f32[72,128]{1,0:T(8,128)S(1)}, u32[]{:S(2)}, u32[]{:S(2)}) %collective-permute-start.15) | collective-permute-done | bytes 36896 | tf_op jit(solution)/shard_map/ppermute | solution.py:620
  39.7 1.1 %shard_map.53 = (f32[4,16,16,128]{3,2,1,0:T(8,128)S(1)}, f32[8,128]{1,0:T(8,128)}) custom-call(s32[1]{0:T(128)} %bitcast.place, bf16[16,8,16,128]{3,2,1,0:T(8,128)(2,1)S(1)} %get-tuple-element.31.own_h, bf16[16,8,16,128]{3,2,1,0:T(8,128)(2,1)S(1)} %get-tuple-element.32.own_l, f32[288,128]{1,0:T(8,128)S(1)} %collective-permute-done.12.near_x, ...), custom_call_target="tpu_custom_call" | custom-call | tf_op jit(solution)/shard_map/pallas_call | solution.py:160
  40.8 0.3 collective-permute-done.17.other
  41.1 2.3 %shard_map.54 = f32[128,16,128]{2,1,0:T(8,128)} custom-call(s32[1]{0:T(128)} %bitcast.place, f32[288,128]{1,0:T(8,128)S(1)} %pad_maximum_fusion.own, f32[288,128]{1,0:T(8,128)S(1)} %collective-permute-done.17.other, f32[4,16,16,128]{3,2,1,0:T(8,128)S(1)} %get-tuple-element.39.conv_a, f32[4,16,16,128]{3,2,1,0:T(8,128)S(1)} %get-tuple-element.40.conv_b, ...), custom_call_target="tpu_custom_call" | custom-call | tf_op jit(solution)/shard_map/pallas_call | solution.py:604
  (32 shorter events, 0.5 us)
Async XLA Ops:
  0.0 1.2 %copy-start = (f32[16,8,16,128]{3,2,1,0:T(8,128)S(1)}, f32[16,8,16,128]{3,2,1,0:T(8,128)}, u32[]{:S(2)}) copy-start(f32[16,8,16,128]{3,2,1,0:T(8,128)} %param.4) | copy-start | bytes 3145732
  1.2 1.7 %copy-start.1 = (f32[2,16,16,1,216]{4,3,2,1,0:T(1,128)S(1)}, f32[2,16,16,1,216]{4,3,2,1,0:T(1,128)}, u32[]{:S(2)}) copy-start(f32[2,16,16,1,216]{4,3,2,1,0:T(1,128)} %param.6) | copy-start | bytes 1327108
  2.4 1.6 %collective-permute-start = (f32[416,128]{1,0:T(8,128)S(1)}, f32[416,128]{1,0:T(8,128)S(1)}, u32[]{:S(2)}, u32[]{:S(2)}) collective-permute-start(f32[416,128]{1,0:T(8,128)S(1)} %get-tuple-element.24), channel_id=1, source_target_pairs={{0,1},{1,0},{2,3},{3,2},{4,5},{5,4},{6,7},{7,6},{8,9},{9,8},{10,11... | collective-permute-start | bytes 638984 | tf_op jit(solution)/shard_map/ppermute | solution.py:620
  3.8 8.0 %collective-permute-start.7 = (f32[1024,128]{1,0:T(8,128)S(1)}, f32[1024,128]{1,0:T(8,128)S(1)}, u32[]{:S(2)}, u32[]{:S(2)}) collective-permute-start(f32[1024,128]{1,0:T(8,128)S(1)} %shard_map.48), channel_id=1, source_target_pairs={{0,1},{1,0},{2,3},{3,2},{4,5},{5,4},{6,7},{7,6},{8,9},{9,8},{10,11... | collective-permute-start | bytes 1572872 | tf_op jit(solution)/shard_map/ppermute | solution.py:620
  4.1 7.7 %collective-permute-start.2 = (f32[200,128]{1,0:T(8,128)S(1)}, f32[200,128]{1,0:T(8,128)S(1)}, u32[]{:S(2)}, u32[]{:S(2)}) collective-permute-start(f32[200,128]{1,0:T(8,128)S(1)} %pad_maximum_fusion.1), channel_id=1, source_target_pairs={{0,3},{1,2},{2,1},{3,0},{4,7},{5,6},{6,5},{7,4},{8,11},{9,10},{10,... | collective-permute-start | bytes 307208 | tf_op jit(solution)/shard_map/ppermute | solution.py:620
  6.8 4.9 %collective-permute-start.1 = (f32[72,128]{1,0:T(8,128)S(1)}, f32[72,128]{1,0:T(8,128)S(1)}, u32[]{:S(2)}, u32[]{:S(2)}) collective-permute-start(f32[72,128]{1,0:T(8,128)S(1)} %get-tuple-element.45), channel_id=1, source_target_pairs={{0,6},{1,7},{2,4},{3,5},{4,2},{5,3},{6,0},{7,1},{8,14},{9,15},{10,... | collective-permute-start | bytes 110600 | tf_op jit(solution)/shard_map/ppermute | solution.py:620
  8.2 3.5 %collective-permute-start.3 = (f32[72,128]{1,0:T(8,128)S(1)}, f32[72,128]{1,0:T(8,128)S(1)}, u32[]{:S(2)}, u32[]{:S(2)}) collective-permute-start(f32[72,128]{1,0:T(8,128)S(1)} %get-tuple-element.43), channel_id=1, source_target_pairs={{0,5},{1,4},{2,7},{3,6},{4,1},{5,0},{6,3},{7,2},{8,13},{9,12},{10,... | collective-permute-start | bytes 110600 | tf_op jit(solution)/shard_map/ppermute | solution.py:620
  11.8 10.6 %collective-permute-start.8 = (f32[512,128]{1,0:T(8,128)S(1)}, f32[512,128]{1,0:T(8,128)S(1)}, u32[]{:S(2)}, u32[]{:S(2)}) collective-permute-start(f32[512,128]{1,0:T(8,128)S(1)} %get-tuple-element.41), channel_id=1, source_target_pairs={{0,5},{1,4},{2,7},{3,6},{4,1},{5,0},{6,3},{7,2},{8,13},{9,12},{10,... | collective-permute-start | bytes 786440 | tf_op jit(solution)/shard_map/ppermute | solution.py:620
  13.2 6.2 %collective-permute-start.4 = (f32[72,128]{1,0:T(8,128)S(1)}, f32[72,128]{1,0:T(8,128)S(1)}, u32[]{:S(2)}, u32[]{:S(2)}) collective-permute-start(f32[72,128]{1,0:T(8,128)S(1)} %get-tuple-element.27), channel_id=1, source_target_pairs={{0,25},{1,24},{2,27},{3,26},{4,29},{5,28},{6,31},{7,30},{8,17},{9,... | collective-permute-start | bytes 110600 | tf_op jit(solution)/shard_map/ppermute | solution.py:620
  17.6 4.9 %collective-permute-start.5 = (f32[72,128]{1,0:T(8,128)S(1)}, f32[72,128]{1,0:T(8,128)S(1)}, u32[]{:S(2)}, u32[]{:S(2)}) collective-permute-start(f32[72,128]{1,0:T(8,128)S(1)} %get-tuple-element.28), channel_id=1, source_target_pairs={{0,16},{1,17},{2,18},{3,19},{4,20},{5,21},{6,22},{7,23},{8,24},{9,... | collective-permute-start | bytes 110600 | tf_op jit(solution)/shard_map/ppermute | solution.py:620
  17.6 4.9 %collective-permute-start.6 = (f32[72,128]{1,0:T(8,128)S(1)}, f32[72,128]{1,0:T(8,128)S(1)}, u32[]{:S(2)}, u32[]{:S(2)}) collective-permute-start(f32[72,128]{1,0:T(8,128)S(1)} %get-tuple-element.29), channel_id=1, source_target_pairs={{0,9},{1,8},{2,11},{3,10},{4,13},{5,12},{6,15},{7,14},{8,1},{9,0},... | collective-permute-start | bytes 110600 | tf_op jit(solution)/shard_map/ppermute | solution.py:620
  22.9 6.1 %copy-start.3 = (f32[27,16,16]{0,2,1:T(8,128)S(1)}, f32[27,16,16]{0,2,1:T(8,128)}, u32[]{:S(2)}) copy-start(f32[27,16,16]{0,2,1:T(8,128)} %param.5) | copy-start | bytes 82948
  22.9 12.8 %collective-permute-start.12 = (f32[288,128]{1,0:T(8,128)S(1)}, f32[288,128]{1,0:T(8,128)S(1)}, u32[]{:S(2)}, u32[]{:S(2)}) collective-permute-start(f32[288,128]{1,0:T(8,128)S(1)} %get-tuple-element.35), channel_id=1, source_target_pairs={{0,4},{1,5},{2,6},{3,7},{4,0},{5,1},{6,2},{7,3},{8,12},{9,13},{10,... | collective-permute-start | bytes 442376 | tf_op jit(solution)/shard_map/ppermute | solution.py:620
  23.3 12.4 %collective-permute-start.13 = (f32[288,128]{1,0:T(8,128)S(1)}, f32[288,128]{1,0:T(8,128)S(1)}, u32[]{:S(2)}, u32[]{:S(2)}) collective-permute-start(f32[288,128]{1,0:T(8,128)S(1)} %get-tuple-element.36), channel_id=1, source_target_pairs={{0,28},{4,8},{8,4},{12,16},{16,12},{20,24},{24,20},{28,0},{1,29},{... | collective-permute-start | bytes 442376 | tf_op jit(solution)/shard_map/ppermute | solution.py:625
  25.8 6.3 %collective-permute-start.10 = (f32[72,128]{1,0:T(8,128)S(1)}, f32[72,128]{1,0:T(8,128)S(1)}, u32[]{:S(2)}, u32[]{:S(2)}) collective-permute-start(f32[72,128]{1,0:T(8,128)S(1)} %shard_map.49.refs_0_.after), channel_id=1, source_target_pairs={{0,16},{1,17},{2,18},{3,19},{4,20},{5,21},{6,22},{7,23},{8,24},{9,... | collective-permute-start | bytes 110600 | tf_op jit(solution)/shard_map/ppermute | solution.py:620
  25.8 6.3 %collective-permute-start.11 = (f32[72,128]{1,0:T(8,128)S(1)}, f32[72,128]{1,0:T(8,128)S(1)}, u32[]{:S(2)}, u32[]{:S(2)}) collective-permute-start(f32[72,128]{1,0:T(8,128)S(1)} %shard_map.49.refs_0_.after), channel_id=1, source_target_pairs={{0,25},{1,24},{2,27},{3,26},{4,29},{5,28},{6,31},{7,30},{8,17},{9,... | collective-permute-start | bytes 110600 | tf_op jit(solution)/shard_map/ppermute | solution.py:620
  26.5 5.6 %collective-permute-start.9 = (f32[72,128]{1,0:T(8,128)S(1)}, f32[72,128]{1,0:T(8,128)S(1)}, u32[]{:S(2)}, u32[]{:S(2)}) collective-permute-start(f32[72,128]{1,0:T(8,128)S(1)} %shard_map.49.refs_0_.after), channel_id=1, source_target_pairs={{0,9},{1,8},{2,11},{3,10},{4,13},{5,12},{6,15},{7,14},{8,1},{9,0},... | collective-permute-start | bytes 110600 | tf_op jit(solution)/shard_map/ppermute | solution.py:620
  32.7 4.1 %collective-permute-start.14 = (f32[72,128]{1,0:T(8,128)S(1)}, f32[72,128]{1,0:T(8,128)S(1)}, u32[]{:S(2)}, u32[]{:S(2)}) collective-permute-start(f32[72,128]{1,0:T(8,128)S(1)} %get-tuple-element.38), channel_id=1, source_target_pairs={{0,5},{1,4},{2,7},{3,6},{4,1},{5,0},{6,3},{7,2},{8,13},{9,12},{10,... | collective-permute-start | bytes 110600 | tf_op jit(solution)/shard_map/ppermute | solution.py:620
  34.1 5.5 %collective-permute-start.16 = (f32[72,128]{1,0:T(8,128)S(1)}, f32[72,128]{1,0:T(8,128)S(1)}, u32[]{:S(2)}, u32[]{:S(2)}) collective-permute-start(f32[72,128]{1,0:T(8,128)S(1)} %get-tuple-element.38), channel_id=1, source_target_pairs={{0,6},{1,7},{2,4},{3,5},{4,2},{5,3},{6,0},{7,1},{8,14},{9,15},{10,... | collective-permute-start | bytes 110600 | tf_op jit(solution)/shard_map/ppermute | solution.py:620
  35.5 4.1 %collective-permute-start.15 = (f32[72,128]{1,0:T(8,128)S(1)}, f32[72,128]{1,0:T(8,128)S(1)}, u32[]{:S(2)}, u32[]{:S(2)}) collective-permute-start(f32[72,128]{1,0:T(8,128)S(1)} %get-tuple-element.30.after), channel_id=1, source_target_pairs={{0,3},{1,2},{2,1},{3,0},{4,7},{5,6},{6,5},{7,4},{8,11},{9,10},{10,... | collective-permute-start | bytes 110600 | tf_op jit(solution)/shard_map/ppermute | solution.py:620
  39.6 1.5 %copy-start.2 = (bf16[384,512]{1,0:T(8,128)(2,1)S(1)}, bf16[384,512]{1,0:T(8,128)(2,1)}, u32[]{:S(2)}) copy-start(bf16[384,512]{1,0:T(8,128)(2,1)} %constant.50.clone.table_z) | copy-start | bytes 1179652
  39.6 1.4 %collective-permute-start.17 = (f32[288,128]{1,0:T(8,128)S(1)}, f32[288,128]{1,0:T(8,128)S(1)}, u32[]{:S(2)}, u32[]{:S(2)}) collective-permute-start(f32[288,128]{1,0:T(8,128)S(1)} %pad_maximum_fusion.own), channel_id=1, source_target_pairs={{0,1},{1,0},{2,3},{3,2},{4,5},{5,4},{6,7},{7,6},{8,9},{9,8},{10,11... | collective-permute-start | bytes 442376 | tf_op jit(solution)/shard_map/ppermute | solution.py:620

commit v4 on v3

--- a/solution.py
+++ b/solution.py
@@ -72,9 +72,10 @@
             high[y, x], low[y, x] = halves(feat[:, x, y, :])
 
 
-def conv_kernel(first, rows_y, count_gy, place, own_h, own_l, near_x, far_x, near_y, far_y, weight, after, out, token, edge_h, edge_l, rim_h, rim_l):
+def conv_kernel(columns, rows_y, count_gy, place, own_h, own_l, near_x, far_x, near_y, far_y, weight, after, out, *refs):
+    tokens, (edge_h, edge_l, rim_h, rim_l) = refs[:-4], refs[-4:]
     cells_y, cells_x, channels, length_z = own_h.shape
-    count = out.shape[0]
+    needed = sorted({x + a for x in columns for a in range(3)})
     span = rows_y + 2
     depth = 3 * span * channels
     even_x, even_y = place[0] // count_gy % 2 == 0, place[0] % count_gy % 2 == 0
@@ -88,7 +89,7 @@
         return halves(jnp.where(even, near, far) if side else jnp.where(even, far, near))
 
     for side in range(2):
-        if (0, cells_x + 1)[side] in range(first, first + count + 2):
+        if (0, cells_x + 1)[side] in needed:
             for y in range(cells_y):
                 edge_h[side, y + 1], edge_l[side, y + 1] = pick(side, even_x, near_x, far_x, column, y)
             corners = [
@@ -98,7 +99,7 @@
             for up in range(2):
                 value = jnp.where(even_y == bool(up), *corners)
                 edge_h[side, up * (cells_y + 1)], edge_l[side, up * (cells_y + 1)] = halves(value)
-        for x in range(max(first - 1, 0), min(first + count + 1, cells_x)):
+        for x in [n - 1 for n in needed if 0 < n <= cells_x]:
             rim_h[side, x], rim_l[side, x] = pick(side, even_y, near_y, far_y, row, x)
 
     def cell(which, x, y):
@@ -121,15 +122,15 @@
         for which in range(2):
             bands[which].append(dot(taps[which], match).astype(BF16))
     bands = [jnp.concatenate(b, axis=0) for b in bands]
-    for x in range(0, count, 2):
+    for n in range(0, len(columns), 2):
         for y in range(0, cells_y, rows_y):
             field = []
             for which in range(2):
-                columns = []
+                lanes = []
                 for p in range(2):
-                    cells = [cell(which, first + x + p + a, y + k) for a in range(3) for k in range(span)]
-                    columns.append(jnp.concatenate(cells, axis=0))
-                field.append(jnp.concatenate(columns, axis=1))
+                    cells = [cell(which, columns[n + p] + a, y + k) for a in range(3) for k in range(span)]
+                    lanes.append(jnp.concatenate(cells, axis=0))
+                field.append(jnp.concatenate(lanes, axis=1))
             value = dot3(bands, field)
             for k in range(rows_y):
                 for p in range(2):
@@ -140,8 +141,9 @@
                         if c != 1:
                             piece = pltpu.roll(piece, (1 - c) % length_z, 1)
                         total = piece if total is None else total + piece
-                    out[x + p, y + k] = total
-    token[...] = jnp.zeros(token.shape, F32)
+                    out[n + p, y + k] = total
+    for token in tokens:
+        token[...] = jnp.zeros(token.shape, F32)
 
 
 def conv_taps(conv_weight):
@@ -155,11 +157,14 @@
     return [pl.BlockSpec(memory_space=pltpu.SMEM)] + [vmem] * count
 
 
-def conv_bricks(place, own, near_x, far_x, near_y, far_y, taps, after, first, count):
+def conv_bricks(place, own, near_x, far_x, near_y, far_y, taps, after, columns, mark=False):
     cells_y, cells_x, channels, length_z = own[0].shape
+    outs = [jax.ShapeDtypeStruct((len(columns), cells_y, channels, length_z), F32)]
+    if mark:
+        outs.append(jax.ShapeDtypeStruct((8, length_z), F32))
     return kernel_call(
-        functools.partial(conv_kernel, first, 2, lax.axis_size("gy")),
-        [jax.ShapeDtypeStruct((count, cells_y, channels, length_z), F32), jax.ShapeDtypeStruct((8, LANES), F32)],
+        functools.partial(conv_kernel, tuple(columns), 2, lax.axis_size("gy")),
+        outs,
         [pltpu.VMEM((2, cells_y + 2, channels, length_z), BF16)] * 2 + [pltpu.VMEM((2, cells_x, channels, length_z), BF16)] * 2,
         in_specs=specs(8),
     )(place, *own, near_x, far_x, near_y, far_y, taps, after)
@@ -266,7 +271,7 @@
     def fits(feature_shape, count_gx, count_gy):
         channels, cells_x, cells_y, length_z = feature_shape
         outer = count_gx // 2
-        if count_gy != 4 or count_gx % 2 or outer & (outer - 1) or outer > 4:
+        if count_gy != 4 or count_gx < 4 or count_gx % 2 or outer & (outer - 1) or outer > 4:
             return False
         if KX % count_gx or (KY * KZ) % (2 * count_gy) or channels * cells_x != LANES:
             return False
@@ -274,6 +279,8 @@
         per = KX // count_gx
         return (
             length_z == LANES
+            and cells_x >= 4
+            and cells_x % 2 == 0
             and cells_y % (LANES // (2 * (-(-KZ // 8) * 8))) == 0
             and channels % 16 == 0
             and (2 * part) % 8 == 0
@@ -401,7 +408,7 @@
     return jnp.concatenate([value, jnp.zeros((LANES - value.shape[0], LANES), F32)], axis=0).T
 
 
-def x_forward_kernel(plan, place, own, from_xy, from_y, from_x, *refs):
+def x_forward_kernel(plan, place, own, from_x, from_y, from_xy, *refs):
     outs = refs[: plan.outer]
     straight, crossed, found = refs[plan.outer :]
     rows, channels, per = plan.rows, plan.channels, 2 * plan.per_gx
@@ -515,7 +522,7 @@
 
 def mix_kernel(plan, *refs):
     parts = refs[: plan.outer]
-    near, far, out = refs[plan.outer :]
+    near, far, _, out = refs[plan.outer :]
     channels, part, per, rows = plan.channels, plan.part, plan.per_gx, plan.rows
     total = parts[0][...]
     for p in parts[1:]:
@@ -556,13 +563,13 @@
     out[...] = jnp.concatenate(blocks, axis=0).T[:rows]
 
 
-def mix_modes(plan, parts, near, far):
+def mix_modes(plan, parts, near, far, before):
     return kernel_call(functools.partial(mix_kernel, plan), jax.ShapeDtypeStruct((plan.rows, LANES), F32))(
-        *parts, near, far
+        *parts, near, far, before
     )
 
 
-def final_kernel(plan, place, own, other, conv_a, conv_b, table_z, out, field, ready, sems):
+def final_kernel(plan, place, own, other, outer, inner, table_z, out, field, ready, sems):
     channels, cells_x, cells_y = plan.channels, plan.cells_x, plan.cells_y
     pieces = ready.shape[0]
     deep = cells_y // pieces
@@ -582,7 +589,7 @@
         value = dot(triple(planes, 1, False), z_table)
         for k in range(group):
             y = g * group + k
-            conv = [ref[x, y] for ref in (conv_a, conv_b) for x in range(ref.shape[0])]
+            conv = [outer[0, y]] + [inner[x, y] for x in range(inner.shape[0])] + [outer[1, y]]
             layer = jnp.concatenate(conv, axis=0) + value[:, k * LANES : (k + 1) * LANES]
             layer = layer * 0.5 * (1.0 + lax.erf(layer * math.sqrt(0.5)))
             flat = ready.at[y // deep].reshape(channels * cells_x * deep, plan.length_z)
@@ -648,26 +655,26 @@
     from_xy = swap(plan, sums[3], pair=1, yy=1)
     away = after(away, from_x, far_y, from_xy)
     far_weight = swap(plan, away, pair=1, core=1)
-    chunks = x_forward(plan, place, [sums[0], from_xy, far_y, from_x])
+    chunks = x_forward(plan, place, [sums[0], from_x, far_y, from_xy])
     got = {s: swap(plan, chunks[s], outer=s, core=s % 2) for s in range(plan.outer - 1, 0, -1)}
-    parts = [chunks[0]] + [got[s] for s in range(plan.outer - 1, 0, -1)]
-    mixed = mix_modes(plan, parts, weight, far_weight)
-    to_near, to_far = faces(plan, place, near_x, far_x, near_y, far_y, mixed)
-    near_x = swap(plan, to_near, pair=1)
+    parts = [chunks[0]] + [got[s] for s in (*range(2, plan.outer), 1)]
+    taps = conv_taps(conv_weight)
+    mixed = mix_modes(plan, parts, weight, far_weight, taps)
+    to_near, to_far = faces(plan, place, near_x, far_x, near_y, far_y, chunks[0])
+    near_x = swap(plan, after(to_near, mixed), pair=1)
     far_x = next_pair(to_far, "gx")
     got = {s: swap(plan, mixed, outer=s, core=s % 2) for s in range(plan.outer - 1, 0, -1)}
     parts = [mixed] + [got[s] for s in range(1, plan.outer)]
-    args = (near_x, far_x, near_y, far_y, conv_taps(conv_weight))
-    half = cells_x // 2
+    args = (near_x, far_x, near_y, far_y, taps)
     mine, theirs = x_inverse(plan, place, parts)
     from_x = swap(plan, theirs, pair=1, core=1)
     from_y = swap(plan, mine, yy=1, core=1)
     from_xy = swap(plan, theirs, pair=1, yy=1)
-    conv_a, token_a = conv_bricks(place, (own_h, own_l), *args, mine, 0, half)
-    conv_b, _ = conv_bricks(place, (own_h, own_l), *args, mine, half, cells_x - half)
-    own = jnp.concatenate([mine + token_a[:1], from_x, from_y, from_xy], axis=0)
+    inner, token = conv_bricks(place, (own_h, own_l), near_y, near_y, *args[2:], mine, range(1, cells_x - 1), True)
+    (outer,) = conv_bricks(place, (own_h, own_l), *args, mine, (0, cells_x - 1))
+    own = jnp.concatenate([mine + token[:1], from_x, from_y, from_xy], axis=0)
     other = swap(plan, own, core=1)
-    return final_layer(plan, place, own, other, (conv_a, conv_b))
+    return final_layer(plan, place, own, other, (outer, inner))
 
 
 def layer_any(features, conv_weight, mix_weight):
@@ -675,7 +682,7 @@
     own = jax.ShapeDtypeStruct((cells_y, cells_x, channels, length_z), BF16)
     own = kernel_call(split_kernel, [own, own])(features)
     taps = conv_taps(conv_weight)
-    conv, _ = conv_bricks(jnp.zeros((1,), jnp.int32), own, *halos(features), taps, taps, 0, cells_x)
+    (conv,) = conv_bricks(jnp.zeros((1,), jnp.int32), own, *halos(features), taps, taps, range(cells_x))
     return jax.nn.gelu(conv.transpose(2, 0, 1, 3) + spectral_any(features, mix_weight), approximate=False)
 
 

time: 43.5 us -> 39.7 us (0.913)
  waiting for transfers between devices: 13.8 us -> 8.52 us
  starting transfers between devices: 19.5 us -> 21 us
    ppermute x17, waiting for transfers between devices: 13.8 us -> 8.52 us  [swap(): return lax.ppermute(value, ('gx', 'gy'), perm)]
    ppermute x17, starting transfers between devices: 17 us -> 18.2 us  [swap(): return lax.ppermute(value, ('gx', 'gy'), perm)]
  transfers between devices with their start and end apart: 18 -> 18, of which waited for: 8 -> 11; matrix products, arithmetic and copies ran while one was open for 1% -> 1% of each run, Pallas kernels for 10% -> 12%
where the time goes in v4:
time: 39.7 us; the launch traced here: 39.5 us
  starting transfers between devices  21 us (53%)
  waiting for transfers between devices  8.52 us (21%)
  Pallas kernels  8 us (20%)
  local copies, waits for them, and re-layouts  1.71 us (4%)
    ppermute x17, starting transfers between devices, swap(): return lax.ppermute(value, ('gx', 'gy'), perm)  18.2 us
    ppermute x17, waiting for transfers between devices, swap(): return lax.ppermute(value, ('gx', 'gy'), perm)  8.52 us
    ppermute x1, starting transfers between devices, next_pair(): lax.ppermute(value, axis, [(i, (i + (1 if i % 2 else -1)) % size) for i i...  2.74 us
    pallas_call x1, Pallas kernels, final_layer(): kernel_call(functools.partial(final_kernel, plan), jax.ShapeDtypeStruct(f...  2.26 us
    pallas_call x2, Pallas kernels, conv_bricks(): kernel_call(functools.partial(conv_kernel, tuple(columns), 2, lax.axis_si...  2.16 us
    unnamed x9, local copies, waits for them, and re-layouts  1.42 us
    pallas_call x1, Pallas kernels, forward_modes(): kernel_call(functools.partial(forward_kernel, plan), [shape(half, LANES),...  1.17 us
    pallas_call x1, Pallas kernels, weight_parts(): kernel_call(functools.partial(weight_kernel, plan), jax.ShapeDtypeStruct(...  0.83 us
  transfers between devices with their start and end apart: 18, of which 11 were waited for; matrix products, arithmetic and copies ran while one was open for 1% of the time, Pallas kernels for 12%

profile of v4, /device:TPU:0, one launch (start us, length us, event | category | flops | bytes accessed | tf_op | source)
XLA Modules:
  0.0 39.5 jit_solution(8166613291350034348)
XLA Ops:
  0.0 1.2 %copy-done = f32[16,8,16,128]{3,2,1,0:T(8,128)S(1)} copy-done((f32[16,8,16,128]{3,2,1,0:T(8,128)S(1)}, f32[16,8,16,128]{3,2,1,0:T(8,128)}, u32[]{:S(2)}) %copy-start) | copy-done | bytes 1048600
  1.2 1.2 %shard_map.46 = (f32[288,128]{1,0:T(8,128)S(1)}, f32[416,128]{1,0:T(8,128)S(1)}, bf16[16,8,16,128]{3,2,1,0:T(8,128)(2,1)S(1)}, bf16[16,8,16,128]{3,2,1,0:T(8,128...) custom-call(s32[1]{0:T(128)} %bitcast.place, f32[2048,128]{1,0:T(8,128)S(1)} %bitcast.13), custom_call_target="tpu_custom_call" | custom-call | tf_op jit(solution)/shard_map/pallas_call | solution.py:392
  2.4 0.5 %collective-permute-start = (f32[416,128]{1,0:T(8,128)S(1)}, f32[416,128]{1,0:T(8,128)S(1)}, u32[]{:S(2)}, u32[]{:S(2)}) collective-permute-start(f32[416,128]{1,0:T(8,128)S(1)} %get-tuple-element.23), channel_id=1, source_target_pairs={{0,1},{1,0},{2,3},{3,2},{4,5},{5,4},{6,7},{7,6},{8,9},{9,8},{10,11... | collective-permute-start | bytes 638984 | tf_op jit(solution)/shard_map/ppermute | solution.py:627
  2.9 0.8 %shard_map.48 = f32[1024,128]{1,0:T(8,128)S(1)} custom-call(s32[1]{0:T(128)} %bitcast.place, f32[2,256,1,216]{3,2,1,0:T(1,128)S(1)} %bitcast.14), custom_call_target="tpu_custom_call" | custom-call | tf_op jit(solution)/shard_map/pallas_call | solution.py:495
  4.1 2.7 %collective-permute-start.2 = (f32[200,128]{1,0:T(8,128)S(1)}, f32[200,128]{1,0:T(8,128)S(1)}, u32[]{:S(2)}, u32[]{:S(2)}) collective-permute-start(f32[200,128]{1,0:T(8,128)S(1)} %pad_maximum_fusion.1), channel_id=1, source_target_pairs={{0,3},{1,2},{2,1},{3,0},{4,7},{5,6},{6,5},{7,4},{8,11},{9,10},{10,... | collective-permute-start | bytes 307208 | tf_op jit(solution)/shard_map/ppermute | solution.py:627
  6.8 1.4 %collective-permute-start.3 = (f32[72,128]{1,0:T(8,128)S(1)}, f32[72,128]{1,0:T(8,128)S(1)}, u32[]{:S(2)}, u32[]{:S(2)}) collective-permute-start(f32[72,128]{1,0:T(8,128)S(1)} %get-tuple-element.41), channel_id=1, source_target_pairs={{0,6},{1,7},{2,4},{3,5},{4,2},{5,3},{6,0},{7,1},{8,14},{9,15},{10,... | collective-permute-start | bytes 110600 | tf_op jit(solution)/shard_map/ppermute | solution.py:627
  8.2 3.4 %collective-permute-done.3.from_xy = f32[72,128]{1,0:T(8,128)S(1)} collective-permute-done((f32[72,128]{1,0:T(8,128)S(1)}, f32[72,128]{1,0:T(8,128)S(1)}, u32[]{:S(2)}, u32[]{:S(2)}) %collective-permute-start.3) | collective-permute-done | bytes 36896 | tf_op jit(solution)/shard_map/ppermute | solution.py:627
  11.9 0.8 %collective-permute-start.8 = (f32[512,128]{1,0:T(8,128)S(1)}, f32[512,128]{1,0:T(8,128)S(1)}, u32[]{:S(2)}, u32[]{:S(2)}) collective-permute-start(f32[512,128]{1,0:T(8,128)S(1)} %get-tuple-element.39), channel_id=1, source_target_pairs={{0,5},{1,4},{2,7},{3,6},{4,1},{5,0},{6,3},{7,2},{8,13},{9,12},{10,... | collective-permute-start | bytes 786440 | tf_op jit(solution)/shard_map/ppermute | solution.py:627
  12.7 0.5 %shard_map.47 = (f32[72,128]{1,0:T(8,128)S(1)}, f32[72,128]{1,0:T(8,128)S(1)}, f32[72,128]{1,0:T(8,128)S(1)}, f32[72,128]{1,0:T(8,128)S(1)}) custom-call(s32[1]{0:T(128)} %bitcast.place, f32[72,128]{1,0:T(8,128)S(1)} %get-tuple-element.44.own, f32[72,128]{1,0:T(8,128)S(1)} %collective-permute-done.1.from_x, ...), custom_call_target="tpu_custom_call" | custom-call | tf_op jit(solution)/shard_map/pallas_call | solution.py:454
  13.2 2.8 %collective-permute-start.4 = (f32[72,128]{1,0:T(8,128)S(1)}, f32[72,128]{1,0:T(8,128)S(1)}, u32[]{:S(2)}, u32[]{:S(2)}) collective-permute-start(f32[72,128]{1,0:T(8,128)S(1)} %get-tuple-element.26), channel_id=1, source_target_pairs={{0,16},{1,17},{2,18},{3,19},{4,20},{5,21},{6,22},{7,23},{8,24},{9,... | collective-permute-start | bytes 110600 | tf_op jit(solution)/shard_map/ppermute | solution.py:627
  16.0 1.7 %collective-permute-start.5 = (f32[72,128]{1,0:T(8,128)S(1)}, f32[72,128]{1,0:T(8,128)S(1)}, u32[]{:S(2)}, u32[]{:S(2)}) collective-permute-start(f32[72,128]{1,0:T(8,128)S(1)} %get-tuple-element.27), channel_id=1, source_target_pairs={{0,25},{1,24},{2,27},{3,26},{4,29},{5,28},{6,31},{7,30},{8,17},{9,... | collective-permute-start | bytes 110600 | tf_op jit(solution)/shard_map/ppermute | solution.py:627
  17.7 0.2 collective-permute-start.6
  17.9 0.2 copy.6
  18.4 2.7 %collective-permute-start.17 = (f32[288,128]{1,0:T(8,128)S(1)}, f32[288,128]{1,0:T(8,128)S(1)}, u32[]{:S(2)}, u32[]{:S(2)}) collective-permute-start(f32[288,128]{1,0:T(8,128)S(1)} %get-tuple-element.37), channel_id=1, source_target_pairs={{0,28},{4,8},{8,4},{12,16},{16,12},{20,24},{24,20},{28,0},{1,29},{... | collective-permute-start | bytes 442376 | tf_op jit(solution)/shard_map/ppermute | solution.py:632
  21.1 0.2 collective-permute-done.5.refs_2_
  21.3 0.8 %collective-permute-done.6.refs_3_ = f32[72,128]{1,0:T(8,128)S(1)} collective-permute-done((f32[72,128]{1,0:T(8,128)S(1)}, f32[72,128]{1,0:T(8,128)S(1)}, u32[]{:S(2)}, u32[]{:S(2)}) %collective-permute-start.6) | collective-permute-done | bytes 36896 | tf_op jit(solution)/shard_map/ppermute | solution.py:627
  22.1 0.4 %shard_map.49.refs_0_ = f32[72,128]{1,0:T(8,128)S(1)} custom-call(f32[72,128]{1,0:T(8,128)S(1)} %get-tuple-element.25.refs_0_.after, f32[72,128]{1,0:T(8,128)S(1)} %collective-permute-done.4.refs_1_, f32[72,128]{1,0:T(8,128)S(1)} %collective-permute-done.5.refs_2_, f32[72,128]{1,0:T(8,128)S(1)} %collective-permute-done.6.refs_3_, ...), custom_call_target="tpu_custom_call" | custom-call | tf_op jit(solution)/shard_map/pallas_call | solution.py:567
  22.6 2.2 %collective-permute-start.11 = (f32[72,128]{1,0:T(8,128)S(1)}, f32[72,128]{1,0:T(8,128)S(1)}, u32[]{:S(2)}, u32[]{:S(2)}) collective-permute-start(f32[72,128]{1,0:T(8,128)S(1)} %shard_map.49.refs_0_), channel_id=1, source_target_pairs={{0,25},{1,24},{2,27},{3,26},{4,29},{5,28},{6,31},{7,30},{8,17},{9,... | collective-permute-start | bytes 110600 | tf_op jit(solution)/shard_map/ppermute | solution.py:627
  24.8 1.7 %collective-permute-start.9 = (f32[72,128]{1,0:T(8,128)S(1)}, f32[72,128]{1,0:T(8,128)S(1)}, u32[]{:S(2)}, u32[]{:S(2)}) collective-permute-start(f32[72,128]{1,0:T(8,128)S(1)} %shard_map.49.refs_0_), channel_id=1, source_target_pairs={{0,9},{1,8},{2,11},{3,10},{4,13},{5,12},{6,15},{7,14},{8,1},{9,0},... | collective-permute-start | bytes 110600 | tf_op jit(solution)/shard_map/ppermute | solution.py:627
  26.5 0.3 collective-permute-start.16
  26.8 1.2 %collective-permute-done.11.refs_3_ = f32[72,128]{1,0:T(8,128)S(1)} collective-permute-done((f32[72,128]{1,0:T(8,128)S(1)}, f32[72,128]{1,0:T(8,128)S(1)}, u32[]{:S(2)}, u32[]{:S(2)}) %collective-permute-start.11) | collective-permute-done | bytes 36896 | tf_op jit(solution)/shard_map/ppermute | solution.py:627
  28.0 1.8 %collective-permute-done.10.refs_2_ = f32[72,128]{1,0:T(8,128)S(1)} collective-permute-done((f32[72,128]{1,0:T(8,128)S(1)}, f32[72,128]{1,0:T(8,128)S(1)}, u32[]{:S(2)}, u32[]{:S(2)}) %collective-permute-start.10) | collective-permute-done | bytes 36896 | tf_op jit(solution)/shard_map/ppermute | solution.py:627
  29.8 0.6 %shard_map.50 = (f32[72,128]{1,0:T(8,128)S(1)}, f32[72,128]{1,0:T(8,128)S(1)}) custom-call(s32[1]{0:T(128)} %bitcast.place, f32[72,128]{1,0:T(8,128)S(1)} %shard_map.49.refs_0_, f32[72,128]{1,0:T(8,128)S(1)} %collective-permute-done.9.refs_1_, f32[72,128]{1,0:T(8,128)S(1)} %collective-permute-done.10.refs_2_, f32[72,128]{1,0:T(8,128)S(1)} %collective-permute-done.11.refs_3_), custom_call_target="tpu_custom_call" | custom-call | tf_op jit(solution)/shard_map/pallas_call | solution.py:462
  30.4 1.4 %collective-permute-start.14 = (f32[72,128]{1,0:T(8,128)S(1)}, f32[72,128]{1,0:T(8,128)S(1)}, u32[]{:S(2)}, u32[]{:S(2)}) collective-permute-start(f32[72,128]{1,0:T(8,128)S(1)} %get-tuple-element.33), channel_id=1, source_target_pairs={{0,6},{1,7},{2,4},{3,5},{4,2},{5,3},{6,0},{7,1},{8,14},{9,15},{10,... | collective-permute-start | bytes 110600 | tf_op jit(solution)/shard_map/ppermute | solution.py:627
  31.9 0.2 collective-permute-start.12
  32.0 1.6 %collective-permute-start.13 = (f32[72,128]{1,0:T(8,128)S(1)}, f32[72,128]{1,0:T(8,128)S(1)}, u32[]{:S(2)}, u32[]{:S(2)}) collective-permute-start(f32[72,128]{1,0:T(8,128)S(1)} %get-tuple-element.29.after), channel_id=1, source_target_pairs={{0,3},{1,2},{2,1},{3,0},{4,7},{5,6},{6,5},{7,4},{8,11},{9,10},{10,... | collective-permute-start | bytes 110600 | tf_op jit(solution)/shard_map/ppermute | solution.py:627
  33.7 1.4 %shard_map.51 = (f32[6,16,16,128]{3,2,1,0:T(8,128)S(1)}, f32[8,128]{1,0:T(8,128)S(1)}) custom-call(s32[1]{0:T(128)} %bitcast.place, bf16[16,8,16,128]{3,2,1,0:T(8,128)(2,1)S(1)} %get-tuple-element.30.own_h, bf16[16,8,16,128]{3,2,1,0:T(8,128)(2,1)S(1)} %get-tuple-element.31.own_l, f32[416,128]{1,0:T(8,128)S(1)} %collective-permute-done.near_x.far_x.near_y, ...), custom_call_target="tpu_custom_call" | custom-call | tf_op jit(solution)/shard_map/pallas_call | solution.py:165
  35.1 0.4 %collective-permute-done.14 = f32[72,128]{1,0:T(8,128)S(1)} collective-permute-done((f32[72,128]{1,0:T(8,128)S(1)}, f32[72,128]{1,0:T(8,128)S(1)}, u32[]{:S(2)}, u32[]{:S(2)}) %collective-permute-start.14) | collective-permute-done | bytes 36896 | tf_op jit(solution)/shard_map/ppermute | solution.py:627
  35.8 0.5 %collective-permute-start.15 = (f32[288,128]{1,0:T(8,128)S(1)}, f32[288,128]{1,0:T(8,128)S(1)}, u32[]{:S(2)}, u32[]{:S(2)}) collective-permute-start(f32[288,128]{1,0:T(8,128)S(1)} %pad_maximum_fusion.own), channel_id=1, source_target_pairs={{0,1},{1,0},{2,3},{3,2},{4,5},{5,4},{6,7},{7,6},{8,9},{9,8},{10,11... | collective-permute-start | bytes 442376 | tf_op jit(solution)/shard_map/ppermute | solution.py:627
  36.2 0.8 %shard_map.53.outer = f32[2,16,16,128]{3,2,1,0:T(8,128)S(1)} custom-call(s32[1]{0:T(128)} %bitcast.place, bf16[16,8,16,128]{3,2,1,0:T(8,128)(2,1)S(1)} %get-tuple-element.30.own_h, bf16[16,8,16,128]{3,2,1,0:T(8,128)(2,1)S(1)} %get-tuple-element.31.own_l, f32[288,128]{1,0:T(8,128)S(1)} %collective-permute-done.16.near_x, ...), custom_call_target="tpu_custom_call" | custom-call | tf_op jit(solution)/shard_map/pallas_call | solution.py:165
  37.0 0.2 collective-permute-done.15.other
  37.3 2.3 %shard_map.54 = f32[128,16,128]{2,1,0:T(8,128)} custom-call(s32[1]{0:T(128)} %bitcast.place, f32[288,128]{1,0:T(8,128)S(1)} %pad_maximum_fusion.own, f32[288,128]{1,0:T(8,128)S(1)} %collective-permute-done.15.other, f32[2,16,16,128]{3,2,1,0:T(8,128)S(1)} %shard_map.53.outer, f32[6,16,16,128]{3,2,1,0:T(8,128)S(1)} %get-tuple-element.38.inner, ...), custom_call_target="tpu_custom_call" | custom-call | tf_op jit(solution)/shard_map/pallas_call | solution.py:611
  (34 shorter events, 1.1 us)
Async XLA Ops:
  0.0 1.2 %copy-start = (f32[16,8,16,128]{3,2,1,0:T(8,128)S(1)}, f32[16,8,16,128]{3,2,1,0:T(8,128)}, u32[]{:S(2)}) copy-start(f32[16,8,16,128]{3,2,1,0:T(8,128)} %param.4) | copy-start | bytes 3145732
  1.2 1.7 %copy-start.1 = (f32[2,16,16,1,216]{4,3,2,1,0:T(1,128)S(1)}, f32[2,16,16,1,216]{4,3,2,1,0:T(1,128)}, u32[]{:S(2)}) copy-start(f32[2,16,16,1,216]{4,3,2,1,0:T(1,128)} %param.6) | copy-start | bytes 1327108
  2.4 1.6 %collective-permute-start = (f32[416,128]{1,0:T(8,128)S(1)}, f32[416,128]{1,0:T(8,128)S(1)}, u32[]{:S(2)}, u32[]{:S(2)}) collective-permute-start(f32[416,128]{1,0:T(8,128)S(1)} %get-tuple-element.23), channel_id=1, source_target_pairs={{0,1},{1,0},{2,3},{3,2},{4,5},{5,4},{6,7},{7,6},{8,9},{9,8},{10,11... | collective-permute-start | bytes 638984 | tf_op jit(solution)/shard_map/ppermute | solution.py:627
  3.8 8.0 %collective-permute-start.7 = (f32[1024,128]{1,0:T(8,128)S(1)}, f32[1024,128]{1,0:T(8,128)S(1)}, u32[]{:S(2)}, u32[]{:S(2)}) collective-permute-start(f32[1024,128]{1,0:T(8,128)S(1)} %shard_map.48), channel_id=1, source_target_pairs={{0,1},{1,0},{2,3},{3,2},{4,5},{5,4},{6,7},{7,6},{8,9},{9,8},{10,11... | collective-permute-start | bytes 1572872 | tf_op jit(solution)/shard_map/ppermute | solution.py:627
  4.1 7.7 %collective-permute-start.2 = (f32[200,128]{1,0:T(8,128)S(1)}, f32[200,128]{1,0:T(8,128)S(1)}, u32[]{:S(2)}, u32[]{:S(2)}) collective-permute-start(f32[200,128]{1,0:T(8,128)S(1)} %pad_maximum_fusion.1), channel_id=1, source_target_pairs={{0,3},{1,2},{2,1},{3,0},{4,7},{5,6},{6,5},{7,4},{8,11},{9,10},{10,... | collective-permute-start | bytes 307208 | tf_op jit(solution)/shard_map/ppermute | solution.py:627
  6.8 4.9 %collective-permute-start.3 = (f32[72,128]{1,0:T(8,128)S(1)}, f32[72,128]{1,0:T(8,128)S(1)}, u32[]{:S(2)}, u32[]{:S(2)}) collective-permute-start(f32[72,128]{1,0:T(8,128)S(1)} %get-tuple-element.41), channel_id=1, source_target_pairs={{0,6},{1,7},{2,4},{3,5},{4,2},{5,3},{6,0},{7,1},{8,14},{9,15},{10,... | collective-permute-start | bytes 110600 | tf_op jit(solution)/shard_map/ppermute | solution.py:627
  8.2 3.5 %collective-permute-start.1 = (f32[72,128]{1,0:T(8,128)S(1)}, f32[72,128]{1,0:T(8,128)S(1)}, u32[]{:S(2)}, u32[]{:S(2)}) collective-permute-start(f32[72,128]{1,0:T(8,128)S(1)} %get-tuple-element.43), channel_id=1, source_target_pairs={{0,5},{1,4},{2,7},{3,6},{4,1},{5,0},{6,3},{7,2},{8,13},{9,12},{10,... | collective-permute-start | bytes 110600 | tf_op jit(solution)/shard_map/ppermute | solution.py:627
  11.8 6.1 %copy-start.3 = (f32[27,16,16]{0,2,1:T(8,128)S(1)}, f32[27,16,16]{0,2,1:T(8,128)}, u32[]{:S(2)}) copy-start(f32[27,16,16]{0,2,1:T(8,128)} %param.5) | copy-start | bytes 82948
  11.9 10.3 %collective-permute-start.8 = (f32[512,128]{1,0:T(8,128)S(1)}, f32[512,128]{1,0:T(8,128)S(1)}, u32[]{:S(2)}, u32[]{:S(2)}) collective-permute-start(f32[512,128]{1,0:T(8,128)S(1)} %get-tuple-element.39), channel_id=1, source_target_pairs={{0,5},{1,4},{2,7},{3,6},{4,1},{5,0},{6,3},{7,2},{8,13},{9,12},{10,... | collective-permute-start | bytes 786440 | tf_op jit(solution)/shard_map/ppermute | solution.py:627
  13.2 7.9 %collective-permute-start.4 = (f32[72,128]{1,0:T(8,128)S(1)}, f32[72,128]{1,0:T(8,128)S(1)}, u32[]{:S(2)}, u32[]{:S(2)}) collective-permute-start(f32[72,128]{1,0:T(8,128)S(1)} %get-tuple-element.26), channel_id=1, source_target_pairs={{0,16},{1,17},{2,18},{3,19},{4,20},{5,21},{6,22},{7,23},{8,24},{9,... | collective-permute-start | bytes 110600 | tf_op jit(solution)/shard_map/ppermute | solution.py:627
  16.0 5.3 %collective-permute-start.5 = (f32[72,128]{1,0:T(8,128)S(1)}, f32[72,128]{1,0:T(8,128)S(1)}, u32[]{:S(2)}, u32[]{:S(2)}) collective-permute-start(f32[72,128]{1,0:T(8,128)S(1)} %get-tuple-element.27), channel_id=1, source_target_pairs={{0,25},{1,24},{2,27},{3,26},{4,29},{5,28},{6,31},{7,30},{8,17},{9,... | collective-permute-start | bytes 110600 | tf_op jit(solution)/shard_map/ppermute | solution.py:627
  17.7 4.5 %collective-permute-start.6 = (f32[72,128]{1,0:T(8,128)S(1)}, f32[72,128]{1,0:T(8,128)S(1)}, u32[]{:S(2)}, u32[]{:S(2)}) collective-permute-start(f32[72,128]{1,0:T(8,128)S(1)} %get-tuple-element.28), channel_id=1, source_target_pairs={{0,9},{1,8},{2,11},{3,10},{4,13},{5,12},{6,15},{7,14},{8,1},{9,0},... | collective-permute-start | bytes 110600 | tf_op jit(solution)/shard_map/ppermute | solution.py:627
  18.4 17.8 %collective-permute-start.17 = (f32[288,128]{1,0:T(8,128)S(1)}, f32[288,128]{1,0:T(8,128)S(1)}, u32[]{:S(2)}, u32[]{:S(2)}) collective-permute-start(f32[288,128]{1,0:T(8,128)S(1)} %get-tuple-element.37), channel_id=1, source_target_pairs={{0,28},{4,8},{8,4},{12,16},{16,12},{20,24},{24,20},{28,0},{1,29},{... | collective-permute-start | bytes 442376 | tf_op jit(solution)/shard_map/ppermute | solution.py:632
  22.6 5.4 %collective-permute-start.11 = (f32[72,128]{1,0:T(8,128)S(1)}, f32[72,128]{1,0:T(8,128)S(1)}, u32[]{:S(2)}, u32[]{:S(2)}) collective-permute-start(f32[72,128]{1,0:T(8,128)S(1)} %shard_map.49.refs_0_), channel_id=1, source_target_pairs={{0,25},{1,24},{2,27},{3,26},{4,29},{5,28},{6,31},{7,30},{8,17},{9,... | collective-permute-start | bytes 110600 | tf_op jit(solution)/shard_map/ppermute | solution.py:627
  24.8 5.0 %collective-permute-start.10 = (f32[72,128]{1,0:T(8,128)S(1)}, f32[72,128]{1,0:T(8,128)S(1)}, u32[]{:S(2)}, u32[]{:S(2)}) collective-permute-start(f32[72,128]{1,0:T(8,128)S(1)} %shard_map.49.refs_0_), channel_id=1, source_target_pairs={{0,16},{1,17},{2,18},{3,19},{4,20},{5,21},{6,22},{7,23},{8,24},{9,... | collective-permute-start | bytes 110600 | tf_op jit(solution)/shard_map/ppermute | solution.py:627
  24.8 5.0 %collective-permute-start.9 = (f32[72,128]{1,0:T(8,128)S(1)}, f32[72,128]{1,0:T(8,128)S(1)}, u32[]{:S(2)}, u32[]{:S(2)}) collective-permute-start(f32[72,128]{1,0:T(8,128)S(1)} %shard_map.49.refs_0_), channel_id=1, source_target_pairs={{0,9},{1,8},{2,11},{3,10},{4,13},{5,12},{6,15},{7,14},{8,1},{9,0},... | collective-permute-start | bytes 110600 | tf_op jit(solution)/shard_map/ppermute | solution.py:627
  26.5 9.7 %collective-permute-start.16 = (f32[288,128]{1,0:T(8,128)S(1)}, f32[288,128]{1,0:T(8,128)S(1)}, u32[]{:S(2)}, u32[]{:S(2)}) collective-permute-start(f32[288,128]{1,0:T(8,128)S(1)} %broadcast_add_fusion), channel_id=1, source_target_pairs={{0,4},{1,5},{2,6},{3,7},{4,0},{5,1},{6,2},{7,3},{8,12},{9,13},{10,... | collective-permute-start | bytes 442376 | tf_op jit(solution)/shard_map/ppermute | solution.py:627
  30.4 5.1 %collective-permute-start.14 = (f32[72,128]{1,0:T(8,128)S(1)}, f32[72,128]{1,0:T(8,128)S(1)}, u32[]{:S(2)}, u32[]{:S(2)}) collective-permute-start(f32[72,128]{1,0:T(8,128)S(1)} %get-tuple-element.33), channel_id=1, source_target_pairs={{0,6},{1,7},{2,4},{3,5},{4,2},{5,3},{6,0},{7,1},{8,14},{9,15},{10,... | collective-permute-start | bytes 110600 | tf_op jit(solution)/shard_map/ppermute | solution.py:627
  31.9 3.8 %collective-permute-start.12 = (f32[72,128]{1,0:T(8,128)S(1)}, f32[72,128]{1,0:T(8,128)S(1)}, u32[]{:S(2)}, u32[]{:S(2)}) collective-permute-start(f32[72,128]{1,0:T(8,128)S(1)} %get-tuple-element.33), channel_id=1, source_target_pairs={{0,5},{1,4},{2,7},{3,6},{4,1},{5,0},{6,3},{7,2},{8,13},{9,12},{10,... | collective-permute-start | bytes 110600 | tf_op jit(solution)/shard_map/ppermute | solution.py:627
  32.0 3.7 %collective-permute-start.13 = (f32[72,128]{1,0:T(8,128)S(1)}, f32[72,128]{1,0:T(8,128)S(1)}, u32[]{:S(2)}, u32[]{:S(2)}) collective-permute-start(f32[72,128]{1,0:T(8,128)S(1)} %get-tuple-element.29.after), channel_id=1, source_target_pairs={{0,3},{1,2},{2,1},{3,0},{4,7},{5,6},{6,5},{7,4},{8,11},{9,10},{10,... | collective-permute-start | bytes 110600 | tf_op jit(solution)/shard_map/ppermute | solution.py:627
  35.7 1.5 %copy-start.2 = (bf16[384,512]{1,0:T(8,128)(2,1)S(1)}, bf16[384,512]{1,0:T(8,128)(2,1)}, u32[]{:S(2)}) copy-start(bf16[384,512]{1,0:T(8,128)(2,1)} %constant.50.clone.table_z) | copy-start | bytes 1179652
  35.8 1.5 %collective-permute-start.15 = (f32[288,128]{1,0:T(8,128)S(1)}, f32[288,128]{1,0:T(8,128)S(1)}, u32[]{:S(2)}, u32[]{:S(2)}) collective-permute-start(f32[288,128]{1,0:T(8,128)S(1)} %pad_maximum_fusion.own), channel_id=1, source_target_pairs={{0,1},{1,0},{2,3},{3,2},{4,5},{5,4},{6,7},{7,6},{8,9},{9,8},{10,11... | collective-permute-start | bytes 442376 | tf_op jit(solution)/shard_map/ppermute | solution.py:627

commit v5 on v4

--- a/solution.py
+++ b/solution.py
@@ -653,7 +653,7 @@
     far_y = swap(plan, jnp.concatenate([sums[2], far_y], axis=0), yy=1, core=1)
     from_x = swap(plan, sums[1], pair=1, core=1)
     from_xy = swap(plan, sums[3], pair=1, yy=1)
-    away = after(away, from_x, far_y, from_xy)
+    away = after(away, from_xy, far_y, from_x)
     far_weight = swap(plan, away, pair=1, core=1)
     chunks = x_forward(plan, place, [sums[0], from_x, far_y, from_xy])
     got = {s: swap(plan, chunks[s], outer=s, core=s % 2) for s in range(plan.outer - 1, 0, -1)}

time: 39.7 us -> 39.7 us (level)
  no operation moved by 1% of the time
where the time goes in v5:
time: 39.7 us; the launch traced here: 39.5 us
  starting transfers between devices  21 us (53%)
  waiting for transfers between devices  8.52 us (21%)
  Pallas kernels  8 us (20%)
  local copies, waits for them, and re-layouts  1.71 us (4%)
    ppermute x17, starting transfers between devices, swap(): return lax.ppermute(value, ('gx', 'gy'), perm)  18.2 us
    ppermute x17, waiting for transfers between devices, swap(): return lax.ppermute(value, ('gx', 'gy'), perm)  8.52 us
    ppermute x1, starting transfers between devices, next_pair(): lax.ppermute(value, axis, [(i, (i + (1 if i % 2 else -1)) % size) for i i...  2.74 us
    pallas_call x1, Pallas kernels, final_layer(): kernel_call(functools.partial(final_kernel, plan), jax.ShapeDtypeStruct(f...  2.26 us
    pallas_call x2, Pallas kernels, conv_bricks(): kernel_call(functools.partial(conv_kernel, tuple(columns), 2, lax.axis_si...  2.16 us
    unnamed x9, local copies, waits for them, and re-layouts  1.42 us
    pallas_call x1, Pallas kernels, forward_modes(): kernel_call(functools.partial(forward_kernel, plan), [shape(half, LANES),...  1.17 us
    pallas_call x1, Pallas kernels, weight_parts(): kernel_call(functools.partial(weight_kernel, plan), jax.ShapeDtypeStruct(...  0.83 us
  transfers between devices with their start and end apart: 18, of which 11 were waited for; matrix products, arithmetic and copies ran while one was open for 1% of the time, Pallas kernels for 12%

profile of v5, /device:TPU:0, one launch (start us, length us, event | category | flops | bytes accessed | tf_op | source)
XLA Modules:
  0.0 39.5 jit_solution(16896346996219808275)
XLA Ops:
  0.0 1.2 %copy-done = f32[16,8,16,128]{3,2,1,0:T(8,128)S(1)} copy-done((f32[16,8,16,128]{3,2,1,0:T(8,128)S(1)}, f32[16,8,16,128]{3,2,1,0:T(8,128)}, u32[]{:S(2)}) %copy-start) | copy-done | bytes 1048600
  1.2 1.2 %shard_map.46 = (f32[288,128]{1,0:T(8,128)S(1)}, f32[416,128]{1,0:T(8,128)S(1)}, bf16[16,8,16,128]{3,2,1,0:T(8,128)(2,1)S(1)}, bf16[16,8,16,128]{3,2,1,0:T(8,128...) custom-call(s32[1]{0:T(128)} %bitcast.place, f32[2048,128]{1,0:T(8,128)S(1)} %bitcast.13), custom_call_target="tpu_custom_call" | custom-call | tf_op jit(solution)/shard_map/pallas_call | solution.py:392
  2.4 0.5 %collective-permute-start = (f32[416,128]{1,0:T(8,128)S(1)}, f32[416,128]{1,0:T(8,128)S(1)}, u32[]{:S(2)}, u32[]{:S(2)}) collective-permute-start(f32[416,128]{1,0:T(8,128)S(1)} %get-tuple-element.23), channel_id=1, source_target_pairs={{0,1},{1,0},{2,3},{3,2},{4,5},{5,4},{6,7},{7,6},{8,9},{9,8},{10,11... | collective-permute-start | bytes 638984 | tf_op jit(solution)/shard_map/ppermute | solution.py:627
  2.9 0.8 %shard_map.48 = f32[1024,128]{1,0:T(8,128)S(1)} custom-call(s32[1]{0:T(128)} %bitcast.place, f32[2,256,1,216]{3,2,1,0:T(1,128)S(1)} %bitcast.14), custom_call_target="tpu_custom_call" | custom-call | tf_op jit(solution)/shard_map/pallas_call | solution.py:495
  4.1 2.7 %collective-permute-start.2 = (f32[200,128]{1,0:T(8,128)S(1)}, f32[200,128]{1,0:T(8,128)S(1)}, u32[]{:S(2)}, u32[]{:S(2)}) collective-permute-start(f32[200,128]{1,0:T(8,128)S(1)} %pad_maximum_fusion.1), channel_id=1, source_target_pairs={{0,3},{1,2},{2,1},{3,0},{4,7},{5,6},{6,5},{7,4},{8,11},{9,10},{10,... | collective-permute-start | bytes 307208 | tf_op jit(solution)/shard_map/ppermute | solution.py:627
  6.8 1.4 %collective-permute-start.3 = (f32[72,128]{1,0:T(8,128)S(1)}, f32[72,128]{1,0:T(8,128)S(1)}, u32[]{:S(2)}, u32[]{:S(2)}) collective-permute-start(f32[72,128]{1,0:T(8,128)S(1)} %get-tuple-element.41), channel_id=1, source_target_pairs={{0,6},{1,7},{2,4},{3,5},{4,2},{5,3},{6,0},{7,1},{8,14},{9,15},{10,... | collective-permute-start | bytes 110600 | tf_op jit(solution)/shard_map/ppermute | solution.py:627
  8.2 3.4 %collective-permute-done.3.from_xy = f32[72,128]{1,0:T(8,128)S(1)} collective-permute-done((f32[72,128]{1,0:T(8,128)S(1)}, f32[72,128]{1,0:T(8,128)S(1)}, u32[]{:S(2)}, u32[]{:S(2)}) %collective-permute-start.3) | collective-permute-done | bytes 36896 | tf_op jit(solution)/shard_map/ppermute | solution.py:627
  11.9 0.8 %collective-permute-start.8 = (f32[512,128]{1,0:T(8,128)S(1)}, f32[512,128]{1,0:T(8,128)S(1)}, u32[]{:S(2)}, u32[]{:S(2)}) collective-permute-start(f32[512,128]{1,0:T(8,128)S(1)} %get-tuple-element.39), channel_id=1, source_target_pairs={{0,5},{1,4},{2,7},{3,6},{4,1},{5,0},{6,3},{7,2},{8,13},{9,12},{10,... | collective-permute-start | bytes 786440 | tf_op jit(solution)/shard_map/ppermute | solution.py:627
  12.7 0.5 %shard_map.47 = (f32[72,128]{1,0:T(8,128)S(1)}, f32[72,128]{1,0:T(8,128)S(1)}, f32[72,128]{1,0:T(8,128)S(1)}, f32[72,128]{1,0:T(8,128)S(1)}) custom-call(s32[1]{0:T(128)} %bitcast.place, f32[72,128]{1,0:T(8,128)S(1)} %get-tuple-element.44.own, f32[72,128]{1,0:T(8,128)S(1)} %collective-permute-done.1.from_x, ...), custom_call_target="tpu_custom_call" | custom-call | tf_op jit(solution)/shard_map/pallas_call | solution.py:454
  13.2 2.8 %collective-permute-start.4 = (f32[72,128]{1,0:T(8,128)S(1)}, f32[72,128]{1,0:T(8,128)S(1)}, u32[]{:S(2)}, u32[]{:S(2)}) collective-permute-start(f32[72,128]{1,0:T(8,128)S(1)} %get-tuple-element.26), channel_id=1, source_target_pairs={{0,16},{1,17},{2,18},{3,19},{4,20},{5,21},{6,22},{7,23},{8,24},{9,... | collective-permute-start | bytes 110600 | tf_op jit(solution)/shard_map/ppermute | solution.py:627
  16.0 1.7 %collective-permute-start.5 = (f32[72,128]{1,0:T(8,128)S(1)}, f32[72,128]{1,0:T(8,128)S(1)}, u32[]{:S(2)}, u32[]{:S(2)}) collective-permute-start(f32[72,128]{1,0:T(8,128)S(1)} %get-tuple-element.27), channel_id=1, source_target_pairs={{0,25},{1,24},{2,27},{3,26},{4,29},{5,28},{6,31},{7,30},{8,17},{9,... | collective-permute-start | bytes 110600 | tf_op jit(solution)/shard_map/ppermute | solution.py:627
  17.7 0.2 collective-permute-start.6
  17.9 0.2 copy.6
  18.4 2.7 %collective-permute-start.17 = (f32[288,128]{1,0:T(8,128)S(1)}, f32[288,128]{1,0:T(8,128)S(1)}, u32[]{:S(2)}, u32[]{:S(2)}) collective-permute-start(f32[288,128]{1,0:T(8,128)S(1)} %get-tuple-element.37), channel_id=1, source_target_pairs={{0,28},{4,8},{8,4},{12,16},{16,12},{20,24},{24,20},{28,0},{1,29},{... | collective-permute-start | bytes 442376 | tf_op jit(solution)/shard_map/ppermute | solution.py:632
  21.1 0.2 collective-permute-done.5.refs_2_
  21.3 0.8 %collective-permute-done.6.refs_3_ = f32[72,128]{1,0:T(8,128)S(1)} collective-permute-done((f32[72,128]{1,0:T(8,128)S(1)}, f32[72,128]{1,0:T(8,128)S(1)}, u32[]{:S(2)}, u32[]{:S(2)}) %collective-permute-start.6) | collective-permute-done | bytes 36896 | tf_op jit(solution)/shard_map/ppermute | solution.py:627
  22.1 0.4 %shard_map.49.refs_0_ = f32[72,128]{1,0:T(8,128)S(1)} custom-call(f32[72,128]{1,0:T(8,128)S(1)} %get-tuple-element.25.refs_0_.after, f32[72,128]{1,0:T(8,128)S(1)} %collective-permute-done.4.refs_1_, f32[72,128]{1,0:T(8,128)S(1)} %collective-permute-done.5.refs_2_, f32[72,128]{1,0:T(8,128)S(1)} %collective-permute-done.6.refs_3_, ...), custom_call_target="tpu_custom_call" | custom-call | tf_op jit(solution)/shard_map/pallas_call | solution.py:567
  22.6 2.2 %collective-permute-start.11 = (f32[72,128]{1,0:T(8,128)S(1)}, f32[72,128]{1,0:T(8,128)S(1)}, u32[]{:S(2)}, u32[]{:S(2)}) collective-permute-start(f32[72,128]{1,0:T(8,128)S(1)} %shard_map.49.refs_0_), channel_id=1, source_target_pairs={{0,25},{1,24},{2,27},{3,26},{4,29},{5,28},{6,31},{7,30},{8,17},{9,... | collective-permute-start | bytes 110600 | tf_op jit(solution)/shard_map/ppermute | solution.py:627
  24.8 1.7 %collective-permute-start.9 = (f32[72,128]{1,0:T(8,128)S(1)}, f32[72,128]{1,0:T(8,128)S(1)}, u32[]{:S(2)}, u32[]{:S(2)}) collective-permute-start(f32[72,128]{1,0:T(8,128)S(1)} %shard_map.49.refs_0_), channel_id=1, source_target_pairs={{0,9},{1,8},{2,11},{3,10},{4,13},{5,12},{6,15},{7,14},{8,1},{9,0},... | collective-permute-start | bytes 110600 | tf_op jit(solution)/shard_map/ppermute | solution.py:627
  26.5 0.3 collective-permute-start.16
  26.8 1.2 %collective-permute-done.11.refs_3_ = f32[72,128]{1,0:T(8,128)S(1)} collective-permute-done((f32[72,128]{1,0:T(8,128)S(1)}, f32[72,128]{1,0:T(8,128)S(1)}, u32[]{:S(2)}, u32[]{:S(2)}) %collective-permute-start.11) | collective-permute-done | bytes 36896 | tf_op jit(solution)/shard_map/ppermute | solution.py:627
  28.0 1.8 %collective-permute-done.10.refs_2_ = f32[72,128]{1,0:T(8,128)S(1)} collective-permute-done((f32[72,128]{1,0:T(8,128)S(1)}, f32[72,128]{1,0:T(8,128)S(1)}, u32[]{:S(2)}, u32[]{:S(2)}) %collective-permute-start.10) | collective-permute-done | bytes 36896 | tf_op jit(solution)/shard_map/ppermute | solution.py:627
  29.8 0.6 %shard_map.50 = (f32[72,128]{1,0:T(8,128)S(1)}, f32[72,128]{1,0:T(8,128)S(1)}) custom-call(s32[1]{0:T(128)} %bitcast.place, f32[72,128]{1,0:T(8,128)S(1)} %shard_map.49.refs_0_, f32[72,128]{1,0:T(8,128)S(1)} %collective-permute-done.9.refs_1_, f32[72,128]{1,0:T(8,128)S(1)} %collective-permute-done.10.refs_2_, f32[72,128]{1,0:T(8,128)S(1)} %collective-permute-done.11.refs_3_), custom_call_target="tpu_custom_call" | custom-call | tf_op jit(solution)/shard_map/pallas_call | solution.py:462
  30.4 1.4 %collective-permute-start.14 = (f32[72,128]{1,0:T(8,128)S(1)}, f32[72,128]{1,0:T(8,128)S(1)}, u32[]{:S(2)}, u32[]{:S(2)}) collective-permute-start(f32[72,128]{1,0:T(8,128)S(1)} %get-tuple-element.33), channel_id=1, source_target_pairs={{0,6},{1,7},{2,4},{3,5},{4,2},{5,3},{6,0},{7,1},{8,14},{9,15},{10,... | collective-permute-start | bytes 110600 | tf_op jit(solution)/shard_map/ppermute | solution.py:627
  31.9 0.2 collective-permute-start.12
  32.0 1.6 %collective-permute-start.13 = (f32[72,128]{1,0:T(8,128)S(1)}, f32[72,128]{1,0:T(8,128)S(1)}, u32[]{:S(2)}, u32[]{:S(2)}) collective-permute-start(f32[72,128]{1,0:T(8,128)S(1)} %get-tuple-element.29.after), channel_id=1, source_target_pairs={{0,3},{1,2},{2,1},{3,0},{4,7},{5,6},{6,5},{7,4},{8,11},{9,10},{10,... | collective-permute-start | bytes 110600 | tf_op jit(solution)/shard_map/ppermute | solution.py:627
  33.7 1.4 %shard_map.51 = (f32[6,16,16,128]{3,2,1,0:T(8,128)S(1)}, f32[8,128]{1,0:T(8,128)S(1)}) custom-call(s32[1]{0:T(128)} %bitcast.place, bf16[16,8,16,128]{3,2,1,0:T(8,128)(2,1)S(1)} %get-tuple-element.30.own_h, bf16[16,8,16,128]{3,2,1,0:T(8,128)(2,1)S(1)} %get-tuple-element.31.own_l, f32[416,128]{1,0:T(8,128)S(1)} %collective-permute-done.near_x.far_x.near_y, ...), custom_call_target="tpu_custom_call" | custom-call | tf_op jit(solution)/shard_map/pallas_call | solution.py:165
  35.1 0.4 %collective-permute-done.14 = f32[72,128]{1,0:T(8,128)S(1)} collective-permute-done((f32[72,128]{1,0:T(8,128)S(1)}, f32[72,128]{1,0:T(8,128)S(1)}, u32[]{:S(2)}, u32[]{:S(2)}) %collective-permute-start.14) | collective-permute-done | bytes 36896 | tf_op jit(solution)/shard_map/ppermute | solution.py:627
  35.8 0.5 %collective-permute-start.15 = (f32[288,128]{1,0:T(8,128)S(1)}, f32[288,128]{1,0:T(8,128)S(1)}, u32[]{:S(2)}, u32[]{:S(2)}) collective-permute-start(f32[288,128]{1,0:T(8,128)S(1)} %pad_maximum_fusion.own), channel_id=1, source_target_pairs={{0,1},{1,0},{2,3},{3,2},{4,5},{5,4},{6,7},{7,6},{8,9},{9,8},{10,11... | collective-permute-start | bytes 442376 | tf_op jit(solution)/shard_map/ppermute | solution.py:627
  36.2 0.8 %shard_map.53.outer = f32[2,16,16,128]{3,2,1,0:T(8,128)S(1)} custom-call(s32[1]{0:T(128)} %bitcast.place, bf16[16,8,16,128]{3,2,1,0:T(8,128)(2,1)S(1)} %get-tuple-element.30.own_h, bf16[16,8,16,128]{3,2,1,0:T(8,128)(2,1)S(1)} %get-tuple-element.31.own_l, f32[288,128]{1,0:T(8,128)S(1)} %collective-permute-done.16.near_x, ...), custom_call_target="tpu_custom_call" | custom-call | tf_op jit(solution)/shard_map/pallas_call | solution.py:165
  37.0 0.2 collective-permute-done.15.other
  37.3 2.3 %shard_map.54 = f32[128,16,128]{2,1,0:T(8,128)} custom-call(s32[1]{0:T(128)} %bitcast.place, f32[288,128]{1,0:T(8,128)S(1)} %pad_maximum_fusion.own, f32[288,128]{1,0:T(8,128)S(1)} %collective-permute-done.15.other, f32[2,16,16,128]{3,2,1,0:T(8,128)S(1)} %shard_map.53.outer, f32[6,16,16,128]{3,2,1,0:T(8,128)S(1)} %get-tuple-element.38.inner, ...), custom_call_target="tpu_custom_call" | custom-call | tf_op jit(solution)/shard_map/pallas_call | solution.py:611
  (34 shorter events, 1.1 us)
Async XLA Ops:
  0.0 1.2 %copy-start = (f32[16,8,16,128]{3,2,1,0:T(8,128)S(1)}, f32[16,8,16,128]{3,2,1,0:T(8,128)}, u32[]{:S(2)}) copy-start(f32[16,8,16,128]{3,2,1,0:T(8,128)} %param.4) | copy-start | bytes 3145732
  1.2 1.7 %copy-start.1 = (f32[2,16,16,1,216]{4,3,2,1,0:T(1,128)S(1)}, f32[2,16,16,1,216]{4,3,2,1,0:T(1,128)}, u32[]{:S(2)}) copy-start(f32[2,16,16,1,216]{4,3,2,1,0:T(1,128)} %param.6) | copy-start | bytes 1327108
  2.4 1.6 %collective-permute-start = (f32[416,128]{1,0:T(8,128)S(1)}, f32[416,128]{1,0:T(8,128)S(1)}, u32[]{:S(2)}, u32[]{:S(2)}) collective-permute-start(f32[416,128]{1,0:T(8,128)S(1)} %get-tuple-element.23), channel_id=1, source_target_pairs={{0,1},{1,0},{2,3},{3,2},{4,5},{5,4},{6,7},{7,6},{8,9},{9,8},{10,11... | collective-permute-start | bytes 638984 | tf_op jit(solution)/shard_map/ppermute | solution.py:627
  3.8 8.0 %collective-permute-start.7 = (f32[1024,128]{1,0:T(8,128)S(1)}, f32[1024,128]{1,0:T(8,128)S(1)}, u32[]{:S(2)}, u32[]{:S(2)}) collective-permute-start(f32[1024,128]{1,0:T(8,128)S(1)} %shard_map.48), channel_id=1, source_target_pairs={{0,1},{1,0},{2,3},{3,2},{4,5},{5,4},{6,7},{7,6},{8,9},{9,8},{10,11... | collective-permute-start | bytes 1572872 | tf_op jit(solution)/shard_map/ppermute | solution.py:627
  4.1 7.7 %collective-permute-start.2 = (f32[200,128]{1,0:T(8,128)S(1)}, f32[200,128]{1,0:T(8,128)S(1)}, u32[]{:S(2)}, u32[]{:S(2)}) collective-permute-start(f32[200,128]{1,0:T(8,128)S(1)} %pad_maximum_fusion.1), channel_id=1, source_target_pairs={{0,3},{1,2},{2,1},{3,0},{4,7},{5,6},{6,5},{7,4},{8,11},{9,10},{10,... | collective-permute-start | bytes 307208 | tf_op jit(solution)/shard_map/ppermute | solution.py:627
  6.8 4.9 %collective-permute-start.3 = (f32[72,128]{1,0:T(8,128)S(1)}, f32[72,128]{1,0:T(8,128)S(1)}, u32[]{:S(2)}, u32[]{:S(2)}) collective-permute-start(f32[72,128]{1,0:T(8,128)S(1)} %get-tuple-element.41), channel_id=1, source_target_pairs={{0,6},{1,7},{2,4},{3,5},{4,2},{5,3},{6,0},{7,1},{8,14},{9,15},{10,... | collective-permute-start | bytes 110600 | tf_op jit(solution)/shard_map/ppermute | solution.py:627
  8.2 3.5 %collective-permute-start.1 = (f32[72,128]{1,0:T(8,128)S(1)}, f32[72,128]{1,0:T(8,128)S(1)}, u32[]{:S(2)}, u32[]{:S(2)}) collective-permute-start(f32[72,128]{1,0:T(8,128)S(1)} %get-tuple-element.43), channel_id=1, source_target_pairs={{0,5},{1,4},{2,7},{3,6},{4,1},{5,0},{6,3},{7,2},{8,13},{9,12},{10,... | collective-permute-start | bytes 110600 | tf_op jit(solution)/shard_map/ppermute | solution.py:627
  11.8 6.1 %copy-start.3 = (f32[27,16,16]{0,2,1:T(8,128)S(1)}, f32[27,16,16]{0,2,1:T(8,128)}, u32[]{:S(2)}) copy-start(f32[27,16,16]{0,2,1:T(8,128)} %param.5) | copy-start | bytes 82948
  11.9 10.3 %collective-permute-start.8 = (f32[512,128]{1,0:T(8,128)S(1)}, f32[512,128]{1,0:T(8,128)S(1)}, u32[]{:S(2)}, u32[]{:S(2)}) collective-permute-start(f32[512,128]{1,0:T(8,128)S(1)} %get-tuple-element.39), channel_id=1, source_target_pairs={{0,5},{1,4},{2,7},{3,6},{4,1},{5,0},{6,3},{7,2},{8,13},{9,12},{10,... | collective-permute-start | bytes 786440 | tf_op jit(solution)/shard_map/ppermute | solution.py:627
  13.2 7.9 %collective-permute-start.4 = (f32[72,128]{1,0:T(8,128)S(1)}, f32[72,128]{1,0:T(8,128)S(1)}, u32[]{:S(2)}, u32[]{:S(2)}) collective-permute-start(f32[72,128]{1,0:T(8,128)S(1)} %get-tuple-element.26), channel_id=1, source_target_pairs={{0,16},{1,17},{2,18},{3,19},{4,20},{5,21},{6,22},{7,23},{8,24},{9,... | collective-permute-start | bytes 110600 | tf_op jit(solution)/shard_map/ppermute | solution.py:627
  16.0 5.3 %collective-permute-start.5 = (f32[72,128]{1,0:T(8,128)S(1)}, f32[72,128]{1,0:T(8,128)S(1)}, u32[]{:S(2)}, u32[]{:S(2)}) collective-permute-start(f32[72,128]{1,0:T(8,128)S(1)} %get-tuple-element.27), channel_id=1, source_target_pairs={{0,25},{1,24},{2,27},{3,26},{4,29},{5,28},{6,31},{7,30},{8,17},{9,... | collective-permute-start | bytes 110600 | tf_op jit(solution)/shard_map/ppermute | solution.py:627
  17.7 4.5 %collective-permute-start.6 = (f32[72,128]{1,0:T(8,128)S(1)}, f32[72,128]{1,0:T(8,128)S(1)}, u32[]{:S(2)}, u32[]{:S(2)}) collective-permute-start(f32[72,128]{1,0:T(8,128)S(1)} %get-tuple-element.28), channel_id=1, source_target_pairs={{0,9},{1,8},{2,11},{3,10},{4,13},{5,12},{6,15},{7,14},{8,1},{9,0},... | collective-permute-start | bytes 110600 | tf_op jit(solution)/shard_map/ppermute | solution.py:627
  18.4 17.8 %collective-permute-start.17 = (f32[288,128]{1,0:T(8,128)S(1)}, f32[288,128]{1,0:T(8,128)S(1)}, u32[]{:S(2)}, u32[]{:S(2)}) collective-permute-start(f32[288,128]{1,0:T(8,128)S(1)} %get-tuple-element.37), channel_id=1, source_target_pairs={{0,28},{4,8},{8,4},{12,16},{16,12},{20,24},{24,20},{28,0},{1,29},{... | collective-permute-start | bytes 442376 | tf_op jit(solution)/shard_map/ppermute | solution.py:632
  22.6 5.4 %collective-permute-start.11 = (f32[72,128]{1,0:T(8,128)S(1)}, f32[72,128]{1,0:T(8,128)S(1)}, u32[]{:S(2)}, u32[]{:S(2)}) collective-permute-start(f32[72,128]{1,0:T(8,128)S(1)} %shard_map.49.refs_0_), channel_id=1, source_target_pairs={{0,25},{1,24},{2,27},{3,26},{4,29},{5,28},{6,31},{7,30},{8,17},{9,... | collective-permute-start | bytes 110600 | tf_op jit(solution)/shard_map/ppermute | solution.py:627
  24.8 5.0 %collective-permute-start.10 = (f32[72,128]{1,0:T(8,128)S(1)}, f32[72,128]{1,0:T(8,128)S(1)}, u32[]{:S(2)}, u32[]{:S(2)}) collective-permute-start(f32[72,128]{1,0:T(8,128)S(1)} %shard_map.49.refs_0_), channel_id=1, source_target_pairs={{0,16},{1,17},{2,18},{3,19},{4,20},{5,21},{6,22},{7,23},{8,24},{9,... | collective-permute-start | bytes 110600 | tf_op jit(solution)/shard_map/ppermute | solution.py:627
  24.8 5.0 %collective-permute-start.9 = (f32[72,128]{1,0:T(8,128)S(1)}, f32[72,128]{1,0:T(8,128)S(1)}, u32[]{:S(2)}, u32[]{:S(2)}) collective-permute-start(f32[72,128]{1,0:T(8,128)S(1)} %shard_map.49.refs_0_), channel_id=1, source_target_pairs={{0,9},{1,8},{2,11},{3,10},{4,13},{5,12},{6,15},{7,14},{8,1},{9,0},... | collective-permute-start | bytes 110600 | tf_op jit(solution)/shard_map/ppermute | solution.py:627
  26.5 9.7 %collective-permute-start.16 = (f32[288,128]{1,0:T(8,128)S(1)}, f32[288,128]{1,0:T(8,128)S(1)}, u32[]{:S(2)}, u32[]{:S(2)}) collective-permute-start(f32[288,128]{1,0:T(8,128)S(1)} %broadcast_add_fusion), channel_id=1, source_target_pairs={{0,4},{1,5},{2,6},{3,7},{4,0},{5,1},{6,2},{7,3},{8,12},{9,13},{10,... | collective-permute-start | bytes 442376 | tf_op jit(solution)/shard_map/ppermute | solution.py:627
  30.4 5.1 %collective-permute-start.14 = (f32[72,128]{1,0:T(8,128)S(1)}, f32[72,128]{1,0:T(8,128)S(1)}, u32[]{:S(2)}, u32[]{:S(2)}) collective-permute-start(f32[72,128]{1,0:T(8,128)S(1)} %get-tuple-element.33), channel_id=1, source_target_pairs={{0,6},{1,7},{2,4},{3,5},{4,2},{5,3},{6,0},{7,1},{8,14},{9,15},{10,... | collective-permute-start | bytes 110600 | tf_op jit(solution)/shard_map/ppermute | solution.py:627
  31.9 3.8 %collective-permute-start.12 = (f32[72,128]{1,0:T(8,128)S(1)}, f32[72,128]{1,0:T(8,128)S(1)}, u32[]{:S(2)}, u32[]{:S(2)}) collective-permute-start(f32[72,128]{1,0:T(8,128)S(1)} %get-tuple-element.33), channel_id=1, source_target_pairs={{0,5},{1,4},{2,7},{3,6},{4,1},{5,0},{6,3},{7,2},{8,13},{9,12},{10,... | collective-permute-start | bytes 110600 | tf_op jit(solution)/shard_map/ppermute | solution.py:627
  32.0 3.7 %collective-permute-start.13 = (f32[72,128]{1,0:T(8,128)S(1)}, f32[72,128]{1,0:T(8,128)S(1)}, u32[]{:S(2)}, u32[]{:S(2)}) collective-permute-start(f32[72,128]{1,0:T(8,128)S(1)} %get-tuple-element.29.after), channel_id=1, source_target_pairs={{0,3},{1,2},{2,1},{3,0},{4,7},{5,6},{6,5},{7,4},{8,11},{9,10},{10,... | collective-permute-start | bytes 110600 | tf_op jit(solution)/shard_map/ppermute | solution.py:627
  35.7 1.5 %copy-start.2 = (bf16[384,512]{1,0:T(8,128)(2,1)S(1)}, bf16[384,512]{1,0:T(8,128)(2,1)}, u32[]{:S(2)}) copy-start(bf16[384,512]{1,0:T(8,128)(2,1)} %constant.50.clone.table_z) | copy-start | bytes 1179652
  35.8 1.5 %collective-permute-start.15 = (f32[288,128]{1,0:T(8,128)S(1)}, f32[288,128]{1,0:T(8,128)S(1)}, u32[]{:S(2)}, u32[]{:S(2)}) collective-permute-start(f32[288,128]{1,0:T(8,128)S(1)} %pad_maximum_fusion.own), channel_id=1, source_target_pairs={{0,1},{1,0},{2,3},{3,2},{4,5},{5,4},{6,7},{7,6},{8,9},{9,8},{10,11... | collective-permute-start | bytes 442376 | tf_op jit(solution)/shard_map/ppermute | solution.py:627

commit v6 on v4

--- a/solution.py
+++ b/solution.py
@@ -280,6 +280,7 @@
         return (
             length_z == LANES
             and cells_x >= 4
+            and cells_y % 8 == 0
             and cells_x % 2 == 0
             and cells_y % (LANES // (2 * (-(-KZ // 8) * 8))) == 0
             and channels % 16 == 0
@@ -585,8 +586,10 @@
     z_table = table_z[...]
     group = LANES // plan.pad_z
     for g in range(cells_y // group):
-        planes = halves(field[g * LANES : (g + 1) * LANES, :].T)
-        value = dot(triple(planes, 1, False), z_table)
+        if g % 2 == 0:
+            planes = halves(jnp.concatenate([field[n * LANES : (n + 1) * LANES, :].T for n in (g, g + 1)], axis=0))
+            both = dot(triple(planes, 1, False), z_table)
+        value = both[(g % 2) * LANES : (g % 2 + 1) * LANES]
         for k in range(group):
             y = g * group + k
             conv = [outer[0, y]] + [inner[x, y] for x in range(inner.shape[0])] + [outer[1, y]]

time: 39.7 us -> 39.7 us (level)
  no operation moved by 1% of the time
where the time goes in v6:
time: 39.7 us; the launch traced here: 39.5 us
  starting transfers between devices  21 us (53%)
  waiting for transfers between devices  8.52 us (21%)
  Pallas kernels  7.99 us (20%)
  local copies, waits for them, and re-layouts  1.71 us (4%)
    ppermute x17, starting transfers between devices, swap(): return lax.ppermute(value, ('gx', 'gy'), perm)  18.2 us
    ppermute x17, waiting for transfers between devices, swap(): return lax.ppermute(value, ('gx', 'gy'), perm)  8.52 us
    ppermute x1, starting transfers between devices, next_pair(): lax.ppermute(value, axis, [(i, (i + (1 if i % 2 else -1)) % size) for i i...  2.74 us
    pallas_call x1, Pallas kernels, final_layer(): kernel_call(functools.partial(final_kernel, plan), jax.ShapeDtypeStruct(f...  2.25 us
    pallas_call x2, Pallas kernels, conv_bricks(): kernel_call(functools.partial(conv_kernel, tuple(columns), 2, lax.axis_si...  2.16 us
    unnamed x9, local copies, waits for them, and re-layouts  1.42 us
    pallas_call x1, Pallas kernels, forward_modes(): kernel_call(functools.partial(forward_kernel, plan), [shape(half, LANES),...  1.17 us
    pallas_call x1, Pallas kernels, weight_parts(): kernel_call(functools.partial(weight_kernel, plan), jax.ShapeDtypeStruct(...  0.83 us
  transfers between devices with their start and end apart: 18, of which 11 were waited for; matrix products, arithmetic and copies ran while one was open for 1% of the time, Pallas kernels for 12%

profile of v6, /device:TPU:0, one launch (start us, length us, event | category | flops | bytes accessed | tf_op | source)
XLA Modules:
  0.0 39.5 jit_solution(9190612324468072343)
XLA Ops:
  0.0 1.2 %copy-done = f32[16,8,16,128]{3,2,1,0:T(8,128)S(1)} copy-done((f32[16,8,16,128]{3,2,1,0:T(8,128)S(1)}, f32[16,8,16,128]{3,2,1,0:T(8,128)}, u32[]{:S(2)}) %copy-start) | copy-done | bytes 1048600
  1.2 1.2 %shard_map.46 = (f32[288,128]{1,0:T(8,128)S(1)}, f32[416,128]{1,0:T(8,128)S(1)}, bf16[16,8,16,128]{3,2,1,0:T(8,128)(2,1)S(1)}, bf16[16,8,16,128]{3,2,1,0:T(8,128...) custom-call(s32[1]{0:T(128)} %bitcast.place, f32[2048,128]{1,0:T(8,128)S(1)} %bitcast.13), custom_call_target="tpu_custom_call" | custom-call | tf_op jit(solution)/shard_map/pallas_call | solution.py:393
  2.4 0.5 %collective-permute-start = (f32[416,128]{1,0:T(8,128)S(1)}, f32[416,128]{1,0:T(8,128)S(1)}, u32[]{:S(2)}, u32[]{:S(2)}) collective-permute-start(f32[416,128]{1,0:T(8,128)S(1)} %get-tuple-element.23), channel_id=1, source_target_pairs={{0,1},{1,0},{2,3},{3,2},{4,5},{5,4},{6,7},{7,6},{8,9},{9,8},{10,11... | collective-permute-start | bytes 638984 | tf_op jit(solution)/shard_map/ppermute | solution.py:630
  2.9 0.8 %shard_map.48 = f32[1024,128]{1,0:T(8,128)S(1)} custom-call(s32[1]{0:T(128)} %bitcast.place, f32[2,256,1,216]{3,2,1,0:T(1,128)S(1)} %bitcast.14), custom_call_target="tpu_custom_call" | custom-call | tf_op jit(solution)/shard_map/pallas_call | solution.py:496
  4.1 2.7 %collective-permute-start.2 = (f32[200,128]{1,0:T(8,128)S(1)}, f32[200,128]{1,0:T(8,128)S(1)}, u32[]{:S(2)}, u32[]{:S(2)}) collective-permute-start(f32[200,128]{1,0:T(8,128)S(1)} %pad_maximum_fusion.1), channel_id=1, source_target_pairs={{0,3},{1,2},{2,1},{3,0},{4,7},{5,6},{6,5},{7,4},{8,11},{9,10},{10,... | collective-permute-start | bytes 307208 | tf_op jit(solution)/shard_map/ppermute | solution.py:630
  6.8 1.4 %collective-permute-start.3 = (f32[72,128]{1,0:T(8,128)S(1)}, f32[72,128]{1,0:T(8,128)S(1)}, u32[]{:S(2)}, u32[]{:S(2)}) collective-permute-start(f32[72,128]{1,0:T(8,128)S(1)} %get-tuple-element.41), channel_id=1, source_target_pairs={{0,6},{1,7},{2,4},{3,5},{4,2},{5,3},{6,0},{7,1},{8,14},{9,15},{10,... | collective-permute-start | bytes 110600 | tf_op jit(solution)/shard_map/ppermute | solution.py:630
  8.2 3.4 %collective-permute-done.3.from_xy = f32[72,128]{1,0:T(8,128)S(1)} collective-permute-done((f32[72,128]{1,0:T(8,128)S(1)}, f32[72,128]{1,0:T(8,128)S(1)}, u32[]{:S(2)}, u32[]{:S(2)}) %collective-permute-start.3) | collective-permute-done | bytes 36896 | tf_op jit(solution)/shard_map/ppermute | solution.py:630
  11.9 0.8 %collective-permute-start.8 = (f32[512,128]{1,0:T(8,128)S(1)}, f32[512,128]{1,0:T(8,128)S(1)}, u32[]{:S(2)}, u32[]{:S(2)}) collective-permute-start(f32[512,128]{1,0:T(8,128)S(1)} %get-tuple-element.39), channel_id=1, source_target_pairs={{0,5},{1,4},{2,7},{3,6},{4,1},{5,0},{6,3},{7,2},{8,13},{9,12},{10,... | collective-permute-start | bytes 786440 | tf_op jit(solution)/shard_map/ppermute | solution.py:630
  12.7 0.5 %shard_map.47 = (f32[72,128]{1,0:T(8,128)S(1)}, f32[72,128]{1,0:T(8,128)S(1)}, f32[72,128]{1,0:T(8,128)S(1)}, f32[72,128]{1,0:T(8,128)S(1)}) custom-call(s32[1]{0:T(128)} %bitcast.place, f32[72,128]{1,0:T(8,128)S(1)} %get-tuple-element.44.own, f32[72,128]{1,0:T(8,128)S(1)} %collective-permute-done.1.from_x, ...), custom_call_target="tpu_custom_call" | custom-call | tf_op jit(solution)/shard_map/pallas_call | solution.py:455
  13.2 2.8 %collective-permute-start.4 = (f32[72,128]{1,0:T(8,128)S(1)}, f32[72,128]{1,0:T(8,128)S(1)}, u32[]{:S(2)}, u32[]{:S(2)}) collective-permute-start(f32[72,128]{1,0:T(8,128)S(1)} %get-tuple-element.26), channel_id=1, source_target_pairs={{0,16},{1,17},{2,18},{3,19},{4,20},{5,21},{6,22},{7,23},{8,24},{9,... | collective-permute-start | bytes 110600 | tf_op jit(solution)/shard_map/ppermute | solution.py:630
  16.0 1.7 %collective-permute-start.5 = (f32[72,128]{1,0:T(8,128)S(1)}, f32[72,128]{1,0:T(8,128)S(1)}, u32[]{:S(2)}, u32[]{:S(2)}) collective-permute-start(f32[72,128]{1,0:T(8,128)S(1)} %get-tuple-element.27), channel_id=1, source_target_pairs={{0,25},{1,24},{2,27},{3,26},{4,29},{5,28},{6,31},{7,30},{8,17},{9,... | collective-permute-start | bytes 110600 | tf_op jit(solution)/shard_map/ppermute | solution.py:630
  17.7 0.2 collective-permute-start.6
  17.9 0.2 copy.6
  18.4 2.7 %collective-permute-start.17 = (f32[288,128]{1,0:T(8,128)S(1)}, f32[288,128]{1,0:T(8,128)S(1)}, u32[]{:S(2)}, u32[]{:S(2)}) collective-permute-start(f32[288,128]{1,0:T(8,128)S(1)} %get-tuple-element.37), channel_id=1, source_target_pairs={{0,28},{4,8},{8,4},{12,16},{16,12},{20,24},{24,20},{28,0},{1,29},{... | collective-permute-start | bytes 442376 | tf_op jit(solution)/shard_map/ppermute | solution.py:635
  21.1 0.2 collective-permute-done.5.refs_2_
  21.3 0.8 %collective-permute-done.6.refs_3_ = f32[72,128]{1,0:T(8,128)S(1)} collective-permute-done((f32[72,128]{1,0:T(8,128)S(1)}, f32[72,128]{1,0:T(8,128)S(1)}, u32[]{:S(2)}, u32[]{:S(2)}) %collective-permute-start.6) | collective-permute-done | bytes 36896 | tf_op jit(solution)/shard_map/ppermute | solution.py:630
  22.1 0.4 %shard_map.49.refs_0_ = f32[72,128]{1,0:T(8,128)S(1)} custom-call(f32[72,128]{1,0:T(8,128)S(1)} %get-tuple-element.25.refs_0_.after, f32[72,128]{1,0:T(8,128)S(1)} %collective-permute-done.4.refs_1_, f32[72,128]{1,0:T(8,128)S(1)} %collective-permute-done.5.refs_2_, f32[72,128]{1,0:T(8,128)S(1)} %collective-permute-done.6.refs_3_, ...), custom_call_target="tpu_custom_call" | custom-call | tf_op jit(solution)/shard_map/pallas_call | solution.py:568
  22.6 2.2 %collective-permute-start.11 = (f32[72,128]{1,0:T(8,128)S(1)}, f32[72,128]{1,0:T(8,128)S(1)}, u32[]{:S(2)}, u32[]{:S(2)}) collective-permute-start(f32[72,128]{1,0:T(8,128)S(1)} %shard_map.49.refs_0_), channel_id=1, source_target_pairs={{0,25},{1,24},{2,27},{3,26},{4,29},{5,28},{6,31},{7,30},{8,17},{9,... | collective-permute-start | bytes 110600 | tf_op jit(solution)/shard_map/ppermute | solution.py:630
  24.8 1.7 %collective-permute-start.9 = (f32[72,128]{1,0:T(8,128)S(1)}, f32[72,128]{1,0:T(8,128)S(1)}, u32[]{:S(2)}, u32[]{:S(2)}) collective-permute-start(f32[72,128]{1,0:T(8,128)S(1)} %shard_map.49.refs_0_), channel_id=1, source_target_pairs={{0,9},{1,8},{2,11},{3,10},{4,13},{5,12},{6,15},{7,14},{8,1},{9,0},... | collective-permute-start | bytes 110600 | tf_op jit(solution)/shard_map/ppermute | solution.py:630
  26.5 0.3 collective-permute-start.16
  26.8 1.2 %collective-permute-done.11.refs_3_ = f32[72,128]{1,0:T(8,128)S(1)} collective-permute-done((f32[72,128]{1,0:T(8,128)S(1)}, f32[72,128]{1,0:T(8,128)S(1)}, u32[]{:S(2)}, u32[]{:S(2)}) %collective-permute-start.11) | collective-permute-done | bytes 36896 | tf_op jit(solution)/shard_map/ppermute | solution.py:630
  28.0 1.8 %collective-permute-done.10.refs_2_ = f32[72,128]{1,0:T(8,128)S(1)} collective-permute-done((f32[72,128]{1,0:T(8,128)S(1)}, f32[72,128]{1,0:T(8,128)S(1)}, u32[]{:S(2)}, u32[]{:S(2)}) %collective-permute-start.10) | collective-permute-done | bytes 36896 | tf_op jit(solution)/shard_map/ppermute | solution.py:630
  29.8 0.6 %shard_map.50 = (f32[72,128]{1,0:T(8,128)S(1)}, f32[72,128]{1,0:T(8,128)S(1)}) custom-call(s32[1]{0:T(128)} %bitcast.place, f32[72,128]{1,0:T(8,128)S(1)} %shard_map.49.refs_0_, f32[72,128]{1,0:T(8,128)S(1)} %collective-permute-done.9.refs_1_, f32[72,128]{1,0:T(8,128)S(1)} %collective-permute-done.10.refs_2_, f32[72,128]{1,0:T(8,128)S(1)} %collective-permute-done.11.refs_3_), custom_call_target="tpu_custom_call" | custom-call | tf_op jit(solution)/shard_map/pallas_call | solution.py:463
  30.4 1.4 %collective-permute-start.14 = (f32[72,128]{1,0:T(8,128)S(1)}, f32[72,128]{1,0:T(8,128)S(1)}, u32[]{:S(2)}, u32[]{:S(2)}) collective-permute-start(f32[72,128]{1,0:T(8,128)S(1)} %get-tuple-element.33), channel_id=1, source_target_pairs={{0,6},{1,7},{2,4},{3,5},{4,2},{5,3},{6,0},{7,1},{8,14},{9,15},{10,... | collective-permute-start | bytes 110600 | tf_op jit(solution)/shard_map/ppermute | solution.py:630
  31.9 0.2 collective-permute-start.12
  32.0 1.6 %collective-permute-start.13 = (f32[72,128]{1,0:T(8,128)S(1)}, f32[72,128]{1,0:T(8,128)S(1)}, u32[]{:S(2)}, u32[]{:S(2)}) collective-permute-start(f32[72,128]{1,0:T(8,128)S(1)} %get-tuple-element.29.after), channel_id=1, source_target_pairs={{0,3},{1,2},{2,1},{3,0},{4,7},{5,6},{6,5},{7,4},{8,11},{9,10},{10,... | collective-permute-start | bytes 110600 | tf_op jit(solution)/shard_map/ppermute | solution.py:630
  33.7 1.4 %shard_map.51 = (f32[6,16,16,128]{3,2,1,0:T(8,128)S(1)}, f32[8,128]{1,0:T(8,128)S(1)}) custom-call(s32[1]{0:T(128)} %bitcast.place, bf16[16,8,16,128]{3,2,1,0:T(8,128)(2,1)S(1)} %get-tuple-element.30.own_h, bf16[16,8,16,128]{3,2,1,0:T(8,128)(2,1)S(1)} %get-tuple-element.31.own_l, f32[416,128]{1,0:T(8,128)S(1)} %collective-permute-done.near_x.far_x.near_y, ...), custom_call_target="tpu_custom_call" | custom-call | tf_op jit(solution)/shard_map/pallas_call | solution.py:165
  35.1 0.4 %collective-permute-done.14 = f32[72,128]{1,0:T(8,128)S(1)} collective-permute-done((f32[72,128]{1,0:T(8,128)S(1)}, f32[72,128]{1,0:T(8,128)S(1)}, u32[]{:S(2)}, u32[]{:S(2)}) %collective-permute-start.14) | collective-permute-done | bytes 36896 | tf_op jit(solution)/shard_map/ppermute | solution.py:630
  35.8 0.5 %collective-permute-start.15 = (f32[288,128]{1,0:T(8,128)S(1)}, f32[288,128]{1,0:T(8,128)S(1)}, u32[]{:S(2)}, u32[]{:S(2)}) collective-permute-start(f32[288,128]{1,0:T(8,128)S(1)} %pad_maximum_fusion.own), channel_id=1, source_target_pairs={{0,1},{1,0},{2,3},{3,2},{4,5},{5,4},{6,7},{7,6},{8,9},{9,8},{10,11... | collective-permute-start | bytes 442376 | tf_op jit(solution)/shard_map/ppermute | solution.py:630
  36.2 0.8 %shard_map.53.outer = f32[2,16,16,128]{3,2,1,0:T(8,128)S(1)} custom-call(s32[1]{0:T(128)} %bitcast.place, bf16[16,8,16,128]{3,2,1,0:T(8,128)(2,1)S(1)} %get-tuple-element.30.own_h, bf16[16,8,16,128]{3,2,1,0:T(8,128)(2,1)S(1)} %get-tuple-element.31.own_l, f32[288,128]{1,0:T(8,128)S(1)} %collective-permute-done.16.near_x, ...), custom_call_target="tpu_custom_call" | custom-call | tf_op jit(solution)/shard_map/pallas_call | solution.py:165
  37.0 0.2 collective-permute-done.15.other
  37.3 2.3 %shard_map.54 = f32[128,16,128]{2,1,0:T(8,128)} custom-call(s32[1]{0:T(128)} %bitcast.place, f32[288,128]{1,0:T(8,128)S(1)} %pad_maximum_fusion.own, f32[288,128]{1,0:T(8,128)S(1)} %collective-permute-done.15.other, f32[2,16,16,128]{3,2,1,0:T(8,128)S(1)} %shard_map.53.outer, f32[6,16,16,128]{3,2,1,0:T(8,128)S(1)} %get-tuple-element.38.inner, ...), custom_call_target="tpu_custom_call" | custom-call | tf_op jit(solution)/shard_map/pallas_call | solution.py:614
  (34 shorter events, 1.1 us)
Async XLA Ops:
  0.0 1.2 %copy-start = (f32[16,8,16,128]{3,2,1,0:T(8,128)S(1)}, f32[16,8,16,128]{3,2,1,0:T(8,128)}, u32[]{:S(2)}) copy-start(f32[16,8,16,128]{3,2,1,0:T(8,128)} %param.4) | copy-start | bytes 3145732
  1.2 1.7 %copy-start.1 = (f32[2,16,16,1,216]{4,3,2,1,0:T(1,128)S(1)}, f32[2,16,16,1,216]{4,3,2,1,0:T(1,128)}, u32[]{:S(2)}) copy-start(f32[2,16,16,1,216]{4,3,2,1,0:T(1,128)} %param.6) | copy-start | bytes 1327108
  2.4 1.6 %collective-permute-start = (f32[416,128]{1,0:T(8,128)S(1)}, f32[416,128]{1,0:T(8,128)S(1)}, u32[]{:S(2)}, u32[]{:S(2)}) collective-permute-start(f32[416,128]{1,0:T(8,128)S(1)} %get-tuple-element.23), channel_id=1, source_target_pairs={{0,1},{1,0},{2,3},{3,2},{4,5},{5,4},{6,7},{7,6},{8,9},{9,8},{10,11... | collective-permute-start | bytes 638984 | tf_op jit(solution)/shard_map/ppermute | solution.py:630
  3.8 8.0 %collective-permute-start.7 = (f32[1024,128]{1,0:T(8,128)S(1)}, f32[1024,128]{1,0:T(8,128)S(1)}, u32[]{:S(2)}, u32[]{:S(2)}) collective-permute-start(f32[1024,128]{1,0:T(8,128)S(1)} %shard_map.48), channel_id=1, source_target_pairs={{0,1},{1,0},{2,3},{3,2},{4,5},{5,4},{6,7},{7,6},{8,9},{9,8},{10,11... | collective-permute-start | bytes 1572872 | tf_op jit(solution)/shard_map/ppermute | solution.py:630
  4.1 7.7 %collective-permute-start.2 = (f32[200,128]{1,0:T(8,128)S(1)}, f32[200,128]{1,0:T(8,128)S(1)}, u32[]{:S(2)}, u32[]{:S(2)}) collective-permute-start(f32[200,128]{1,0:T(8,128)S(1)} %pad_maximum_fusion.1), channel_id=1, source_target_pairs={{0,3},{1,2},{2,1},{3,0},{4,7},{5,6},{6,5},{7,4},{8,11},{9,10},{10,... | collective-permute-start | bytes 307208 | tf_op jit(solution)/shard_map/ppermute | solution.py:630
  6.8 4.9 %collective-permute-start.3 = (f32[72,128]{1,0:T(8,128)S(1)}, f32[72,128]{1,0:T(8,128)S(1)}, u32[]{:S(2)}, u32[]{:S(2)}) collective-permute-start(f32[72,128]{1,0:T(8,128)S(1)} %get-tuple-element.41), channel_id=1, source_target_pairs={{0,6},{1,7},{2,4},{3,5},{4,2},{5,3},{6,0},{7,1},{8,14},{9,15},{10,... | collective-permute-start | bytes 110600 | tf_op jit(solution)/shard_map/ppermute | solution.py:630
  8.2 3.5 %collective-permute-start.1 = (f32[72,128]{1,0:T(8,128)S(1)}, f32[72,128]{1,0:T(8,128)S(1)}, u32[]{:S(2)}, u32[]{:S(2)}) collective-permute-start(f32[72,128]{1,0:T(8,128)S(1)} %get-tuple-element.43), channel_id=1, source_target_pairs={{0,5},{1,4},{2,7},{3,6},{4,1},{5,0},{6,3},{7,2},{8,13},{9,12},{10,... | collective-permute-start | bytes 110600 | tf_op jit(solution)/shard_map/ppermute | solution.py:630
  11.8 6.1 %copy-start.3 = (f32[27,16,16]{0,2,1:T(8,128)S(1)}, f32[27,16,16]{0,2,1:T(8,128)}, u32[]{:S(2)}) copy-start(f32[27,16,16]{0,2,1:T(8,128)} %param.5) | copy-start | bytes 82948
  11.9 10.3 %collective-permute-start.8 = (f32[512,128]{1,0:T(8,128)S(1)}, f32[512,128]{1,0:T(8,128)S(1)}, u32[]{:S(2)}, u32[]{:S(2)}) collective-permute-start(f32[512,128]{1,0:T(8,128)S(1)} %get-tuple-element.39), channel_id=1, source_target_pairs={{0,5},{1,4},{2,7},{3,6},{4,1},{5,0},{6,3},{7,2},{8,13},{9,12},{10,... | collective-permute-start | bytes 786440 | tf_op jit(solution)/shard_map/ppermute | solution.py:630
  13.2 7.9 %collective-permute-start.4 = (f32[72,128]{1,0:T(8,128)S(1)}, f32[72,128]{1,0:T(8,128)S(1)}, u32[]{:S(2)}, u32[]{:S(2)}) collective-permute-start(f32[72,128]{1,0:T(8,128)S(1)} %get-tuple-element.26), channel_id=1, source_target_pairs={{0,16},{1,17},{2,18},{3,19},{4,20},{5,21},{6,22},{7,23},{8,24},{9,... | collective-permute-start | bytes 110600 | tf_op jit(solution)/shard_map/ppermute | solution.py:630
  16.0 5.3 %collective-permute-start.5 = (f32[72,128]{1,0:T(8,128)S(1)}, f32[72,128]{1,0:T(8,128)S(1)}, u32[]{:S(2)}, u32[]{:S(2)}) collective-permute-start(f32[72,128]{1,0:T(8,128)S(1)} %get-tuple-element.27), channel_id=1, source_target_pairs={{0,25},{1,24},{2,27},{3,26},{4,29},{5,28},{6,31},{7,30},{8,17},{9,... | collective-permute-start | bytes 110600 | tf_op jit(solution)/shard_map/ppermute | solution.py:630
  17.7 4.5 %collective-permute-start.6 = (f32[72,128]{1,0:T(8,128)S(1)}, f32[72,128]{1,0:T(8,128)S(1)}, u32[]{:S(2)}, u32[]{:S(2)}) collective-permute-start(f32[72,128]{1,0:T(8,128)S(1)} %get-tuple-element.28), channel_id=1, source_target_pairs={{0,9},{1,8},{2,11},{3,10},{4,13},{5,12},{6,15},{7,14},{8,1},{9,0},... | collective-permute-start | bytes 110600 | tf_op jit(solution)/shard_map/ppermute | solution.py:630
  18.4 17.8 %collective-permute-start.17 = (f32[288,128]{1,0:T(8,128)S(1)}, f32[288,128]{1,0:T(8,128)S(1)}, u32[]{:S(2)}, u32[]{:S(2)}) collective-permute-start(f32[288,128]{1,0:T(8,128)S(1)} %get-tuple-element.37), channel_id=1, source_target_pairs={{0,28},{4,8},{8,4},{12,16},{16,12},{20,24},{24,20},{28,0},{1,29},{... | collective-permute-start | bytes 442376 | tf_op jit(solution)/shard_map/ppermute | solution.py:635
  22.6 5.4 %collective-permute-start.11 = (f32[72,128]{1,0:T(8,128)S(1)}, f32[72,128]{1,0:T(8,128)S(1)}, u32[]{:S(2)}, u32[]{:S(2)}) collective-permute-start(f32[72,128]{1,0:T(8,128)S(1)} %shard_map.49.refs_0_), channel_id=1, source_target_pairs={{0,25},{1,24},{2,27},{3,26},{4,29},{5,28},{6,31},{7,30},{8,17},{9,... | collective-permute-start | bytes 110600 | tf_op jit(solution)/shard_map/ppermute | solution.py:630
  24.8 5.0 %collective-permute-start.10 = (f32[72,128]{1,0:T(8,128)S(1)}, f32[72,128]{1,0:T(8,128)S(1)}, u32[]{:S(2)}, u32[]{:S(2)}) collective-permute-start(f32[72,128]{1,0:T(8,128)S(1)} %shard_map.49.refs_0_), channel_id=1, source_target_pairs={{0,16},{1,17},{2,18},{3,19},{4,20},{5,21},{6,22},{7,23},{8,24},{9,... | collective-permute-start | bytes 110600 | tf_op jit(solution)/shard_map/ppermute | solution.py:630
  24.8 5.0 %collective-permute-start.9 = (f32[72,128]{1,0:T(8,128)S(1)}, f32[72,128]{1,0:T(8,128)S(1)}, u32[]{:S(2)}, u32[]{:S(2)}) collective-permute-start(f32[72,128]{1,0:T(8,128)S(1)} %shard_map.49.refs_0_), channel_id=1, source_target_pairs={{0,9},{1,8},{2,11},{3,10},{4,13},{5,12},{6,15},{7,14},{8,1},{9,0},... | collective-permute-start | bytes 110600 | tf_op jit(solution)/shard_map/ppermute | solution.py:630
  26.5 9.7 %collective-permute-start.16 = (f32[288,128]{1,0:T(8,128)S(1)}, f32[288,128]{1,0:T(8,128)S(1)}, u32[]{:S(2)}, u32[]{:S(2)}) collective-permute-start(f32[288,128]{1,0:T(8,128)S(1)} %broadcast_add_fusion), channel_id=1, source_target_pairs={{0,4},{1,5},{2,6},{3,7},{4,0},{5,1},{6,2},{7,3},{8,12},{9,13},{10,... | collective-permute-start | bytes 442376 | tf_op jit(solution)/shard_map/ppermute | solution.py:630
  30.4 5.1 %collective-permute-start.14 = (f32[72,128]{1,0:T(8,128)S(1)}, f32[72,128]{1,0:T(8,128)S(1)}, u32[]{:S(2)}, u32[]{:S(2)}) collective-permute-start(f32[72,128]{1,0:T(8,128)S(1)} %get-tuple-element.33), channel_id=1, source_target_pairs={{0,6},{1,7},{2,4},{3,5},{4,2},{5,3},{6,0},{7,1},{8,14},{9,15},{10,... | collective-permute-start | bytes 110600 | tf_op jit(solution)/shard_map/ppermute | solution.py:630
  31.9 3.8 %collective-permute-start.12 = (f32[72,128]{1,0:T(8,128)S(1)}, f32[72,128]{1,0:T(8,128)S(1)}, u32[]{:S(2)}, u32[]{:S(2)}) collective-permute-start(f32[72,128]{1,0:T(8,128)S(1)} %get-tuple-element.33), channel_id=1, source_target_pairs={{0,5},{1,4},{2,7},{3,6},{4,1},{5,0},{6,3},{7,2},{8,13},{9,12},{10,... | collective-permute-start | bytes 110600 | tf_op jit(solution)/shard_map/ppermute | solution.py:630
  32.0 3.7 %collective-permute-start.13 = (f32[72,128]{1,0:T(8,128)S(1)}, f32[72,128]{1,0:T(8,128)S(1)}, u32[]{:S(2)}, u32[]{:S(2)}) collective-permute-start(f32[72,128]{1,0:T(8,128)S(1)} %get-tuple-element.29.after), channel_id=1, source_target_pairs={{0,3},{1,2},{2,1},{3,0},{4,7},{5,6},{6,5},{7,4},{8,11},{9,10},{10,... | collective-permute-start | bytes 110600 | tf_op jit(solution)/shard_map/ppermute | solution.py:630
  35.7 1.5 %copy-start.2 = (bf16[384,512]{1,0:T(8,128)(2,1)S(1)}, bf16[384,512]{1,0:T(8,128)(2,1)}, u32[]{:S(2)}) copy-start(bf16[384,512]{1,0:T(8,128)(2,1)} %constant.50.clone.table_z) | copy-start | bytes 1179652
  35.8 1.5 %collective-permute-start.15 = (f32[288,128]{1,0:T(8,128)S(1)}, f32[288,128]{1,0:T(8,128)S(1)}, u32[]{:S(2)}, u32[]{:S(2)}) collective-permute-start(f32[288,128]{1,0:T(8,128)S(1)} %pad_maximum_fusion.own), channel_id=1, source_target_pairs={{0,1},{1,0},{2,3},{3,2},{4,5},{5,4},{6,7},{7,6},{8,9},{9,8},{10,11... | collective-permute-start | bytes 442376 | tf_op jit(solution)/shard_map/ppermute | solution.py:630
